TPU v7x, 32 devices: a whole 2x2x4 slice. The times are simulated.
32 devices in a mesh: dp: 2 (over x), fsdp: 16 (over z, y, core).
Axes of the slice: x: 2, y: 2, z: 4, core: 2. Of those that a mesh axis runs over, the one named last changes fastest.
Arguments:
- input_token_index: int32 [32, 1024], P(('dp', 'fsdp')), may hold values from 0 to 51199
- sentence_numbers: int32 [32, 1024], P(('dp', 'fsdp')), may hold values from 0 to 15, never falling along the last dimension, each value on 1 to 128 neighbouring positions
- label_positions: int32 [32, 128], P(('dp', 'fsdp')), may hold values from 0 to 1023
- label_target_token: int32 [32, 128], P(('dp', 'fsdp')), may hold values from 0 to 51199
- sequence_task_index: int32 [32], P(('dp', 'fsdp')), may hold values from 0 to 3
- task_loss_weight: float32 [4], replicated, may hold values from 0.5 to 2
- optimizer_step_count: int32 [1], replicated, may hold values from 2 to 20
- embed: bfloat16 [51200, 768], P('dp'), may hold values from -0.4375 to 0.4375
- position_embedding: bfloat16 [128, 768], replicated, may hold values from -0.4375 to 0.4375
- norm_gain_vector: float32 [6, 768], replicated, may hold values from 0.5 to 1.5
- norm_bias_vector: float32 [6, 768], replicated, may hold values from -2 to 2
- attention_in_weight: bfloat16 [2, 768, 2304], P(None, None, ('dp', 'fsdp')), may hold values from -0.21875 to 0.21875
- attention_out_weight: bfloat16 [2, 768, 768], P(None, None, ('dp', 'fsdp')), may hold values from -1.75 to 1.75
- feedforward_up: bfloat16 [2, 768, 3072], P(None, None, ('dp', 'fsdp')), may hold values from -0.21875 to 0.21875
- feedforward_down: bfloat16 [2, 3072, 768], P(None, ('dp', 'fsdp')), may hold values from -0.109375 to 0.109375
- layer_bias_vector: float32 [2, 6144], replicated, may hold values from -2 to 2
- head_dense_bias: float32 [768], replicated, may hold values from -2 to 2
- vocabulary_bias: float32 [51200], P(('dp', 'fsdp')), may hold values from -3 to 3
- adapter_down_matrix: bfloat16 [2, 2, 768, 8], replicated, may hold values from -0.21875 to 0.21875
- adapter_up_matrix: float32 [2, 2, 8, 768], P(None, None, None, ('dp', 'fsdp')), may hold values from -0.6 to 0.6
- adapter_moment_first: float32 [2, 2, 8, 768], P(None, None, None, ('dp', 'fsdp')), may hold values from -1.9073486e-05 to 1.9073486e-05
- adapter_moment_second: float32 [2, 2, 8, 768], P(None, None, None, ('dp', 'fsdp')), may hold values from 1.6276042e-13 to 6.5104167e-13
- head_projection: float32 [768, 768], P(('dp', 'fsdp')), may hold values from -0.21875 to 0.21875
- head_moment_first: float32 [768, 768], P(('dp', 'fsdp')), may hold values from -1.9073486e-05 to 1.9073486e-05
- head_moment_second: float32 [768, 768], P(('dp', 'fsdp')), may hold values from 1.6276042e-13 to 6.5104167e-13
Outputs:
- masked_task_loss: float32 [], replicated
- gradient_norm: float32 [], replicated
- lora_up_next: float32 [2, 2, 8, 768], P(None, None, None, ('dp', 'fsdp'))
- lora_first_next: float32 [2, 2, 8, 768], P(None, None, None, ('dp', 'fsdp'))
- lora_second_next: float32 [2, 2, 8, 768], P(None, None, None, ('dp', 'fsdp'))
- head_dense_next: float32 [768, 768], P(('dp', 'fsdp'))
- head_first_next: float32 [768, 768], P(('dp', 'fsdp'))
- head_second_next: float32 [768, 768], P(('dp', 'fsdp'))
Inputs may be any that keep to these rules, and one draw needn't show every extreme that they name: `sentence_numbers`: segment numbers never fall along a sequence; each sentence holds 1 to 128 tokens.
All inputs are finite; a program needn't handle non-finite values.
Results may differ from a plain program's by a relative error of at most 0.0044.
Values may be sent and summed in bfloat16 or wider, within the bound.
A program may use at most 448 MiB of HBM per device.

v0:
```python
import functools

import jax
import jax.numpy as jnp
from jax import lax
from jax.experimental import pallas as pl
from jax.experimental.pallas import tpu as pltpu
from jax.sharding import PartitionSpec as P

HEADS = 12
TASKS = 4
REACH = 128

norm_eps = 1e-05
adapter_scale = 2.0
clip_limit = 0.01
learn_rate = 0.05
beta_first = 0.9
beta_second = 0.999
adam_eps = 1e-08
decay_rate = 0.01
masked_score = -1e30

BF = jnp.bfloat16
F32 = jnp.float32
BOTH = ("dp", "fsdp")
VMEM_BYTES = 60 * 1024 * 1024


def mm(a, b):
    return lax.dot_general(a, b, (((1,), (0,)), ((), ())), preferred_element_type=F32)


def mm_nt(a, b):
    return lax.dot_general(a, b, (((1,), (1,)), ((), ())), preferred_element_type=F32)


def mm_tn(a, b):
    return lax.dot_general(a, b, (((0,), (0,)), ((), ())), preferred_element_type=F32)


def layer_norm(rows_in, gain, shift):
    center = rows_in - jnp.mean(rows_in, -1, keepdims=True)
    spread = jnp.mean(center * center, -1, keepdims=True)
    return center * lax.rsqrt(spread + norm_eps) * gain + shift


def norm_back(rows_in, gain, gradient):
    center = rows_in - jnp.mean(rows_in, -1, keepdims=True)
    inverse = lax.rsqrt(jnp.mean(center * center, -1, keepdims=True) + norm_eps)
    unit = center * inverse
    scaled = gradient * gain
    return inverse * (
        scaled
        - jnp.mean(scaled, -1, keepdims=True)
        - unit * jnp.mean(scaled * unit, -1, keepdims=True)
    )


def gelu_pair(v):
    size = jnp.abs(v) * 0.7071067811865476
    base = 1.0 + 0.3275911 * size
    t = pl.reciprocal(base, approx=True)
    t = t * (2.0 - base * t)
    bell = jnp.exp(-0.5 * v * v)
    poly = t * (
        0.127414796 + t * (-0.142248368 + t * (0.7107068705 + t * (-0.7265760135 + t * 0.5307027145)))
    )
    tail = poly * bell
    phi = jnp.where(v >= 0.0, 1.0 - tail, tail)
    return v * phi, phi + v * (bell * 0.3989422804014327)


def params(**more):
    return pltpu.CompilerParams(vmem_limit_bytes=VMEM_BYTES, **more)


def full(shape):
    return pl.BlockSpec(shape, lambda *_: (0,) * len(shape))


def split_of(total, most, step):
    size = (min(most, total) // step) * step
    while size > step and total % size:
        size -= step
    return size if size and total % size == 0 else total


def pair_rows(block, width):
    first = lax.broadcasted_iota(jnp.int32, block.shape, 1) < width
    return jnp.concatenate([jnp.where(first, block, 0.0), jnp.where(first, 0.0, block)], 0).astype(BF)


def pair_join(wide, width):
    rows = wide.shape[1] // 2
    return jnp.concatenate([wide[:width, :rows], wide[width:, rows:]], 0)


def masked(scores, same):
    rows = scores.shape[1] // 2
    return jnp.concatenate(
        [
            jnp.where(same, scores[:, :rows], masked_score),
            jnp.where(same, scores[:, rows:], masked_score),
        ],
        1,
    )


def qkv_bias(bias_ref, layer, start, size):
    hidden = bias_ref.shape[1] // 8
    if start >= 2 * hidden:
        return bias_ref[layer : layer + 1, start - hidden : start - hidden + size]
    return bias_ref[layer : layer + 1, start : start + size] if start < hidden else 0.0


def norm_of(norm_refs, k):
    return norm_refs[0][k : k + 1, :], norm_refs[1][k : k + 1, :]


def project_body(
    own_ref, got_ref, code_ref, spots_ref, gain_ref, shift_ref, down_ref, w_ref, up_ref, bias_ref,
    out_ref, mid_ref, x_ref,
):
    mine = code_ref[...] % 2
    choose = (
        lax.broadcasted_iota(jnp.int32, (own_ref.shape[0], spots_ref.shape[0]), 1) == code_ref[...] // 2
    )
    summed = jnp.where(
        mine > 0, own_ref[...].astype(F32), got_ref[...].astype(F32)
    ) + mm(choose.astype(F32).astype(BF), spots_ref[...])
    x = layer_norm(summed, *norm_of((gain_ref, shift_ref), 0))
    x_ref[...] = x
    low = x.astype(BF)
    mid = mm(low, down_ref[0]).astype(BF)
    mid_ref[...] = mid
    total = w_ref.shape[0]
    step = total // 3
    for start in range(0, total, step):
        part = slice(start, start + step)
        out_ref[:, part] = (
            mm_nt(low, w_ref[part, :]) + mm(mid, up_ref[0, :, part]) + qkv_bias(bias_ref, 0, start, step)
        ).astype(BF)


def project(own, got, code, spots, gains, shifts, down, w, up, bias):
    rows, width = code.shape[0], own.shape[1]
    tile = split_of(rows, 256, 16)
    total = w.shape[0]
    row = lambda n: pl.BlockSpec((tile, n), lambda i: (i, 0))
    return pl.pallas_call(
        project_body,
        grid=(rows // tile,),
        in_specs=[row(width), row(width), row(1)]
        + [full(a.shape) for a in (spots, gains, shifts, down, w, up, bias)],
        out_specs=[row(total), row(down.shape[2]), row(width)],
        out_shape=[
            jax.ShapeDtypeStruct((rows, total), BF),
            jax.ShapeDtypeStruct((rows, down.shape[2]), BF),
            jax.ShapeDtypeStruct((rows, width), F32),
        ],
        compiler_params=params(),
        name="project",
    )(own, got, code, spots, gains, shifts, down, w, up, bias)


def attend_body(q_ref, k_ref, v_ref, seg_ref, seg_row_ref, ctx_ref, log_ref):
    rows = q_ref.shape[0]
    width = q_ref.shape[1] // 2
    scale = width**-0.5
    turned = turn_blocks(v_ref)

    def scored(start):
        own, near = reach_of(start, rows)
        return mm_nt(k_ref[near, :], pair_rows(q_ref[own, :].astype(F32) * scale, width))

    scores = scored(0)
    for start in range(0, rows, REACH):
        own, near = reach_of(start, rows)
        later = scored(start + REACH) if start + REACH < rows else None
        same = seg_ref[near, :] == seg_row_ref[:, own]
        scores = masked(scores, same)
        top = jnp.max(scores, 0, keepdims=True)
        weights = jnp.exp(scores - top)
        total = jnp.sum(weights, 0, keepdims=True)
        context = mm(turned[:, near], weights.astype(BF)) * (1.0 / total)
        ctx_ref[own, :] = pair_join(context, width).T.astype(BF)
        log_ref[0, :, 2 * start : 2 * start + 2 * REACH] = top + jnp.log(total)
        scores = later


def reach_of(start, rows):
    return slice(start, start + REACH), slice(max(0, start - REACH), min(rows, start + 2 * REACH))


def turn_blocks(ref):
    blocks = [ref[k : k + 128, :].astype(F32).T.astype(BF) for k in range(0, ref.shape[0], 128)]
    return jnp.concatenate(blocks, 1)


def attend(qkv, seg_wide, seg_row):
    rows, total = qkv.shape
    hidden = total // 3
    lanes = 2 * (hidden // HEADS)
    pairs = hidden // lanes
    column = lambda kind: pl.BlockSpec((rows, lanes), lambda p: (0, kind * pairs + p))
    return pl.pallas_call(
        attend_body,
        grid=(pairs,),
        in_specs=[column(0), column(1), column(2), full(seg_wide.shape), full(seg_row.shape)],
        out_specs=[
            pl.BlockSpec((rows, lanes), lambda p: (0, p)),
            pl.BlockSpec((1, 1, 2 * rows), lambda p: (p, 0, 0)),
        ],
        out_shape=[
            jax.ShapeDtypeStruct((rows, hidden), BF),
            jax.ShapeDtypeStruct((pairs, 1, 2 * rows), F32),
        ],
        compiler_params=params(),
        name="attend",
    )(qkv, qkv, qkv, seg_wide, seg_row)


def flat(ref):
    whole = ref[...]
    return whole.reshape(-1, whole.shape[-1])


def rows_of(ref, start, size):
    each = ref.shape[1]
    if size % each == 0 and start % each == 0 and each % 16 == 0:
        part = ref[start // each : (start + size) // each, :, :]
        return part.reshape(size, part.shape[-1])
    return flat(ref)[start : start + size, :]


def feed_step(ref):
    units = ref.shape[0] * ref.shape[1]
    step = ref.shape[1]
    while units % (2 * step) == 0 and 2 * step <= 768 and ref.shape[0] > 1:
        step *= 2
    return units, (step if ref.shape[0] > 1 else split_of(units, 768, 128))


def later_biases(bias_ref, layer):
    hidden = bias_ref.shape[1] // 8
    row = bias_ref[layer : layer + 1, :]
    return row[:, 2 * hidden : 3 * hidden], row[:, 3 * hidden : 7 * hidden], row[:, 7 * hidden :]


def after_body(
    ctx_ref, x_ref, wo_ref, up_ref, down_ref, bias_ref, gain_ref, shift_ref,
    out_ref, one_ref, two_ref, slope_ref,
):
    bo, b1, b2 = later_biases(bias_ref, 0)
    one = x_ref[...] + (mm_nt(ctx_ref[...], wo_ref[...]) + bo)
    one_ref[...] = one
    middle = layer_norm(one, *norm_of((gain_ref, shift_ref), 1))
    low = middle.astype(BF)
    total = middle + b2
    units, step = feed_step(up_ref)
    gate = mm_nt(low, rows_of(up_ref, 0, step))
    for start in range(0, units, step):
        part = slice(start, start + step)
        later = mm_nt(low, rows_of(up_ref, start + step, step)) if start + step < units else None
        act, slope = gelu_pair(gate + b1[:, part])
        slope_ref[:, part] = slope.astype(BF)
        total = total + mm(act.astype(BF), rows_of(down_ref, start, step))
        gate = later
    two_ref[...] = total
    out_ref[...] = layer_norm(total, *norm_of((gain_ref, shift_ref), 2))


def slab_spec(slab):
    array, place, rows = slab
    return pl.BlockSpec((array.shape[0], rows, array.shape[2]), lambda *_: (0, place, 0))


def after(ctx, x, wo, up, down, bias, gains, shifts):
    rows, width = x.shape
    tile = split_of(rows, 256, 16)
    units = 4 * width
    row = lambda n: pl.BlockSpec((tile, n), lambda i: (i, 0))
    return pl.pallas_call(
        after_body,
        grid=(rows // tile,),
        in_specs=[row(width), row(width), full(wo.shape), slab_spec(up), slab_spec(down)]
        + [full(a.shape) for a in (bias, gains, shifts)],
        out_specs=[row(width), row(width), row(width), row(units)],
        out_shape=[jax.ShapeDtypeStruct((rows, width), F32)] * 3
        + [jax.ShapeDtypeStruct((rows, units), BF)],
        compiler_params=params(),
        name="after",
    )(ctx, x, wo, up[0], down[0], bias, gains, shifts)


def exact_rows(choose, matrix):
    high = matrix.astype(BF)
    rest = matrix - high.astype(F32)
    middle = rest.astype(BF)
    low = (rest - middle.astype(F32)).astype(BF)
    return mm(choose, high) + mm(choose, middle) + mm(choose, low)


def unpack_rows(slab_ref, targets):
    shards = slab_ref.shape[0]

    @pl.loop(0, shards // 2)
    def _(k):
        first, second = slab_ref[2 * k].astype(F32), slab_ref[2 * k + 1].astype(F32)
        at = 0
        for target in targets:
            each = target.shape[0] // shards
            both = jnp.concatenate([first[at : at + each], second[at : at + each]], 0)
            target[pl.ds(pl.multiple_of(2 * each * k, 2 * each), 2 * each), :] = both.astype(BF)
            at += each


def last_forward_body(
    x_ref, place_ref, place_row_ref, seg_ref, down_ref, adapt_ref, bias_ref, weights_any, up_any, dn_any,
    gain_ref, shift_ref, hbias_ref,
    kv_ref, q_ref, mid_ref, log_ref, one_ref, slope_ref, two_ref, low_ref, act_ref, hslope_ref, feat_ref, *more,
    places, starts,
):
    copies = []
    if starts is None:
        up_ref, dn_ref, ctx_ref, w_ref, wo_ref, hb_ref, sems = more
        sources = zip(weights_any, (w_ref, wo_ref, hb_ref))
    else:
        w_out, wo_out, hb_out, up_ref, dn_ref, ctx_ref, w_ref, wo_ref, hb_ref, in_slab, hb_slab, sems = more
        sources = [
            (weights_any[0].at[:, pl.ds(start, slab.shape[1]), :], slab)
            for start, slab in zip(starts, (in_slab, hb_slab))
        ]
    for source, target in sources:
        copies.append((source, target))
    early = len(copies)
    for source, target, place in ((up_any, up_ref, places[0]), (dn_any, dn_ref, places[1])):
        each = target.shape[1]
        copies.append((source.at[:, pl.ds(place * each, each), :], target))
    copies = [pltpu.make_async_copy(*ends, sems.at[k]) for k, ends in enumerate(copies)]
    for copy in copies:
        copy.start()
    for copy in copies[:early]:
        copy.wait()
    copies = copies[early:]
    if starts is not None:
        unpack_rows(in_slab, (w_ref, wo_ref))
        unpack_rows(hb_slab, (hb_ref,))
        for k, ends in enumerate(((w_ref, w_out), (wo_ref, wo_out), (hb_ref, hb_out))):
            copies.append(pltpu.make_async_copy(*ends, sems.at[4 + k]))
            copies[-1].start()
    rows, hidden = x_ref.shape
    labels = place_ref.shape[0]
    lanes = 2 * (hidden // HEADS)
    width = lanes // 2
    low = x_ref[...].astype(BF)
    mid = mm(low, down_ref[1]).astype(BF)
    mid_ref[...] = mid
    step = split_of(hidden, 768, 128)
    for start in range(hidden, 3 * hidden, step):
        part = slice(start, start + step)
        kv_ref[:, start - hidden : start - hidden + step] = (
            mm_nt(low, w_ref[part, :]) + mm(mid, adapt_ref[1, :, part]) + qkv_bias(bias_ref, 1, start, step)
        ).astype(BF)
    choose = (
        lax.broadcasted_iota(jnp.int32, (labels, rows), 1) == place_ref[...][:, 0:1]
    ).astype(F32).astype(BF)
    own = exact_rows(choose, x_ref[...])
    own_low = own.astype(BF)
    own_mid = mm(choose, mid).astype(BF)
    q_ref[...] = (
        mm_nt(own_low, w_ref[:hidden, :])
        + mm(own_mid, adapt_ref[1, :, :hidden])
        + qkv_bias(bias_ref, 1, 0, hidden)
    ).astype(BF)
    seg = seg_ref[...]
    seg_own = jnp.sum(
        jnp.where(
            lax.broadcasted_iota(jnp.int32, (rows, labels), 0) == place_row_ref[...], seg, 0.0
        ),
        0,
        keepdims=True,
    )
    same = seg == seg_own
    for p in range(hidden // lanes):
        part = slice(p * lanes, (p + 1) * lanes)
        queries = pair_rows(q_ref[:, part].astype(F32) * width**-0.5, width)
        scores = masked(mm_nt(kv_ref[:, part], queries), same)
        top = jnp.max(scores, 0, keepdims=True)
        weights = jnp.exp(scores - top)
        total = jnp.sum(weights, 0, keepdims=True)
        context = mm_tn(
            kv_ref[:, hidden + p * lanes : hidden + (p + 1) * lanes], weights.astype(BF)
        ) * (1.0 / total)
        ctx_ref[:, part] = pair_join(context, width).T.astype(BF)
        log_ref[p : p + 1, :] = top + jnp.log(total)
    bo, b1, b2 = later_biases(bias_ref, 1)
    norms = (gain_ref, shift_ref)
    one = own + (mm_nt(ctx_ref[...], wo_ref[...]) + bo)
    one_ref[...] = one
    middle = layer_norm(one, *norm_of(norms, 3))
    middle_low = middle.astype(BF)
    sum_two = middle + b2
    units, step = feed_step(up_ref)
    for copy in copies:
        copy.wait()
    for start in range(0, units, step):
        part = slice(start, start + step)
        act, slope = gelu_pair(mm_nt(middle_low, rows_of(up_ref, start, step)) + b1[:, part])
        slope_ref[:, part] = slope.astype(BF)
        sum_two = sum_two + mm(act.astype(BF), rows_of(dn_ref, start, step))
    two_ref[...] = sum_two
    out_low = layer_norm(sum_two, *norm_of(norms, 4)).astype(BF)
    low_ref[...] = out_low
    act, slope = gelu_pair(mm(out_low, hb_ref[...]) + hbias_ref[...])
    act_ref[...] = act
    hslope_ref[...] = slope
    feat_ref[...] = layer_norm(act, *norm_of(norms, 5)).astype(BF)


def slab_scratch(slab):
    array, place, rows = slab
    return pltpu.VMEM((array.shape[0], rows, array.shape[2]), BF)


def last_forward(
    x, place_col, place_row, seg_wide, down, adapt, bias, weights, starts, up, dn, gains, shifts, hbias
):
    rows, hidden = x.shape
    labels = place_col.shape[0]
    units = 4 * hidden
    whole = pl.BlockSpec(memory_space=pltpu.VMEM)
    anywhere = pl.BlockSpec(memory_space=pl.ANY)
    shape = jax.ShapeDtypeStruct
    pairs = HEADS // 2
    matrices = [(3 * hidden, hidden), (hidden, hidden), (hidden, hidden)]
    slabs = []
    if starts is not None:
        shards = weights[0].shape[0]
        slabs = [
            pltpu.VMEM((shards, 4 * hidden // shards, hidden), BF),
            pltpu.VMEM((shards, weights[0].shape[1] - starts[1], hidden), BF),
        ]

    def body(*refs):
        head, rest = refs[:7], refs[7:]
        return last_forward_body(
            *head, rest[: len(weights)], *rest[len(weights) :], places=(up[1], dn[1]), starts=starts
        )

    return pl.pallas_call(
        body,
        in_specs=[whole] * 7 + [anywhere] * (len(weights) + 2) + [whole] * 3,
        out_specs=[whole] * 11 + ([anywhere] * 3 if slabs else []),
        out_shape=[
            shape((rows, 2 * hidden), BF),
            shape((labels, hidden), BF),
            shape((rows, down.shape[2]), BF),
            shape((pairs, 2 * labels), F32),
            shape((labels, hidden), F32),
            shape((labels, units), BF),
            shape((labels, hidden), F32),
            shape((labels, hidden), BF),
            shape((labels, hidden), F32),
            shape((labels, hidden), F32),
            shape((labels, hidden), BF),
        ]
        + ([shape(m, BF) for m in matrices] if slabs else []),
        scratch_shapes=[
            slab_scratch(up),
            slab_scratch(dn),
            pltpu.VMEM((labels, hidden), BF),
            *[pltpu.VMEM(m, BF) for m in matrices],
            *slabs,
            pltpu.SemaphoreType.DMA((7,)),
        ],
        compiler_params=params(),
        name="last_forward",
    )(x, place_col, place_row, seg_wide, down, adapt, bias, *weights, up[0], dn[0], gains, shifts, hbias)


def vocab_body(u_ref, e_ref, et_ref, bias_ref, num_ref, log_ref, scores, weights):
    count = e_ref.shape[0]
    step = split_of(count, 640, 16)
    u = u_ref[...]
    rows = u.shape[0]
    labels = num_ref.shape[2]
    top = jnp.full((1, rows), -jnp.inf, F32)
    for start in range(0, count, step):
        part = slice(start, start + step)
        bias = bias_ref[part, :]
        logits = mm_nt(e_ref[part, :], u) + jnp.concatenate([bias] * (rows // bias.shape[1]), 1)
        scores[part, :] = logits
        top = jnp.maximum(top, jnp.max(logits, 0, keepdims=True))
    total = jnp.zeros((1, rows), F32)
    for start in range(0, count, step):
        part = slice(start, start + step)
        grown = jnp.exp(scores[part, :] - top)
        total = total + jnp.sum(grown, 0, keepdims=True)
        weights[part, :] = grown.astype(BF)
    mean = mm(et_ref[...], weights[...]) * (1.0 / total)
    logs = top + jnp.log(total)
    for k in range(rows // labels):
        num_ref[k, :, :] = mean[:, k * labels : (k + 1) * labels]
        log_ref[k, :, :] = logs[:, k * labels : (k + 1) * labels]


def vocab(u, e, et, bias_wide, labels):
    rows, hidden = u.shape
    count = e.shape[0]
    tile = 2 * labels
    return pl.pallas_call(
        vocab_body,
        grid=(rows // tile,),
        in_specs=[
            pl.BlockSpec((tile, hidden), lambda i: (i, 0)),
            full(e.shape),
            full(et.shape),
            full(bias_wide.shape),
        ],
        out_specs=[
            pl.BlockSpec((2, hidden, labels), lambda i: (i, 0, 0)),
            pl.BlockSpec((2, 1, labels), lambda i: (i, 0, 0)),
        ],
        out_shape=[
            jax.ShapeDtypeStruct((rows // labels, hidden, labels), F32),
            jax.ShapeDtypeStruct((rows // labels, 1, labels), F32),
        ],
        scratch_shapes=[pltpu.VMEM((count, tile), F32), pltpu.VMEM((count, tile), BF)],
        compiler_params=params(),
        name="vocab",
    )(u, e, et, bias_wide)


def last_backward_body(
    mean_ref, all_log_ref, target_ref, fact_ref, kv_ref, q_ref, mid_ref, log_ref, one_ref, slope_ref, two_ref,
    low_ref, act_ref, hslope_ref, feat_ref, place_ref, place_row_ref, seg_ref, down_ref, w_ref, adapt_ref, wo_ref,
    up_any, dn_any, gain_ref, hb_ref,
    dx_ref, gh_ref, g_ref, out_fact_ref,
    up_ref, dn_ref, dkv_ref, dq_ref, sems, *, places, edge,
):
    copies = []
    for k, (source, target, place) in enumerate(
        ((up_any, up_ref, places[0]), (dn_any, dn_ref, places[1]))
    ):
        rows = target.shape[1]
        copies.append(
            pltpu.make_async_copy(
                source.at[:, pl.ds(place * rows, rows), :], target, sems.at[k]
            )
        )
        copies[-1].start()
    rows = kv_ref.shape[0]
    labels, hidden = feat_ref.shape
    lanes = 2 * (hidden // HEADS)
    width = lanes // 2
    scale = width**-0.5
    targets = target_ref[...].astype(F32)
    weight = fact_ref[0:1, 0:1]
    chosen = jnp.sum(feat_ref[...].astype(F32) * targets, keepdims=True)
    loss = weight * (jnp.sum(all_log_ref[...] - fact_ref[3:4, :labels], keepdims=True) - chosen)
    out_fact_ref[...] = jnp.where(
        lax.broadcasted_iota(jnp.int32, fact_ref.shape, 0) == 0, loss, fact_ref[...]
    )
    du = weight * (mean_ref[...].T - targets)
    dact = norm_back(act_ref[...], gain_ref[5:6, :], du)
    dz = (hslope_ref[...] * dact).astype(BF)
    dense = mm_tn(low_ref[...], dz)
    if len(gh_ref.shape) == 2:
        gh_ref[...] = dense
    else:
        each = hidden // gh_ref.shape[0]
        spare = jnp.zeros((gh_ref.shape[1] - each, hidden), F32)
        for k in range(gh_ref.shape[0]):
            gh_ref[k] = jnp.concatenate([dense[k * each : (k + 1) * each, :], spare], 0).astype(BF)
    dtwo = norm_back(two_ref[...], gain_ref[4:5, :], mm_nt(dz, hb_ref[...]))
    dtwo_low = dtwo.astype(BF)
    dmiddle = dtwo
    units, step = feed_step(up_ref)
    for copy in copies:
        copy.wait()
    for start in range(0, units, step):
        part = slice(start, start + step)
        dgate = (
            slope_ref[:, part].astype(F32) * mm_nt(dtwo_low, rows_of(dn_ref, start, step))
        ).astype(BF)
        dmiddle = dmiddle + mm(dgate, rows_of(up_ref, start, step))
    done = norm_back(one_ref[...], gain_ref[3:4, :], dmiddle)
    dctx = mm(done.astype(BF), wo_ref[...]).astype(BF)
    seg = seg_ref[...]
    choose_t = lax.broadcasted_iota(jnp.int32, (rows, labels), 0) == place_row_ref[...]
    same = seg == jnp.sum(jnp.where(choose_t, seg, 0.0), 0, keepdims=True)
    for p in range(hidden // lanes):
        part = slice(p * lanes, (p + 1) * lanes)
        later = slice(hidden + p * lanes, hidden + (p + 1) * lanes)
        queries = pair_rows(q_ref[:, part].astype(F32) * scale, width)
        outs = pair_rows(dctx[:, part].astype(F32), width)
        keys = kv_ref[:, part]
        weights = jnp.exp(masked(mm_nt(keys, queries), same) - log_ref[p : p + 1, :])
        dweights = mm_nt(kv_ref[:, later], outs)
        inner = jnp.sum(dweights * weights, 0, keepdims=True)
        dscores = (weights * (dweights - inner)).astype(BF)
        dkv_ref[:, part] = mm(dscores, queries).astype(BF)
        dkv_ref[:, later] = mm(weights.astype(BF), outs).astype(BF)
        dq_ref[:, part] = (pair_join(mm_tn(keys, dscores), width) * scale).T.astype(BF)
    dq = dq_ref[...]
    own_mid = mm(
        (lax.broadcasted_iota(jnp.int32, (labels, rows), 1) == place_ref[...][:, 0:1]).astype(F32).astype(BF),
        mid_ref[...],
    ).astype(BF)
    g_ref[...] = adapter_scale * jnp.where(
        lax.broadcasted_iota(jnp.int32, g_ref.shape, 1) < edge,
        mm_tn(dq, own_mid),
        mm_tn(dkv_ref[:, hidden:], mid_ref[...]),
    )
    dmid_own = mm_nt(dq, adapt_ref[1, :, :hidden]).astype(BF)
    own = done + mm(dq, w_ref[:hidden, :]) + mm_nt(dmid_own, down_ref[1])
    spread = choose_t.astype(F32).astype(BF)
    own_high = own.astype(BF)
    own_rest = (own - own_high.astype(F32)).astype(BF)
    dmid = mm_nt(dkv_ref[:, hidden:], adapt_ref[1, :, 2 * hidden :]).astype(BF)
    step = split_of(hidden, 256, 128)
    for start in range(0, hidden, step):
        part = slice(start, start + step)
        dx_ref[:, part] = (
            mm(dkv_ref[...], w_ref[hidden:, part])
            + mm_nt(dmid, down_ref[1, part, :])
            + mm(spread, own_high[:, part])
            + mm(spread, own_rest[:, part])
        )


def last_backward(
    mean, logs, targets, facts, saved, place_col, place_row, seg_wide, down, w, adapt, wo, up, dn, gains, hb, edge, shards
):
    kv = saved[0]
    rows = kv.shape[0]
    labels, hidden = targets.shape
    whole = pl.BlockSpec(memory_space=pltpu.VMEM)
    anywhere = pl.BlockSpec(memory_space=pl.ANY)
    shape = jax.ShapeDtypeStruct
    return pl.pallas_call(
        functools.partial(last_backward_body, places=(up[1], dn[1]), edge=edge),
        in_specs=[whole] * 22 + [anywhere] * 2 + [whole] * 2,
        out_specs=[whole] * 4,
        out_shape=[
            shape((rows, hidden), F32),
            shape((hidden, hidden), F32)
            if shards is None
            else shape((shards, -(-hidden // shards // 16) * 16, hidden), BF),
            shape((hidden, down.shape[2]), F32),
            shape(facts.shape, F32),
        ],
        scratch_shapes=[
            slab_scratch(up),
            slab_scratch(dn),
            pltpu.VMEM(kv.shape, BF),
            pltpu.VMEM((labels, hidden), BF),
            pltpu.SemaphoreType.DMA((2,)),
        ],
        compiler_params=params(),
        name="last_backward",
    )(mean, logs, targets, facts, *saved, place_col, place_row, seg_wide, down, w, adapt, wo, up[0], dn[0], gains, hb)


def after_back_body(dout_ref, one_ref, two_ref, slope_ref, wo_ref, up_ref, down_ref, gain_ref, dctx_ref):
    dtwo = norm_back(two_ref[...], gain_ref[2:3, :], dout_ref[...])
    low = dtwo.astype(BF)
    dmiddle = dtwo
    units, step = feed_step(up_ref)
    dact = mm_nt(low, rows_of(down_ref, 0, step))
    for start in range(0, units, step):
        part = slice(start, start + step)
        later = mm_nt(low, rows_of(down_ref, start + step, step)) if start + step < units else None
        dgate = (slope_ref[:, part].astype(F32) * dact).astype(BF)
        dmiddle = dmiddle + mm(dgate, rows_of(up_ref, start, step))
        dact = later
    done = norm_back(one_ref[...], gain_ref[1:2, :], dmiddle)
    dctx_ref[...] = mm(done.astype(BF), wo_ref[...]).astype(BF)


def after_back(dout, one, two, slope, wo, up, down, norms):
    rows, width = dout.shape
    tile = split_of(rows, 256, 16)
    row = lambda n: pl.BlockSpec((tile, n), lambda i: (i, 0))
    return pl.pallas_call(
        after_back_body,
        grid=(rows // tile,),
        in_specs=[row(width), row(width), row(width), row(slope.shape[1]), full(wo.shape)]
        + [slab_spec(up), slab_spec(down), full(norms.shape)],
        out_specs=row(width),
        out_shape=jax.ShapeDtypeStruct((rows, width), BF),
        compiler_params=params(),
        name="after_back",
    )(dout, one, two, slope, wo, up[0], down[0], norms)


def attend_back_body(
    q_ref, k_ref, v_ref, dctx_ref, log_ref, seg_ref, seg_row_ref, mid_ref, g_ref, dv_ref, *, edge
):
    rows = q_ref.shape[0]
    width = q_ref.shape[1] // 2
    scale = width**-0.5
    dv_ref[...] = jnp.zeros_like(dv_ref)
    gq = jnp.zeros((2 * width, mid_ref.shape[1]), F32)
    turned = turn_blocks(k_ref)

    def products(start):
        own, near = reach_of(start, rows)
        queries = pair_rows(q_ref[own, :].astype(F32) * scale, width)
        outs = pair_rows(dctx_ref[own, :].astype(F32), width)
        return outs, mm_nt(k_ref[near, :], queries), mm_nt(v_ref[near, :], outs)

    now = products(0)
    for start in range(0, rows, REACH):
        own, near = reach_of(start, rows)
        later = products(start + REACH) if start + REACH < rows else None
        outs, scores, dweights = now
        same = seg_ref[near, :] == seg_row_ref[:, own]
        logs = log_ref[0, :, 2 * start : 2 * start + 2 * REACH]
        weights = jnp.exp(masked(scores, same) - logs)
        inner = jnp.sum(dweights * weights, 0, keepdims=True)
        dscores = (weights * (dweights - inner)).astype(BF)
        dv_ref[near, :] += mm(weights.astype(BF), outs)
        dq = (pair_join(mm(turned[:, near], dscores), width) * scale).astype(BF)
        gq = gq + mm(dq, mid_ref[own, :])
        now = later
    gv = mm_tn(dv_ref[...].astype(BF), mid_ref[...])
    g_ref[...] = adapter_scale * jnp.where(
        lax.broadcasted_iota(jnp.int32, gq.shape, 1) < edge, gq, gv
    )


def attend_back(qkv, dctx, logs, seg_wide, seg_row, mid, edge):
    rows, total = qkv.shape
    hidden = total // 3
    lanes = 2 * (hidden // HEADS)
    pairs = hidden // lanes
    column = lambda kind: pl.BlockSpec((rows, lanes), lambda p: (0, kind * pairs + p))
    return pl.pallas_call(
        functools.partial(attend_back_body, edge=edge),
        grid=(pairs,),
        in_specs=[
            column(0),
            column(1),
            column(2),
            column(0),
            pl.BlockSpec((1, 1, 2 * rows), lambda p: (p, 0, 0)),
            full(seg_wide.shape),
            full(seg_row.shape),
            full(mid.shape),
        ],
        out_specs=pl.BlockSpec((lanes, mid.shape[1]), lambda p: (p, 0)),
        out_shape=jax.ShapeDtypeStruct((hidden, mid.shape[1]), F32),
        scratch_shapes=[pltpu.VMEM((rows, lanes), F32)],
        compiler_params=params(),
        name="attend_back",
    )(qkv, qkv, qkv, dctx, logs, seg_wide, seg_row, mid)


MESH = pl.DeviceIdType.MESH


def position():
    dp, fsdp = lax.axis_index("dp"), lax.axis_index("fsdp")
    return {"x": dp, "z": fsdp // 4, "y": (fsdp // 2) % 2, "c": fsdp % 2}


def device_of(place):
    return (place["x"], (place["z"] * 2 + place["y"]) * 2 + place["c"])


def number_of(place):
    return place["x"] * 16 + (place["z"] * 2 + place["y"]) * 2 + place["c"]


def rank_device(number):
    return (number // 16, number % 16)


def greet_all(shards):
    barrier = pltpu.get_barrier_semaphore()
    me = lax.axis_index("dp") * 16 + lax.axis_index("fsdp")

    @pl.loop(1, shards)
    def _(k):
        pl.semaphore_signal(
            barrier, inc=1, device_id=rank_device((me + k) % shards), device_id_type=MESH
        )


def await_all(shards):
    pl.semaphore_wait(pltpu.get_barrier_semaphore(), shards - 1)


def direct_copy(source, target, sems, me, k, shards):
    return pltpu.make_async_remote_copy(
        src_ref=source,
        dst_ref=target,
        send_sem=sems.at[0],
        recv_sem=sems.at[1],
        device_id=rank_device((me + k) % shards),
        device_id_type=MESH,
    )


def spread(piece_of, buffer, sems, me, shards):
    @pl.loop(1, shards)
    def _(k):
        direct_copy(piece_of((me + k) % shards), buffer.at[me], sems, me, k, shards).start()


def collect(buffer, sems, me, shards):
    whole = buffer.at[pl.ds(0, shards - 1)]
    copy = direct_copy(whole, whole, sems, me, 1, shards)
    copy.wait_recv()
    copy.wait_send()


def relative_places(order):
    places = [
        {"x": dx, "z": dz, "y": dy} for dx in (0, 1) for dz in range(-3, 4) for dy in (0, 1)
    ]
    size = lambda p: abs(p["x"]) + abs(p["z"]) + abs(p["y"])
    return sorted(places, key=lambda p: (abs(p[order[-1]]), size(p), [abs(p[a]) for a in order]))


class Gather:
    def __init__(self, chunk, full_buffer, start, rows, order, sends, receives, hands, hands_got):
        self.chunk, self.full, self.order = chunk, full_buffer, order
        self.part = pl.ds(start, rows)
        self.sends, self.receives, self.hands, self.hands_got = sends, receives, hands, hands_got
        self.here = position()
        self.items = relative_places(order)
        self.pending = []

    def origin(self, item):
        here = self.here
        return {"x": (here["x"] + item["x"]) % 2, "z": here["z"] - item["z"], "y": (here["y"] + item["y"]) % 2, "c": here["c"]}

    def key(self, place):
        return (place["x"] * 4 + place["z"]) * 2 + place["y"]

    def outward(self, item):
        deepest = max([k for k, axis in enumerate(self.order) if item[axis]], default=-1)
        ways = []
        if deepest >= 0 and self.order[deepest] == "z":
            ways.append(("z", 1 if item["z"] > 0 else -1))
        for axis in self.order[deepest + 1 :]:
            ways += [("z", 1), ("z", -1)] if axis == "z" else [(axis, 1)]
        return ways

    def copy(self, index, way, slot, item):
        here = self.here
        place = self.origin(item)
        number, key = number_of(place), self.key(place)
        mine = not any(item.values())
        source = self.chunk.at[self.part, :] if mine else self.full.at[number, self.part, :]
        if way is None:
            target = dict(here, c=1 - here["c"])
            sends, receives = self.hands.at[index], self.hands_got.at[key]
        else:
            axis, step = way
            target = dict(here)
            target[axis] = here["z"] + step if axis == "z" else 1 - here[axis]
            sends, receives = self.sends.at[index * 4 + slot], self.receives.at[key]
        return pltpu.make_async_remote_copy(
            src_ref=source,
            dst_ref=self.full.at[number, self.part, :],
            send_sem=sends,
            recv_sem=receives,
            device_id=device_of(target),
            device_id_type=MESH,
        )

    def valid(self, item):
        z = self.here["z"] - item["z"]
        return (z >= 0) & (z <= 3)

    def step(self, index):
        item = self.items[index]

        @pl.when(self.valid(item))
        def _():
            if any(item.values()):
                self.arrived(index, item)
            for slot, way in enumerate(self.outward(item)):
                self.when_way(way, lambda way=way, slot=slot: self.copy(index, way, slot, item).start())
            self.copy(index, None, 0, item).start()

    def when_way(self, way, act):
        axis, step = way
        if axis == "z":
            z = self.here["z"] + step
            pl.when((z >= 0) & (z <= 3))(act)
        else:
            act()

    def arrived(self, index, item):
        place = self.origin(item)
        spot = self.full.at[number_of(place), self.part, :]
        pltpu.make_async_remote_copy(
            src_ref=spot,
            dst_ref=spot,
            send_sem=self.sends.at[index * 4],
            recv_sem=self.receives.at[self.key(place)],
            device_id=device_of(dict(self.here, c=1 - self.here["c"])),
            device_id_type=MESH,
        ).wait_recv()

    def finish(self):
        for index, item in enumerate(self.items):

            @pl.when(self.valid(item))
            def _(index=index, item=item):
                for slot, way in enumerate(self.outward(item)):
                    self.when_way(way, lambda way=way, slot=slot: self.copy(index, way, slot, item).wait_send())
                self.copy(index, None, 0, item).wait_send()
                place = dict(self.origin(item), c=1 - self.here["c"])
                spot = self.full.at[number_of(place), self.part, :]
                pltpu.make_async_remote_copy(
                    src_ref=spot,
                    dst_ref=spot,
                    send_sem=self.hands.at[index],
                    recv_sem=self.hands_got.at[self.key(place)],
                    device_id=device_of(dict(self.here, c=1 - self.here["c"])),
                    device_id_type=MESH,
                ).wait_recv()


ITEMS = 28


def start_body(
    streams, shards, fact, chunk, table_any, facts, full_chunk, et_out, e_ref, et_ref,
    fact_sems, own_sems, sends, receives, hands, hands_got,
):
    here = position()
    me = number_of(here)
    own = [
        pltpu.make_async_copy(source, target, own_sems.at[k])
        for k, (source, target) in enumerate(
            ((vocab_rows(table_any, e_ref), e_ref), (fact, facts.at[me]), (chunk, full_chunk.at[me]))
        )
    ]
    for copy in own:
        copy.start()
    greet_all(shards)
    await_all(shards)
    gathers = [
        Gather(
            chunk, full_chunk, start, size, order, sends.at[k], receives.at[k], hands.at[k], hands_got.at[k]
        )
        for k, (start, size, order) in enumerate(streams)
    ]
    for gather in gathers:
        gather.step(0)
    spread(lambda peer: fact, facts, fact_sems, me, shards)
    own[0].wait()
    blocks = e_ref.shape[0] // 128
    each = -(-blocks // (ITEMS - 1))
    for index in range(1, ITEMS):
        for k in range((index - 1) * each, min(index * each, blocks)):
            part = slice(k * 128, (k + 1) * 128)
            et_ref[:, part] = e_ref[part, :].astype(F32).T.astype(BF)
        for gather in gathers:
            gather.step(index)
    turned = pltpu.make_async_copy(et_ref, et_out, own_sems.at[3])
    turned.start()
    for gather in gathers:
        gather.finish()
    collect(facts, fact_sems, me, shards)
    for copy in own[1:] + [turned]:
        copy.wait()


def vocab_rows(table, like):
    here = position()
    count = like.shape[0]
    return table.at[pl.ds(pl.multiple_of((here["y"] * 2 + here["c"]) * count, 16), count), :]


def gather_sems(streams):
    sems = pltpu.SemaphoreType.DMA
    count = len(streams)
    return [sems((count, 4 * ITEMS)), sems((count, 16)), sems((count, ITEMS)), sems((count, 16))]


def streams_of(rows, parts):
    streams, start = [], 0
    for k, (order, share) in enumerate(parts):
        size = rows - start if k == len(parts) - 1 else round(rows * share / 16) * 16
        streams.append((start, size, order))
        start += size
    return streams


def start_exchange(fact, chunk, table, shards):
    anywhere = pl.BlockSpec(memory_space=pl.ANY)
    shape = jax.ShapeDtypeStruct
    sems = pltpu.SemaphoreType.DMA
    streams = streams_of(chunk.shape[0], (("zxy", 0.34), ("zyx", 0.34), ("xzy", 0.32)))
    count, hidden = table.shape[0] // 4, table.shape[1]
    return pl.pallas_call(
        functools.partial(start_body, streams, shards),
        in_specs=[anywhere] * 3,
        out_specs=[anywhere] * 3,
        out_shape=[
            shape((shards, *fact.shape), fact.dtype),
            shape((shards, *chunk.shape), chunk.dtype),
            shape((hidden, count), BF),
        ],
        scratch_shapes=[
            pltpu.VMEM((count, hidden), BF),
            pltpu.VMEM((hidden, count), BF),
            sems((2,)),
            sems((4,)),
            *gather_sems(streams),
        ],
        compiler_params=params(collective_id=1, has_side_effects=True),
        name="start_exchange",
    )(fact, chunk, table)


def first_layer_body(
    streams, shards,
    own_any, got_any, in_any, feed_any, chunk, code_ref, spots_ref, gain_ref, shift_ref, down_ref,
    adapt_ref, bias_ref, seg_ref, seg_row_ref,
    qkv_out, x_out, one_out, two_out, slope_out, wo_out, full_chunk, mid_ref, log_ref,
    own, got, in_slab, w, wo, up, dn, x, qkv, ctx, two, out, slope,
    load_sems, tile_sems, out_sems, sends, receives, hands, hands_got,
):
    here = position()
    me = number_of(here)
    rows, hidden = x.shape
    tile = split_of(rows, 256, 16)
    tiles = rows // tile
    lanes = 2 * (hidden // HEADS)
    pairs = hidden // lanes

    def slab(source, target, start):
        return source.at[:, pl.ds(start, target.shape[1]), :]

    loads = [
        pltpu.make_async_copy(source, target, load_sems.at[k])
        for k, (source, target) in enumerate(
            (
                (own_any.at[pl.ds(0, rows), :], own),
                (got_any.at[pl.ds(0, rows), :], got),
                (slab(in_any, in_slab, up.shape[1]), in_slab),
                (slab(in_any, up, 0), up),
                (slab(feed_any, dn, 0), dn),
                (chunk, full_chunk.at[me]),
            )
        )
    ]
    for copy in loads:
        copy.start()
    barrier = pltpu.get_barrier_semaphore()
    peers = [
        dict(here, c=1 - here["c"]),
        dict(here, x=1 - here["x"]),
        dict(here, y=1 - here["y"]),
        *[dict(here, z=flip(here["z"], k)) for k in (1, 2, 3)],
    ]
    for peer in peers:
        pl.semaphore_signal(barrier, inc=1, device_id=device_of(peer), device_id_type=MESH)
    pl.semaphore_wait(barrier, len(peers))
    gathers = [
        Gather(
            chunk, full_chunk, start, size, order, sends.at[k], receives.at[k], hands.at[k], hands_got.at[k]
        )
        for k, (start, size, order) in enumerate(streams)
    ]
    def advance(first, last):
        for index in range(first, last + 1):
            for gather in gathers:
                gather.step(index)

    advance(0, 0)
    for copy in loads[:3]:
        copy.wait()
    unpack_rows(in_slab, (w, wo))

    @pl.loop(0, tiles)
    def _(i):
        part = pl.ds(pl.multiple_of(i * tile, tile), tile)
        project_body(
            own.at[part, :], got.at[part, :], code_ref.at[part, :], spots_ref, gain_ref, shift_ref, down_ref, w,
            adapt_ref, bias_ref, qkv.at[part, :], mid_ref.at[part, :], x.at[part, :],
        )

        @pl.when(i == tiles - 3)
        def _():
            advance(1, 3)

        @pl.when(i == tiles - 1)
        def _():
            advance(4, 5)

    early = [
        pltpu.make_async_copy(qkv, qkv_out, out_sems.at[0]),
        pltpu.make_async_copy(wo, wo_out, out_sems.at[1]),
    ]
    for copy in early:
        copy.start()

    @pl.loop(0, pairs)
    def _(p):
        column = lambda kind: pl.ds(pl.multiple_of((kind * pairs + p) * lanes, lanes), lanes)
        attend_body(
            qkv.at[:, column(0)], qkv.at[:, column(1)], qkv.at[:, column(2)], seg_ref, seg_row_ref,
            ctx.at[:, column(0)], log_ref.at[pl.ds(p, 1)],
        )

        for k, (first, last) in {1: (6, 7), 3: (8, 9), 5: (10, 13)}.items():
            pl.when(p == pairs - 6 + k)(functools.partial(advance, first, last))

    for copy in loads[3:5]:
        copy.wait()

    def tile_copies(i):
        part = pl.ds(pl.multiple_of(i * tile, tile), tile)
        turn = i % 2
        return [
            pltpu.make_async_copy(source, target.at[part, :], tile_sems.at[k, i])
            for k, (source, target) in enumerate(
                (
                    (out.at[turn], x_out),
                    (two.at[turn], two_out),
                    (slope.at[turn], slope_out),
                    (x.at[part, :], one_out),
                )
            )
        ]

    plan = {tiles - 4: (14, 16), tiles - 3: (17, 19), tiles - 2: (20, 23), tiles - 1: (24, 27)}

    @pl.loop(0, tiles)
    def _(i):
        part = pl.ds(pl.multiple_of(i * tile, tile), tile)
        turn = i % 2

        @pl.when(i >= 2)
        def _():
            for copy in tile_copies(i - 2):
                copy.wait()

        after_body(
            ctx.at[part, :], x.at[part, :], wo, up, dn, bias_ref, gain_ref, shift_ref, out.at[turn],
            x.at[part, :], two.at[turn], slope.at[turn],
        )
        for copy in tile_copies(i):
            copy.start()
        for k, (first, last) in plan.items():
            pl.when(i == k)(functools.partial(advance, first, last))

    for gather in gathers:
        gather.finish()
    for i in (tiles - 2, tiles - 1):
        for copy in tile_copies(i):
            copy.wait()
    for copy in early + loads[5:]:
        copy.wait()


def first_layer(own, got, first_in, feed, chunk, more, shards):
    whole = pl.BlockSpec(memory_space=pltpu.VMEM)
    anywhere = pl.BlockSpec(memory_space=pl.ANY)
    code, down = more[0], more[4]
    rows, hidden = code.shape[0], own.shape[1]
    tile = split_of(rows, 256, 16)
    pairs = HEADS // 2
    units = 4 * hidden
    each = units // shards
    shape = jax.ShapeDtypeStruct
    sems = pltpu.SemaphoreType.DMA
    streams = streams_of(chunk.shape[0], (("zxy", 0.4), ("zyx", 0.4), ("xyz", 0.2)))
    return pl.pallas_call(
        functools.partial(first_layer_body, streams, shards),
        in_specs=[anywhere] * 5 + [whole] * len(more),
        out_specs=[anywhere] * 7 + [whole] * 2,
        out_shape=[
            shape((rows, 3 * hidden), BF),
            shape((rows, hidden), F32),
            shape((rows, hidden), F32),
            shape((rows, hidden), F32),
            shape((rows, units), BF),
            shape((hidden, hidden), BF),
            shape((shards, *chunk.shape), BF),
            shape((rows, down.shape[2]), BF),
            shape((pairs, 1, 2 * rows), F32),
        ],
        scratch_shapes=[
            pltpu.VMEM((rows, hidden), BF),
            pltpu.VMEM((rows, hidden), BF),
            pltpu.VMEM((shards, 4 * hidden // shards, hidden), BF),
            pltpu.VMEM((3 * hidden, hidden), BF),
            pltpu.VMEM((hidden, hidden), BF),
            pltpu.VMEM((shards, each, hidden), BF),
            pltpu.VMEM((shards, each, hidden), BF),
            pltpu.VMEM((rows, hidden), F32),
            pltpu.VMEM((rows, 3 * hidden), BF),
            pltpu.VMEM((rows, hidden), BF),
            pltpu.VMEM((2, tile, hidden), F32),
            pltpu.VMEM((2, tile, hidden), F32),
            pltpu.VMEM((2, tile, units), BF),
            sems((6,)),
            sems((4, rows // tile)),
            sems((2,)),
            *gather_sems(streams),
        ],
        compiler_params=params(collective_id=3, has_side_effects=True),
        name="first_layer",
    )(own, got, first_in, feed, chunk, *more)


PICK = 64
GROUP = 16


def look_up_body(ids, low_ref, table, out_ref, stage):
    @pl.loop(0, out_ref.shape[0] // PICK)
    def _(b):
        part = pl.ds(pl.multiple_of(b * PICK, PICK), PICK)

        def one(t, carry):
            stage[t] = table[ids[b * PICK + t]]
            return carry

        lax.fori_loop(0, PICK, one, 0, unroll=8)
        choose = lax.broadcasted_iota(jnp.int32, (PICK, PICK * GROUP), 1) == low_ref[part, :]
        out_ref[part, :] = mm(choose.astype(F32).astype(BF), flat(stage)).astype(BF)


def look_up(ids, table):
    whole = pl.BlockSpec(memory_space=pltpu.VMEM)
    hidden = table.shape[1]
    low = jnp.arange(ids.size, dtype=jnp.int32) % PICK * GROUP + ids % GROUP
    return pl.pallas_call(
        look_up_body,
        in_specs=[pl.BlockSpec(memory_space=pltpu.SMEM), whole, whole],
        out_specs=whole,
        out_shape=jax.ShapeDtypeStruct((ids.size, hidden), table.dtype),
        scratch_shapes=[pltpu.VMEM((PICK, GROUP, hidden), table.dtype)],
        compiler_params=params(),
        name="look_up",
    )(ids // GROUP, low[:, None], table.reshape(-1, GROUP, hidden))


def adam(weight, gradient, moment_one, moment_two, fade_one, fade_two):
    moment_one = beta_first * moment_one + (1.0 - beta_first) * gradient
    moment_two = beta_second * moment_two + (1.0 - beta_second) * gradient * gradient
    one_hat = moment_one / fade_one
    two_hat = moment_two / fade_two
    weight = weight - learn_rate * (one_hat / (jnp.sqrt(two_hat) + adam_eps) + decay_rate * weight)
    return (weight, moment_one, moment_two)


BACK_TILE = 256


def finish_body(
    shards, edge,
    dout_any, one_any, two_any, slope_any, wo_any, up_any, dn_any, qkv_any, gain_ref, log_ref, seg_ref,
    seg_row_ref, mid_ref, parts, late_ref, facts,
    sums_ref, dense_ref, total_ref,
    dout, one, two, slope, wo, up, dn, qkv, dctx, dv, grad, core_got, chip_sum, dense_got, grad_got, note, notes,
    tile_sems, load_sems, core_sems, dense_sems, grad_sems, note_sems,
):
    rows, hidden = dout.shape
    tile = split_of(rows, BACK_TILE, 16)
    tiles = rows // tile
    me = number_of(position())

    def tile_loads(i):
        part = pl.ds(pl.multiple_of(i * tile, tile), tile)
        return [
            pltpu.make_async_copy(source.at[part, :], target.at[part, :], tile_sems.at[k, i])
            for k, (source, target) in enumerate(
                ((two_any, two), (dout_any, dout), (slope_any, slope), (one_any, one))
            )
        ]

    here = position()
    chips = shards // 2
    chip, core = me // 2, here["c"]
    to_core = pltpu.make_async_remote_copy(
        src_ref=parts.at[:, 1 - core],
        dst_ref=core_got,
        send_sem=core_sems.at[0],
        recv_sem=core_sems.at[1],
        device_id=device_of(dict(here, c=1 - core)),
        device_id_type=MESH,
    )

    def to_chip(k):
        peer = (chip + k) % chips
        return pltpu.make_async_remote_copy(
            src_ref=chip_sum.at[peer],
            dst_ref=dense_got.at[chip],
            send_sem=dense_sems.at[0],
            recv_sem=dense_sems.at[1],
            device_id=rank_device(2 * peer + core),
            device_id_type=MESH,
        )

    loads = [
        pltpu.make_async_copy(source, target, load_sems.at[k])
        for k, (source, target) in enumerate(
            (
                (dn_any.at[:, pl.ds(0, dn.shape[1]), :], dn),
                (up_any.at[:, pl.ds(0, up.shape[1]), :], up),
                (wo_any, wo),
                (qkv_any, qkv),
            )
        )
    ]
    for copy in tile_loads(0) + loads[:3]:
        copy.start()
    for i in range(1, tiles):
        for copy in tile_loads(i):
            copy.start()
    loads[3].start()
    greet_all(shards)
    for copy in loads[:3]:
        copy.wait()

    @pl.loop(0, tiles)
    def _(i):
        for copy in tile_loads(i):
            copy.wait()
        part = pl.ds(pl.multiple_of(i * tile, tile), tile)
        after_back_body(
            dout.at[part, :], one.at[part, :], two.at[part, :], slope.at[part, :], wo, up, dn, gain_ref,
            dctx.at[part, :],
        )

        @pl.when(i == 0)
        def _():
            await_all(shards)
            to_core.start()

        @pl.when(i == 1)
        def _():
            to_core.wait_recv()

            @pl.loop(0, chips)
            def _(k):
                chip_sum[k] = (parts[k, core].astype(F32) + core_got[k].astype(F32)).astype(BF)

            dense_got[chip] = chip_sum[chip]

            @pl.loop(1, chips)
            def _(k):
                to_chip(k).start()

    loads[3].wait()
    lanes = 2 * (hidden // HEADS)
    pairs = hidden // lanes

    @pl.loop(0, pairs)
    def _(p):
        column = lambda kind: pl.ds(pl.multiple_of((kind * pairs + p) * lanes, lanes), lanes)
        attend_back_body(
            qkv.at[:, column(0)], qkv.at[:, column(1)], qkv.at[:, column(2)], dctx.at[:, column(0)],
            log_ref.at[pl.ds(p, 1)], seg_ref, seg_row_ref, mid_ref, grad.at[column(0), :], dv, edge=edge,
        )

    grad[...] = grad[...] + late_ref[...]
    each = hidden // shards
    piece = lambda peer: grad.at[pl.ds(pl.multiple_of(peer * each, each), each), :]
    grad_got[me] = piece(me)[...]
    spread(piece, grad_got, grad_sems, me, shards)
    others = chip_sum.at[pl.ds(0, chips - 1)]
    every = pltpu.make_async_remote_copy(
        src_ref=others,
        dst_ref=dense_got.at[pl.ds(0, chips - 1)],
        send_sem=dense_sems.at[0],
        recv_sem=dense_sems.at[1],
        device_id=device_of(dict(here, c=1 - core)),
        device_id_type=MESH,
    )
    every.wait_recv()
    every.wait_send()
    to_core.wait_send()
    dense = jnp.zeros((each, hidden), F32)
    for k in range(chips):
        dense = dense + dense_got[k].astype(F32)[:each, :]
    dense_ref[...] = dense
    square = jnp.sum(dense * dense, keepdims=True)
    collect(grad_got, grad_sems, me, shards)
    total = grad_got[0]
    for k in range(1, shards):
        total = total + grad_got[k]
    total_ref[...] = total
    square = square + jnp.sum(total * total, keepdims=True)
    row = lax.broadcasted_iota(jnp.int32, note.shape, 0)
    note[...] = jnp.where(row == 0, facts[...], jnp.where(row == 1, square, 0.0))
    notes[me] = note[...]
    spread(lambda peer: note, notes, note_sems, me, shards)
    collect(notes, note_sems, me, shards)
    sums = notes[0]
    for k in range(1, shards):
        sums = sums + notes[k]
    sums_ref[...] = sums


def update_body(
    sums_ref, dense_ref, total_ref, facts, head_w, head_m, head_v, adapt_w, adapt_m, adapt_v,
    loss_out, norm_out, head_w_out, head_m_out, head_v_out, adapt_w_out, adapt_m_out, adapt_v_out,
):
    norm = jnp.sqrt(sums_ref[1:2, 0:1])
    loss_out[...] = sums_ref[0:1, 0:1]
    norm_out[...] = norm
    factor = jnp.minimum(1.0, clip_limit / (norm + 1e-06))
    fades = facts[1:2, 0:1], facts[2:3, 0:1]
    new = adam(head_w[...], dense_ref[...] * factor, head_m[...], head_v[...], *fades)
    head_w_out[...], head_m_out[...], head_v_out[...] = new
    grad = (total_ref[...] * factor).T
    layers, kinds, rank, unused = adapt_w.shape
    for layer in range(layers):
        for kind in range(kinds):
            at = (layer * kinds + kind) * rank
            new = adam(
                adapt_w[layer, kind], grad[at : at + rank], adapt_m[layer, kind], adapt_v[layer, kind], *fades
            )
            adapt_w_out[layer, kind], adapt_m_out[layer, kind], adapt_v_out[layer, kind] = new


def update(sums, dense, total, facts, heads, adapts):
    whole = pl.BlockSpec(memory_space=pltpu.VMEM)
    shape = jax.ShapeDtypeStruct
    return pl.pallas_call(
        update_body,
        in_specs=[whole] * 10,
        out_specs=[whole] * 8,
        out_shape=[shape((1, 1), F32)] * 2 + [shape(a.shape, F32) for a in (*heads, *adapts)],
        compiler_params=params(),
        name="update",
    )(sums, dense, total, facts, *heads, *adapts)


def finish(back, qkv, logs, seg_wide, seg_row, mid, parts, late, facts, edge, shards):
    dout, one, two, slope, wo, up, dn, gains = back
    parts = parts.reshape(-1, 2, *parts.shape[1:])
    rows, hidden = dout.shape
    each = hidden // shards
    whole = pl.BlockSpec(memory_space=pltpu.VMEM)
    anywhere = pl.BlockSpec(memory_space=pl.ANY)
    shape = jax.ShapeDtypeStruct
    sems = pltpu.SemaphoreType.DMA
    tiles = rows // split_of(rows, BACK_TILE, 16)
    return pl.pallas_call(
        functools.partial(finish_body, shards, edge),
        in_specs=[anywhere] * 8 + [whole] * 8,
        out_specs=[whole] * 3,
        out_shape=[
            shape((8, 128), F32),
            shape((each, hidden), F32),
            shape((each, late.shape[1]), F32),
        ],
        scratch_shapes=[
            pltpu.VMEM((rows, hidden), F32),
            pltpu.VMEM((rows, hidden), F32),
            pltpu.VMEM((rows, hidden), F32),
            pltpu.VMEM(slope.shape, BF),
            pltpu.VMEM(wo.shape, BF),
            slab_scratch(up),
            slab_scratch(dn),
            pltpu.VMEM(qkv.shape, BF),
            pltpu.VMEM((rows, hidden), BF),
            pltpu.VMEM((rows, 2 * (hidden // HEADS)), F32),
            pltpu.VMEM(late.shape, F32),
            pltpu.VMEM((shards // 2, *parts.shape[2:]), BF),
            pltpu.VMEM((shards // 2, *parts.shape[2:]), BF),
            pltpu.VMEM((shards // 2, *parts.shape[2:]), BF),
            pltpu.VMEM((shards, each, late.shape[1]), F32),
            pltpu.VMEM((8, 128), F32),
            pltpu.VMEM((shards, 8, 128), F32),
            sems((4, tiles)),
            sems((4,)),
            sems((2,)),
            sems((2,)),
            sems((2,)),
            sems((2,)),
        ],
        compiler_params=params(collective_id=2, has_side_effects=True),
        name="finish",
    )(dout, one, two, slope, wo, up[0], dn[0], qkv, gains, logs, seg_wide, seg_row, mid, parts, late, facts)


LOG_ROWS = 16


def flip(z, k):
    return (z % 2 + k % 2) % 2 + 2 * ((z // 2 + k // 2) % 2)


def pack_log(log_row, rows):
    high = log_row.astype(BF).astype(F32)
    middle = (log_row - high).astype(BF).astype(F32)
    low = log_row - high - middle
    row = lax.broadcasted_iota(jnp.int32, (rows, log_row.shape[1]), 0)
    return jnp.where(
        row == 0, high, jnp.where(row == 1, middle, jnp.where(row == 2, low, 0.0))
    ).astype(BF)


def unpack(block, hidden):
    logs = block[hidden : hidden + LOG_ROWS, :].astype(F32)
    return block[:hidden, :].astype(F32), jnp.sum(logs, 0, keepdims=True)


def merged(one, two):
    top = jnp.maximum(one[1], two[1])
    first, second = jnp.exp(one[1] - top), jnp.exp(two[1] - top)
    total = first + second
    inverse = 1.0 / total
    return one[0] * (first * inverse) + two[0] * (second * inverse), top + jnp.log(total)


def store_packed(ref, pair, hidden):
    ref[:hidden, :] = pair[0].astype(BF)
    ref[hidden : hidden + LOG_ROWS, :] = pack_log(pair[1], LOG_ROWS)


def head_body(
    u_ref, bias_ref, table_any, et_any, mean_ref, log_ref,
    e_ref, et_ref, bias_wide, feats, packs, handed, sums,
    loads, far_send, far_get, hand_send, hand_get, part_send, part_get, sum_send, sum_get,
):
    here = position()
    x, y, c = here["x"], here["y"], here["c"]
    labels, hidden = u_ref.shape
    sibling = device_of(dict(here, c=1 - c))

    def chip_at(k):
        return (x + k % 2) % 2, (y + k // 2) % 2

    def device_at(k):
        there = chip_at(k)
        return device_of(dict(here, x=there[0], y=there[1]))

    def slot(k, core):
        there = chip_at(k)
        return (there[0] * 2 + there[1]) * 2 + core

    fills = [
        pltpu.make_async_copy(source, target, loads.at[k])
        for k, (source, target) in enumerate(
            ((vocab_rows(table_any, e_ref), e_ref), (et_any, et_ref))
        )
    ]
    for fill in fills:
        fill.start()
    barrier = pltpu.get_barrier_semaphore()
    for target in (sibling, *[device_at(k) for k in (1, 2, 3)]):
        pl.semaphore_signal(barrier, inc=1, device_id=target, device_id_type=MESH)
    feats[slot(0, c)] = u_ref[...]
    pl.semaphore_wait(barrier, 4)

    def move(place, device, send, get):
        return pltpu.make_async_remote_copy(
            src_ref=feats.at[place],
            dst_ref=feats.at[place],
            send_sem=send,
            recv_sem=get,
            device_id=device,
            device_id_type=MESH,
        )

    def far(k):
        return move(slot(0, c), device_at(k), far_send.at[k], far_get.at[k])

    def far_here(k):
        return move(slot(k, c), device_at(k), far_send.at[k], far_get.at[k])

    def hand(k, core):
        return move(slot(k, core), sibling, hand_send.at[k], hand_get.at[k])

    for k in (1, 2, 3):
        far(k).start()
    hand(0, c).start()

    @pl.loop(0, bias_ref.shape[0])
    def _(b):
        row = jnp.broadcast_to(bias_ref[pl.ds(b, 1), :], (128, 128))
        bias_wide[pl.ds(pl.multiple_of(b * 128, 128), 128), :] = row.T

    for k in (1, 2, 3):
        far_here(k).wait_recv()
        hand(k, c).start()
    for fill in fills:
        fill.wait()
    count = e_ref.shape[0]
    steps = 4

    def target_of(s):
        return (s + 1) % steps

    def hand_part(s):
        return pltpu.make_async_remote_copy(
            src_ref=packs.at[s, 1 - c],
            dst_ref=handed.at[s],
            send_sem=part_send.at[s],
            recv_sem=part_get.at[s],
            device_id=sibling,
            device_id_type=MESH,
        )

    def sum_part(s):
        return pltpu.make_async_remote_copy(
            src_ref=packs.at[s, c],
            dst_ref=sums.at[s],
            send_sem=sum_send.at[s],
            recv_sem=sum_get.at[s],
            device_id=device_at(target_of(s)),
            device_id_type=MESH,
        )

    def together(s):
        hand_part(s).wait_recv()
        return merged(unpack(packs[s, c], hidden), unpack(handed[s], hidden))

    def settle(s):
        store_packed(packs.at[s, c], together(s), hidden)
        sum_part(s).start()

    @pl.loop(0, steps)
    def _(s):
        k = target_of(s)
        hand(k, 1 - c).wait_recv()
        u = feats[pl.ds(slot(k, 0), 2)].reshape(2 * labels, hidden)
        top = total = mean = None

        def scored(start):
            part = slice(start, min(start + 1280, count))
            bias = bias_wide[part, :]
            return mm_nt(e_ref[part, :], u) + jnp.concatenate([bias, bias], 1)

        @pl.when(s > 0)
        def _():
            settle(s - 1)

        logits = scored(0)
        for start in range(0, count, 1280):
            part = slice(start, min(start + 1280, count))
            later = scored(start + 1280) if start + 1280 < count else None
            high = jnp.max(logits, 0, keepdims=True)
            new = high if top is None else jnp.maximum(top, high)
            grown = jnp.exp(logits - new)
            part_sums = jnp.sum(grown, 0, keepdims=True)
            product = mm(et_ref[:, part], grown.astype(BF))
            if top is None:
                total, mean = part_sums, product
            else:
                shrink = jnp.exp(top - new)
                total, mean = total * shrink + part_sums, mean * shrink + product
            top = new
            logits = later
        mean = mean * (1.0 / total)
        logs = top + jnp.log(total)
        for core in range(2):
            half = slice(core * labels, (core + 1) * labels)
            packs[s, core, :hidden, :] = mean[:, half].astype(BF)
            packs[s, core, hidden : hidden + LOG_ROWS, :] = pack_log(logs[:, half], LOG_ROWS)
        hand_part(s).start()

    total = together(steps - 1)
    for s in range(steps - 1):
        sum_part(s).wait_recv()
        total = merged(total, unpack(sums[s], hidden))
    mean_ref[...] = total[0]
    log_ref[...] = total[1]
    for k in (1, 2, 3):
        far(k).wait_send()
    for k in range(4):
        hand(k, c).wait_send()
    for s in range(steps):
        hand_part(s).wait_send()
    for s in range(steps - 1):
        sum_part(s).wait_send()


def head(u, bias, table, et):
    labels, hidden = u.shape
    whole = pl.BlockSpec(memory_space=pltpu.VMEM)
    anywhere = pl.BlockSpec(memory_space=pl.ANY)
    shape = jax.ShapeDtypeStruct
    sems = pltpu.SemaphoreType.DMA
    block = (hidden + LOG_ROWS, labels)
    count = et.shape[1]
    return pl.pallas_call(
        head_body,
        in_specs=[whole] * 2 + [anywhere] * 2,
        out_specs=[whole] * 2,
        out_shape=[shape((hidden, labels), F32), shape((1, labels), F32)],
        scratch_shapes=[
            pltpu.VMEM((count, hidden), BF),
            pltpu.VMEM((hidden, count), BF),
            pltpu.VMEM((count, 128), F32),
            pltpu.VMEM((8, labels, hidden), BF),
            pltpu.VMEM((4, 2, *block), BF),
            pltpu.VMEM((4, *block), BF),
            pltpu.VMEM((4, *block), BF),
            sems((2,)),
        ]
        + [sems((4,))] * 8,
        compiler_params=params(collective_id=4, has_side_effects=True),
        name="head",
    )(u, bias, table, et)


def seg_positions(segments):
    index = jnp.arange(segments.shape[-1], dtype=jnp.int32)
    fresh = jnp.concatenate([jnp.ones((1,), dtype=bool), segments[1:] != segments[:-1]], -1)
    starts = lax.cummax(jnp.where(fresh, index, jnp.zeros_like(index)), axis=0)
    return index - starts


def pad_rows(matrix, multiple):
    return jnp.pad(matrix, ((0, -matrix.shape[0] % multiple), (0, 0)))


def slab_of(gathered, start, rows):
    if rows % 16 == 0 and start % rows == 0:
        return (gathered, start // rows, rows)
    part = gathered[:, start : start + rows].reshape(1, -1, gathered.shape[2])
    return (part, 0, part.shape[1])


def per_device(
    input_token_index,
    sentence_numbers,
    label_positions,
    label_target_token,
    sequence_task_index,
    task_loss_weight,
    optimizer_step_count,
    embed,
    position_embedding,
    norm_gain_vector,
    norm_bias_vector,
    attention_in_weight,
    attention_out_weight,
    feedforward_up,
    feedforward_down,
    layer_bias_vector,
    head_dense_bias,
    vocabulary_bias,
    adapter_down_matrix,
    adapter_up_matrix,
    adapter_moment_first,
    adapter_moment_second,
    head_projection,
    head_moment_first,
    head_moment_second,
):
    shards = lax.axis_size("dp") * lax.axis_size("fsdp")
    dp_index = lax.axis_index("dp")
    fsdp_index = lax.axis_index("fsdp")
    layers, unused, rank, up_part = adapter_up_matrix.shape
    hidden = embed.shape[1]
    tokens = input_token_index.shape[1]
    labels = label_positions.shape[1]
    qkv_rows = attention_in_weight.shape[2]
    out_rows = attention_out_weight.shape[2]
    ff_rows = feedforward_up.shape[2]
    head_rows = head_projection.shape[0]

    grouped = (lax.axis_size("dp"), lax.axis_size("fsdp")) == (2, 16)
    feeds = [[feedforward_up[layer].T, feedforward_down[layer]] for layer in range(layers)]
    attends = [[attention_in_weight[layer].T, attention_out_weight[layer].T] for layer in range(layers)]
    first_in = lax.all_gather(
        jnp.concatenate([feeds[0][0], *attends[0]], 0), BOTH, axis=0, tiled=False
    )
    feed_chunk = feeds[0][1]
    last_chunk = pad_rows(
        jnp.concatenate([feeds[1][0], *attends[1], head_projection.astype(BF)], 0), 32
    )
    last_feed = feeds[1][1]

    table_rows = embed.shape[0]
    wanted = jnp.concatenate([input_token_index[0], label_target_token[0]])
    dp_count = lax.axis_size("dp")
    group_ids = lax.all_gather(wanted, "dp", axis=0, tiled=False) - dp_index * table_rows
    inside = (group_ids >= 0) & (group_ids < table_rows)
    group_ids = jnp.clip(group_ids, 0, table_rows - 1)
    mine = lax.dynamic_index_in_dim(inside, dp_index, 0, keepdims=False)

    task_range = jnp.arange(TASKS, dtype=jnp.int32)
    slice_rows = vocabulary_bias.shape[0]
    ups = adapter_up_matrix.reshape(-1)
    if grouped:
        ids_of = lambda part: lax.dynamic_index_in_dim(group_ids, part, 0, keepdims=False)
        other_rows = look_up(ids_of(1 - dp_index), embed)
        got = lax.ppermute(other_rows, "dp", [(0, 1), (1, 0)])
        own_ids, other_rows = lax.optimization_barrier((ids_of(dp_index), other_rows))
        own_rows = look_up(own_ids, embed)
        fact = jnp.concatenate([vocabulary_bias, ups, sequence_task_index.astype(F32)])
        fact_rows = -(-fact.size // 1024) * 8
        facts, feed_full, own_turned = start_exchange(
            jnp.pad(fact, (0, fact_rows * 128 - fact.size)).reshape(fact_rows, 128),
            feed_chunk,
            embed,
            shards,
        )
        last_feed, facts = lax.optimization_barrier((last_feed, facts))
        facts = facts.reshape(shards, -1)
        all_bias = facts[:, :slice_rows].reshape(-1)
        every_up = facts[:, slice_rows : slice_rows + ups.size]
        every_task = facts[:, slice_rows + ups.size].astype(jnp.int32)
    else:
        looked = jnp.where(
            inside.reshape(-1)[:, None], embed[group_ids.reshape(-1)], jnp.zeros((), BF)
        )
        own_rows = got = lax.psum_scatter(looked, "dp", scatter_dimension=0, tiled=True)
        all_bias = lax.all_gather(vocabulary_bias, BOTH, axis=0, tiled=True)
        every_up = lax.all_gather(ups, BOTH, axis=0, tiled=False)
        every_task = lax.all_gather(sequence_task_index, BOTH, axis=0, tiled=True)
    counts = labels * jnp.sum((every_task[:, None] == task_range[None, :]).astype(F32), 0)
    task_hot = (sequence_task_index[:, None] == task_range[None, :]).astype(F32)
    row_weight = jnp.sum(task_hot[0] * (task_loss_weight / jnp.maximum(counts, 1.0)))
    ups_full = (
        every_up.astype(BF)
        .reshape(shards, layers, 2, rank, up_part)
        .transpose(1, 2, 3, 0, 4)
        .reshape(layers, 2, rank, hidden)
    )
    blank = jnp.zeros((rank, hidden), BF)
    spare = lambda rows: jnp.zeros((rows, 3 * hidden), BF)
    adapters = jnp.stack(
        [
            jnp.concatenate(
                [
                    spare(2 * rank * layer),
                    jnp.concatenate([2 * ups_full[layer, 0], blank, blank], 1),
                    jnp.concatenate([blank, blank, 2 * ups_full[layer, 1]], 1),
                    spare(128 - 2 * rank * (layer + 1)),
                ],
                0,
            )
            for layer in range(layers)
        ]
    )
    downs = jnp.stack(
        [
            jnp.pad(
                jnp.concatenate([adapter_down_matrix[layer, 0], adapter_down_matrix[layer, 1]], 1),
                ((0, 0), (2 * rank * layer, 128 - 2 * rank * (layer + 1))),
            )
            for layer in range(layers)
        ]
    )
    target_rows = jnp.where(mine[tokens:, None], own_rows[tokens:], got[tokens:])
    segments = sentence_numbers[0]
    code = (2 * seg_positions(segments) + mine[:tokens].astype(jnp.int32))[:, None]
    seg_real = segments.astype(F32)
    seg_wide = jnp.broadcast_to(seg_real[:, None], (tokens, 128))
    seg_row = seg_real[None, :]
    place_row = label_positions
    place_col = jnp.broadcast_to(label_positions.reshape(labels, 1), (labels, 128))

    target_bias = all_bias[label_target_token[0]]

    gains, shifts = norm_gain_vector, norm_bias_vector
    last_inputs = (place_col, place_row, seg_wide, downs, adapters, layer_bias_vector)
    in_start = ff_rows
    last_dn = lax.all_gather(last_feed, BOTH, axis=0, tiled=False)
    slabs_of = lambda up_full, dn_full: (slab_of(up_full, 0, ff_rows), slab_of(dn_full, 0, ff_rows))
    if grouped:
        more = (
            code, position_embedding, gains, shifts, downs, adapters, layer_bias_vector, seg_wide, seg_row,
        )
        qkv, x_last, one, two, slope, out_first, last_full, mid, logs = first_layer(
            own_rows, got, first_in, feed_full, last_chunk, more, shards
        )
        slabs = [slabs_of(first_in, feed_full), slabs_of(last_full, last_dn)]
        *saved, in_last, out_last, head_full = last_forward(
            x_last, *last_inputs, (last_full,), (in_start, in_start + qkv_rows + out_rows), *slabs[1], gains,
            shifts, head_dense_bias[None, :],
        )
        count = own_turned.shape[1]
        own_bias = lax.dynamic_slice_in_dim(
            all_bias, dp_index * table_rows + fsdp_index % 4 * count, count, 0
        ).reshape(-1, 128)
        mean_t, own_logs = head(saved[-1], own_bias, embed, own_turned)
    else:
        feed_full = lax.all_gather(feed_chunk, BOTH, axis=0, tiled=False)
        last_full = lax.all_gather(last_chunk, BOTH, axis=0, tiled=False)
        slabs = [slabs_of(first_in, feed_full), slabs_of(last_full, last_dn)]
        taken = lambda full_chunk, start, size: full_chunk[:, start : start + size].reshape(-1, hidden)
        in_first = taken(first_in, ff_rows, qkv_rows)
        out_first = taken(first_in, ff_rows + qkv_rows, out_rows)
        in_last = taken(last_full, in_start, qkv_rows)
        out_last = taken(last_full, in_start + qkv_rows, out_rows)
        head_full = taken(last_full, in_start + qkv_rows + out_rows, head_rows)
        qkv, mid, hidden_rows = project(
            own_rows, got, code, position_embedding, gains, shifts, downs, in_first, adapters, layer_bias_vector
        )
        context, logs = attend(qkv, seg_wide, seg_row)
        x_last, one, two, slope = after(
            context, hidden_rows, out_first, *slabs[0], layer_bias_vector, gains, shifts
        )
        saved = last_forward(
            x_last, *last_inputs, (in_last, out_last, head_full), None, *slabs[1], gains, shifts,
            head_dense_bias[None, :],
        )
        features = saved[-1]
        own_slice = lax.dynamic_slice_in_dim(embed, fsdp_index * slice_rows, slice_rows, 0)
        own_vocab = jnp.concatenate(
            [own_slice]
            + [
                lax.ppermute(
                    own_slice, "dp", [(k, (k + shift) % dp_count) for k in range(dp_count)]
                )
                for shift in range(1, dp_count)
            ],
            0,
        )
        own_bias = jnp.concatenate(
            [
                lax.dynamic_slice_in_dim(
                    all_bias,
                    ((dp_index - shift) % dp_count) * table_rows + fsdp_index * slice_rows,
                    slice_rows,
                    0,
                )
                for shift in range(dp_count)
            ]
        )
        bias_wide = jnp.broadcast_to(own_bias[:, None], (own_bias.shape[0], 128))
        every = lax.all_gather(features, "fsdp", axis=0, tiled=True)
        means, local_logs = vocab(every, own_vocab, own_vocab.T, bias_wide, labels)
        local_logs = local_logs.reshape(-1, labels)
        all_logs = lax.all_gather(local_logs, "fsdp", axis=0, tiled=False)
        whole_logs = jax.nn.logsumexp(all_logs, axis=0)
        scaled = (means * jnp.exp(local_logs - whole_logs)[:, None, :]).astype(BF)
        mean_t = lax.psum_scatter(scaled, "fsdp", scatter_dimension=0, tiled=True)[0].astype(F32)
        own_logs = lax.dynamic_index_in_dim(whole_logs, fsdp_index, 0, keepdims=False)
        own_logs = own_logs[None, :]

    step_as_real = optimizer_step_count[0].astype(F32)
    fades = (1.0 - beta_first**step_as_real, 1.0 - beta_second**step_as_real)
    lanes = lambda value: jnp.pad(
        jnp.broadcast_to(value, (1, value.size if value.ndim else 128)), ((0, 0), (0, 128))
    )[:, :128]
    facts = jnp.concatenate(
        [lanes(value) for value in (row_weight, *fades, target_bias)] + [jnp.zeros((4, 128), F32)]
    )
    hidden_grad, dense_gradient, late, facts = last_backward(
        mean_t, own_logs, target_rows, facts, saved, place_col, place_row, seg_wide, downs, in_last, adapters,
        out_last, *slabs[1], gains, head_full, 3 * rank, shards if grouped else None,
    )
    back = (hidden_grad, one, two, slope, out_first, *slabs[0], gains)
    adapts = (adapter_up_matrix, adapter_moment_first, adapter_moment_second)
    heads = (head_projection, head_moment_first, head_moment_second)
    if grouped:
        sums, dense_portion, adapter_portion = finish(
            back, qkv, logs, seg_wide, seg_row, mid, dense_gradient, late, facts, rank, shards
        )
        loss, norm, *new = update(sums, dense_portion, adapter_portion, facts, heads, adapts)
        return (loss[0, 0], norm[0, 0], *new[3:], *new[:3])
    dctx = after_back(*back)
    first = attend_back(qkv, dctx, logs, seg_wide, seg_row, mid, rank)
    adapter_gradient = (first + late)[:, : 2 * rank * layers].T.reshape(layers, 2, rank, hidden)
    dense_portion = lax.psum_scatter(dense_gradient, BOTH, scatter_dimension=0, tiled=True)
    adapter_portion = lax.psum_scatter(adapter_gradient, BOTH, scatter_dimension=3, tiled=True)
    squared_entries = jnp.sum(adapter_portion * adapter_portion) + jnp.sum(dense_portion * dense_portion)
    masked_task_loss, norm_square = lax.psum((facts[0, 0], squared_entries), BOTH)
    gradient_norm = jnp.sqrt(norm_square)
    factor = jnp.minimum(1.0, clip_limit / (gradient_norm + 1e-06))
    adapter_new = adam(adapts[0], adapter_portion * factor, *adapts[1:], *fades)
    dense_new = adam(heads[0], dense_portion * factor, *heads[1:], *fades)
    return (masked_task_loss, gradient_norm, *adapter_new, *dense_new)


def solution(mesh):
    rows = P(BOTH, None)
    in_specs = (
        rows,
        rows,
        rows,
        rows,
        P(BOTH),
        P(),
        P(),
        P("dp", None),
        P(),
        P(),
        P(),
        P(None, None, BOTH),
        P(None, None, BOTH),
        P(None, None, BOTH),
        P(None, BOTH, None),
        P(),
        P(),
        P(BOTH),
        P(),
        P(None, None, None, BOTH),
        P(None, None, None, BOTH),
        P(None, None, None, BOTH),
        rows,
        rows,
        rows,
    )
    adapter = P(None, None, None, BOTH)
    out_specs = (P(), P(), adapter, adapter, adapter, rows, rows, rows)
    return jax.shard_map(
        per_device, mesh=mesh, in_specs=in_specs, out_specs=out_specs, check_vma=False
    )
```

profile of v0, /device:TPU:0, one launch (start us, length us, event | category | flops | bytes accessed | tf_op | source)
XLA Modules:
  0.0 398.1 jit_solution(15858457266298620085)
XLA Ops:
  7.2 1.4 slice_bitcast_fusion.6
  8.7 1.6 slice_bitcast_fusion.4
  10.3 1.7 slice_bitcast_fusion.1
  12.0 0.7 pad_maximum_fusion.2
  13.4 0.1 reshape.249
  13.5 0.1 concatenate.46
  13.6 0.6 pad_bitcast_fusion.2.fact
  14.2 0.7 slice_bitcast_fusion
  15.0 53.5 %start_exchange.1 = (f32[32,24,128]{2,1,0:T(8,128)}, bf16[32,96,768]{2,1,0:T(8,128)(2,1)}, bf16[768,6400]{1,0:T(8,128)(2,1)}) custom-call(f32[24,128]{1,0:T(8,128)} %pad_bitcast_fusion.2.fact, bf16[96,768]{1,0:T(8,128)(2,1)} %get-tuple-element.105.chunk, bf16[25600,768]{1,0:T(8,128)(2,1)} %table_any.3), custom_call_target="tpu_custom_call" | custom-call | tf_op jit(solution)/shard_map/start_exchange/pallas_call | solution.py:1005
  68.6 4.8 %all-gather.3 = s32[2,1,1152]{2,1,0:T(1,128)S(1)} all-gather(s32[1,1,1152]{2,1,0:T(1,128)S(1)} %reshape.280), channel_id=2, replica_groups=mesh['dp'=2,'fsdp'=16] {'dp'}, dimensions={0}, use_global_device_ids=true | all-gather | bytes 13824 | tf_op jit(solution)/shard_map/all_gather | solution.py:1788
  73.5 0.2 copy.70
  73.7 0.6 add_select_fusion.5.ids
  74.3 1.1 fusion.12.low_ref
  75.5 24.3 %look_up.2 = bf16[1152,768]{1,0:T(8,128)(2,1)} custom-call(s32[1152]{0:T(1024)} %add_select_fusion.5.ids, s32[1152,1]{1,0:T(8,128)} %fusion.12.low_ref, bf16[1600,16,768]{2,1,0:T(8,128)(2,1)} %bitcast.98), custom_call_target="tpu_custom_call" | custom-call | tf_op jit(solution)/shard_map/look_up/pallas_call | solution.py:1241
  99.8 1.1 collective-permute-start
  101.0 0.1 copy.86
  101.0 0.1 slice.170
  101.1 0.7 slice.130
  102.6 0.1 pad.46.clone
  102.7 0.6 pad.43.clone
  103.3 0.6 pad.40.clone
  103.8 0.6 broadcast_in_dim.67.refs_12_
  104.4 0.1 compare_reduce_fusion
  104.5 0.1 add_select_fusion.6
  104.6 0.3 reduce-window.9
  104.9 0.1 slice.103
  105.0 0.6 convert_element_type.60
  105.6 0.8 copy.77
  106.5 0.8 copy.78
  107.3 0.2 copy.76
  107.5 0.1 slice_reduce_fusion
  107.7 0.1 broadcast_maximum_fusion
  107.8 0.2 copy.75
  108.0 0.6 fusion.33
  108.6 1.1 broadcast_in_dim.72.low_ref
  109.7 0.1 slice_convert_fusion.1
  109.7 0.6 copy.84
  110.3 1.1 reshape.255
  111.4 0.4 reshape.253
  111.8 0.1 copy.79
  111.9 0.3 reshape.254
  112.2 0.9 add.115.code_ref
  113.1 24.2 %look_up.3.own_any = bf16[1152,768]{1,0:T(8,128)(2,1)} custom-call(s32[1152]{0:T(1024)} %get-tuple-element.122.ids, s32[1152,1]{1,0:T(8,128)} %broadcast_in_dim.72.low_ref, bf16[1600,16,768]{2,1,0:T(8,128)(2,1)} %bitcast.99), custom_call_target="tpu_custom_call" | custom-call | tf_op jit(solution)/shard_map/look_up/pallas_call | solution.py:1241
  137.4 1.1 gather_fusion
  138.5 0.1 convert_reduce_fusion
  138.7 0.6 fusion.41
  139.3 0.6 pad.35
  139.9 0.6 concatenate.58.fact_ref
  140.6 0.1 pad_bitcast_fusion
  140.8 0.8 fusion.26.chunk
  141.5 0.7 dynamic-slice_bitcast_fusion.bias_ref
  142.2 0.8 pad_maximum_fusion.1.down_ref.refs_4_
  143.0 0.7 slice_bitcast_fusion.12
  143.7 0.2 fusion.16
  143.9 1.2 pad_maximum_fusion.adapt_ref.refs_5_
  145.0 1.9 slice_select_fusion.target_ref
  146.9 1.0 broadcast_in_dim.64.seg_ref.refs_3_
  148.0 91.1 %first_layer.1 = (bf16[1024,2304]{1,0:T(8,128)(2,1)}, f32[1024,768]{1,0:T(8,128)}, f32[1024,768]{1,0:T(8,128)}, f32[1024,768]{1,0:T(8,128)}, bf16[1024,3072]{1,0...) custom-call(bf16[1152,768]{1,0:T(8,128)(2,1)} %look_up.3.own_any, ...), custom_call_target="tpu_custom_call" | custom-call | tf_op jit(solution)/shard_map/first_layer/pallas_call | solution.py:1180
  239.1 0.7 broadcast_in_dim.66.refs_1_.place_ref
  239.8 22.2 %last_forward.1 = (bf16[1024,1536]{1,0:T(8,128)(2,1)}, bf16[128,768]{1,0:T(8,128)(2,1)}, bf16[1024,128]{1,0:T(8,128)(2,1)}, f32[6,256]{1,0:T(8,128)}, f32[128,76...) custom-call(f32[1024,768]{1,0:T(8,128)} %get-tuple-element.58.refs_0, ...), custom_call_target="tpu_custom_call" | custom-call | tf_op jit(solution)/shard_map/last_forward/pallas_call | solution.py:452
  262.0 44.4 %head.1 = (f32[768,128]{1,0:T(8,128)}, f32[1,128]{1,0:T(1,128)}) custom-call(bf16[128,768]{1,0:T(8,128)(2,1)} %get-tuple-element.61.u_ref.feat_ref, f32[50,128]{1,0:T(8,128)} %dynamic-slice_bitcast_fusion.bias_ref, bf16[25600,768]{1,0:T(8,128)(2,1)} %table_any.3, bf16[768,6400]{1,0:T(8,128)(2,1)} %get-tuple-element.62.et_any), custom_call_target="tpu_custom_call" | custom-call | tf_op jit(solution)/shard_map/head/pallas_call | solution.py:1695
  306.5 26.8 %last_backward.1 = (f32[1024,768]{1,0:T(8,128)}, bf16[32,32,768]{2,1,0:T(8,128)(2,1)}, f32[768,128]{1,0:T(8,128)}, f32[8,128]{1,0:T(8,128)}) custom-call(f32[768,128]{1,0:T(8,128)} %get-tuple-element.63.mean_ref, f32[1,128]{1,0:T(1,128)} %get-tuple-element.64.all_log_ref, bf16[128,768]{1,0:T(8,128)(2,1)} %slice_select_fusion.target_ref, ...), custom_call_target="tpu_custom_call" | custom-call | tf_op jit(solution)/shard_map/last_backward/pallas_call | solution.py:643
  333.3 55.9 %finish.1 = (f32[8,128]{1,0:T(8,128)}, f32[24,768]{1,0:T(8,128)}, f32[24,128]{1,0:T(8,128)}) custom-call(f32[1024,768]{1,0:T(8,128)} %get-tuple-element.78.dout_any, f32[1024,768]{1,0:T(8,128)} %get-tuple-element.79.one_any, f32[1024,768]{1,0:T(8,128)} %get-tuple-element.80.two_any, bf16[1024,3072]{1,0:T(8,128)(2,1)} %get-tuple-element.81.slope_any, ...), custom_call_target="tpu_custom_call" | custom-call | tf_op jit(solution)/shard_map/finish/pallas_call | solution.py:1455
  389.3 1.8 update.1
  (78 shorter events, 0.5 us)
Async XLA Ops:
  7.2 6.3 %copy-start.11 = (f32[2,2,8,24]{3,2,1,0:T(8,128)S(1)}, f32[2,2,8,24]{3,2,1,0:T(8,128)}, u32[]{:S(2)}) copy-start(f32[2,2,8,24]{3,2,1,0:T(8,128)} %adapt_w.1) | copy-start | bytes 9220
  7.2 6.4 %copy-start.15 = (f32[1600]{0:T(1024)S(1)}, f32[1600]{0:T(1024)}, u32[]{:S(2)}) copy-start(f32[1600]{0:T(1024)} %param.42) | copy-start | bytes 19204
  7.2 7.0 %copy-start.6 = (bf16[2,96,768]{2,1,0:T(8,128)(2,1)S(1)}, bf16[2,96,768]{2,1,0:T(8,128)(2,1)}, u32[]{:S(2)}) copy-start(bf16[2,96,768]{2,1,0:T(8,128)(2,1)} %param.39) | copy-start | bytes 884740
  7.2 139.7 %all-gather.7.cloned.1.call-start = ((), (), s32[]{:S(2)}) async-start(), calls=%async_computation | async-start | bytes 9732096 | tf_op jit(solution)/shard_map/all_gather | solution.py:1776
  12.7 226.3 %all-gather.9.cloned.1.call-start = ((), (), s32[]{:S(2)}) async-start(), calls=%async_computation.1 | async-start | bytes 4866048 | tf_op jit(solution)/shard_map/all_gather | solution.py:1871
  15.0 53.6 %copy-start.17 = (s32[1,1024]{1,0:T(1,128)S(1)}, s32[1,1024]{1,0:T(1,128)}, u32[]{:S(2)}) copy-start(s32[1,1024]{1,0:T(1,128)} %param.25) | copy-start | bytes 12292
  15.0 53.6 %copy-start.21 = (s32[1,128]{1,0:T(1,128)S(1)}, s32[1,128]{1,0:T(1,128)}, u32[]{:S(2)}) copy-start(s32[1,128]{1,0:T(1,128)} %param.28) | copy-start | bytes 1540
  75.5 25.5 %copy-start.5 = (f32[32,24,128]{2,1,0:T(8,128)S(1)}, f32[32,24,128]{2,1,0:T(8,128)}, u32[]{:S(2)}) copy-start(f32[32,24,128]{2,1,0:T(8,128)} %get-tuple-element.57) | copy-start | bytes 1179652
  99.8 4.0 %copy-start.18 = (f32[768]{0:T(1024)S(1)}, f32[768]{0:T(1024)}, u32[]{:S(2)}) copy-start(f32[768]{0:T(1024)} %param.41) | copy-start | bytes 9220
  99.8 4.6 %copy-start.13 = (s32[1,1024]{1,0:T(1,128)S(1)}, s32[1,1024]{1,0:T(1,128)}, u32[]{:S(2)}) copy-start(s32[1,1024]{1,0:T(1,128)} %param.26) | copy-start | bytes 12292
  99.8 5.2 %copy-start.7 = (f32[24,768]{1,0:T(8,128)S(1)}, f32[24,768]{1,0:T(8,128)}, u32[]{:S(2)}) copy-start(f32[24,768]{1,0:T(8,128)} %head_w.1) | copy-start | bytes 221188
  99.8 5.8 %copy-start.12 = (bf16[2,2,768,8]{2,3,1,0:T(8,128)(2,1)S(1)}, bf16[2,2,768,8]{2,3,1,0:T(8,128)(2,1)}, u32[]{:S(2)}) copy-start(bf16[2,2,768,8]{2,3,1,0:T(8,128)(2,1)} %param.43) | copy-start | bytes 147460
  99.8 45.2 %collective-permute-start = (bf16[1152,768]{1,0:T(8,128)(2,1)}, bf16[1152,768]{1,0:T(8,128)(2,1)S(1)}, u32[]{:S(2)}, u32[]{:S(2)}) collective-permute-start(bf16[1152,768]{1,0:T(8,128)(2,1)} %look_up.2), channel_id=1, source_target_pairs={{0,16},{16,0},{1,17},{17,1},{2,18},{18,2},{3,19},{19,3},{4,20},{20... | collective-permute-start | bytes 5308424 | tf_op jit(solution)/shard_map/ppermute | solution.py:1799
  104.4 42.5 %copy-start.10 = (f32[1,1024]{1,0:T(1,128)}, f32[1,1024]{1,0:T(1,128)S(1)}, u32[]{:S(2)}) copy-start(f32[1,1024]{1,0:T(1,128)S(1)} %convert_element_type.63.seg_row_ref) | copy-start | bytes 12292
  107.3 0.7 copy-start.14
  113.1 24.2 %copy-start.22 = (s32[1,128]{1,0:T(1,128)S(1)}, s32[1,128]{1,0:T(1,128)}, u32[]{:S(2)}) copy-start(s32[1,128]{1,0:T(1,128)} %param.28) | copy-start | bytes 1540
  113.1 25.4 %copy-start.23 = (s32[32,1]{0,1:T(1,128)S(1)}, s32[32,1]{0,1:T(1,128)}, u32[]{:S(2)}) copy-start(s32[32,1]{0,1:T(1,128)} %copy.84) | copy-start | bytes 388
  113.1 25.6 %copy-start.24 = (f32[4]{0:T(128)S(1)}, f32[4]{0:T(128)}, u32[]{:S(2)}) copy-start(f32[4]{0:T(128)} %param.30) | copy-start | bytes 52
  113.1 27.5 %copy-start.1 = (bf16[768,16]{1,0:T(8,128)(2,1)S(1)}, bf16[768,16]{1,0:T(8,128)(2,1)}, u32[]{:S(2)}) copy-start(bf16[768,16]{1,0:T(8,128)(2,1)} %copy.77) | copy-start | bytes 73732
  113.1 27.5 %copy-start.2 = (bf16[768,16]{1,0:T(8,128)(2,1)S(1)}, bf16[768,16]{1,0:T(8,128)(2,1)}, u32[]{:S(2)}) copy-start(bf16[768,16]{1,0:T(8,128)(2,1)} %copy.78) | copy-start | bytes 73732
  137.3 3.4 copy-start.3
  137.3 3.4 copy-start.4
  137.3 3.4 copy-start.8
  137.3 3.4 copy-start.9
  140.5 3.2 copy-start.19
  140.5 3.2 copy-start.20
  145.0 2.9 copy-start
  148.0 91.1 %copy-start.16 = (s32[1,128]{1,0:T(1,128)S(1)}, s32[1,128]{1,0:T(1,128)}, u32[]{:S(2)}) copy-start(s32[1,128]{1,0:T(1,128)} %place_row_ref.1) | copy-start | bytes 1540
Sparse Core Ops, SparseCore 0:
  12.9 91.3 all-gather.6
  107.1 75.2 all-gather.8
where the time goes:
time: 404 us; the launch traced here: 398 us
  Pallas kernels  344 us (85%)
  local copies, waits for them, and re-layouts  20.8 us (5%)
  between operations  16.1 us (4%)
  other arithmetic  10.8 us (3%)
  blocking collectives  4.81 us (1%)
    pallas_call x1, Pallas kernels, first_layer(): pl.pallas_call(functools.partial(first_layer_body, streams, shards), in_s...  91.1 us
    pallas_call x1, Pallas kernels, finish(): pl.pallas_call(functools.partial(finish_body, shards, edge), in_specs=[an...  55.9 us
    pallas_call x1, Pallas kernels, start_exchange(): pl.pallas_call(functools.partial(start_body, streams, shards), in_specs=[...  53.5 us
    pallas_call x2, Pallas kernels, look_up(): pl.pallas_call(look_up_body, in_specs=[pl.BlockSpec(memory_space=pltpu.SM...  48.5 us
    pallas_call x1, Pallas kernels, head(): pl.pallas_call(head_body, in_specs=[whole] * 2 + [anywhere] * 2, out_spec...  44.4 us
    pallas_call x1, Pallas kernels, last_backward(): pl.pallas_call(functools.partial(last_backward_body, places=(up[1], dn[1]...  26.8 us
    pallas_call x1, Pallas kernels, last_forward(): pl.pallas_call(body, in_specs=[whole] * 7 + [anywhere] * (len(weights) +...  22.2 us
  transfers between devices with their start and end apart: 3, of which 0 were waited for; matrix products, arithmetic and copies ran while one was open for 6% of the time, Pallas kernels for 49%

commit v1 on v0

--- a/solution.py
+++ b/solution.py
@@ -143,8 +143,8 @@
         ).astype(BF)
 
 
-def project(own, got, code, spots, gains, shifts, down, w, up, bias):
-    rows, width = code.shape[0], own.shape[1]
+def project(own, got, code, spots, gains, shifts, down, w, up, bias, rows):
+    width = own.shape[1]
     tile = split_of(rows, 256, 16)
     total = w.shape[0]
     row = lambda n: pl.BlockSpec((tile, n), lambda i: (i, 0))
@@ -383,10 +383,16 @@
         keepdims=True,
     )
     same = seg == seg_own
+
+    def scored(p):
+        part = slice(p * lanes, (p + 1) * lanes)
+        return mm_nt(kv_ref[:, part], pair_rows(q_ref[:, part].astype(F32) * width**-0.5, width))
+
+    later = scored(0)
     for p in range(hidden // lanes):
         part = slice(p * lanes, (p + 1) * lanes)
-        queries = pair_rows(q_ref[:, part].astype(F32) * width**-0.5, width)
-        scores = masked(mm_nt(kv_ref[:, part], queries), same)
+        scores = masked(later, same)
+        later = scored(p + 1) if (p + 1) * lanes < hidden else None
         top = jnp.max(scores, 0, keepdims=True)
         weights = jnp.exp(scores - top)
         total = jnp.sum(weights, 0, keepdims=True)
@@ -405,9 +411,12 @@
     units, step = feed_step(up_ref)
     for copy in copies:
         copy.wait()
+    gate = mm_nt(middle_low, rows_of(up_ref, 0, step))
     for start in range(0, units, step):
         part = slice(start, start + step)
-        act, slope = gelu_pair(mm_nt(middle_low, rows_of(up_ref, start, step)) + b1[:, part])
+        later = mm_nt(middle_low, rows_of(up_ref, start + step, step)) if start + step < units else None
+        act, slope = gelu_pair(gate + b1[:, part])
+        gate = later
         slope_ref[:, part] = slope.astype(BF)
         sum_two = sum_two + mm(act.astype(BF), rows_of(dn_ref, start, step))
     two_ref[...] = sum_two
@@ -534,12 +543,20 @@
 
 
 def last_backward_body(
-    mean_ref, all_log_ref, target_ref, fact_ref, kv_ref, q_ref, mid_ref, log_ref, one_ref, slope_ref, two_ref,
+    own_any, got_any, mean_ref, all_log_ref, code_ref, fact_ref, kv_ref, q_ref, mid_ref, log_ref, one_ref, slope_ref, two_ref,
     low_ref, act_ref, hslope_ref, feat_ref, place_ref, place_row_ref, seg_ref, down_ref, w_ref, adapt_ref, wo_ref,
     up_any, dn_any, gain_ref, hb_ref,
     dx_ref, gh_ref, g_ref, out_fact_ref,
-    up_ref, dn_ref, dkv_ref, dq_ref, sems, *, places, edge,
+    up_ref, dn_ref, dkv_ref, dq_ref, aims, sems, *, places, edge,
 ):
+    labels = place_ref.shape[0]
+    tail = pl.ds(kv_ref.shape[0], labels)
+    aimed = [
+        pltpu.make_async_copy(source.at[tail, :], aims.at[k], sems.at[2 + k])
+        for k, source in enumerate((own_any, got_any))
+    ]
+    for copy in aimed:
+        copy.start()
     copies = []
     for k, (source, target, place) in enumerate(
         ((up_any, up_ref, places[0]), (dn_any, dn_ref, places[1]))
@@ -556,7 +573,10 @@
     lanes = 2 * (hidden // HEADS)
     width = lanes // 2
     scale = width**-0.5
-    targets = target_ref[...].astype(F32)
+    for copy in aimed:
+        copy.wait()
+    mine = code_ref[kv_ref.shape[0] :, :] % 2
+    targets = jnp.where(mine > 0, aims[0].astype(F32), aims[1].astype(F32))
     weight = fact_ref[0:1, 0:1]
     chosen = jnp.sum(feat_ref[...].astype(F32) * targets, keepdims=True)
     loss = weight * (jnp.sum(all_log_ref[...] - fact_ref[3:4, :labels], keepdims=True) - chosen)
@@ -580,25 +600,34 @@
     units, step = feed_step(up_ref)
     for copy in copies:
         copy.wait()
+    dact = mm_nt(dtwo_low, rows_of(dn_ref, 0, step))
     for start in range(0, units, step):
         part = slice(start, start + step)
-        dgate = (
-            slope_ref[:, part].astype(F32) * mm_nt(dtwo_low, rows_of(dn_ref, start, step))
-        ).astype(BF)
+        later = mm_nt(dtwo_low, rows_of(dn_ref, start + step, step)) if start + step < units else None
+        dgate = (slope_ref[:, part].astype(F32) * dact).astype(BF)
         dmiddle = dmiddle + mm(dgate, rows_of(up_ref, start, step))
+        dact = later
     done = norm_back(one_ref[...], gain_ref[3:4, :], dmiddle)
     dctx = mm(done.astype(BF), wo_ref[...]).astype(BF)
     seg = seg_ref[...]
     choose_t = lax.broadcasted_iota(jnp.int32, (rows, labels), 0) == place_row_ref[...]
     same = seg == jnp.sum(jnp.where(choose_t, seg, 0.0), 0, keepdims=True)
-    for p in range(hidden // lanes):
+
+    def products(p):
         part = slice(p * lanes, (p + 1) * lanes)
         later = slice(hidden + p * lanes, hidden + (p + 1) * lanes)
         queries = pair_rows(q_ref[:, part].astype(F32) * scale, width)
         outs = pair_rows(dctx[:, part].astype(F32), width)
+        return queries, outs, mm_nt(kv_ref[:, part], queries), mm_nt(kv_ref[:, later], outs)
+
+    ahead = products(0)
+    for p in range(hidden // lanes):
+        part = slice(p * lanes, (p + 1) * lanes)
+        later = slice(hidden + p * lanes, hidden + (p + 1) * lanes)
+        queries, outs, scores, dweights = ahead
+        ahead = products(p + 1) if (p + 1) * lanes < hidden else None
         keys = kv_ref[:, part]
-        weights = jnp.exp(masked(mm_nt(keys, queries), same) - log_ref[p : p + 1, :])
-        dweights = mm_nt(kv_ref[:, later], outs)
+        weights = jnp.exp(masked(scores, same) - log_ref[p : p + 1, :])
         inner = jnp.sum(dweights * weights, 0, keepdims=True)
         dscores = (weights * (dweights - inner)).astype(BF)
         dkv_ref[:, part] = mm(dscores, queries).astype(BF)
@@ -632,17 +661,17 @@
 
 
 def last_backward(
-    mean, logs, targets, facts, saved, place_col, place_row, seg_wide, down, w, adapt, wo, up, dn, gains, hb, edge, shards
+    mean, logs, own, got, code, facts, saved, place_col, place_row, seg_wide, down, w, adapt, wo, up, dn, gains, hb, edge, shards
 ):
     kv = saved[0]
     rows = kv.shape[0]
-    labels, hidden = targets.shape
+    labels, hidden = saved[-1].shape
     whole = pl.BlockSpec(memory_space=pltpu.VMEM)
     anywhere = pl.BlockSpec(memory_space=pl.ANY)
     shape = jax.ShapeDtypeStruct
     return pl.pallas_call(
         functools.partial(last_backward_body, places=(up[1], dn[1]), edge=edge),
-        in_specs=[whole] * 22 + [anywhere] * 2 + [whole] * 2,
+        in_specs=[anywhere] * 2 + [whole] * 22 + [anywhere] * 2 + [whole] * 2,
         out_specs=[whole] * 4,
         out_shape=[
             shape((rows, hidden), F32),
@@ -657,11 +686,12 @@
             slab_scratch(dn),
             pltpu.VMEM(kv.shape, BF),
             pltpu.VMEM((labels, hidden), BF),
-            pltpu.SemaphoreType.DMA((2,)),
+            pltpu.VMEM((2, labels, hidden), BF),
+            pltpu.SemaphoreType.DMA((4,)),
         ],
         compiler_params=params(),
         name="last_backward",
-    )(mean, logs, targets, facts, *saved, place_col, place_row, seg_wide, down, w, adapt, wo, up[0], dn[0], gains, hb)
+    )(own, got, mean, logs, code, facts, *saved, place_col, place_row, seg_wide, down, w, adapt, wo, up[0], dn[0], gains, hb)
 
 
 def after_back_body(dout_ref, one_ref, two_ref, slope_ref, wo_ref, up_ref, down_ref, gain_ref, dctx_ref):
@@ -1019,6 +1049,7 @@
             *gather_sems(streams),
         ],
         compiler_params=params(collective_id=1, has_side_effects=True),
+        cost_estimate=pl.CostEstimate(flops=0, bytes_accessed=200_000_000, transcendentals=0),
         name="start_exchange",
     )(fact, chunk, table)
 
@@ -1039,6 +1070,8 @@
     lanes = 2 * (hidden // HEADS)
     pairs = hidden // lanes
 
+    cut = dn.shape[1] - feed_any.shape[1]
+
     def slab(source, target, start):
         return source.at[:, pl.ds(start, target.shape[1]), :]
 
@@ -1048,9 +1081,10 @@
             (
                 (own_any.at[pl.ds(0, rows), :], own),
                 (got_any.at[pl.ds(0, rows), :], got),
-                (slab(in_any, in_slab, up.shape[1]), in_slab),
+                (slab(in_any, in_slab, in_any.shape[1] - in_slab.shape[1]), in_slab),
                 (slab(in_any, up, 0), up),
-                (slab(feed_any, dn, 0), dn),
+                (in_any.at[:, pl.ds(up.shape[1], cut), :], dn.at[:, pl.ds(0, cut), :]),
+                (feed_any, dn.at[:, pl.ds(cut, dn.shape[1] - cut), :]),
                 (chunk, full_chunk.at[me]),
             )
         )
@@ -1073,12 +1107,17 @@
         )
         for k, (start, size, order) in enumerate(streams)
     ]
-    def advance(first, last):
-        for index in range(first, last + 1):
-            for gather in gathers:
-                gather.step(index)
-
-    advance(0, 0)
+    def advance(*ranges):
+        pairs_of = [(0, ranges[0]), (1, ranges[0])] + [(2, r) for r in ranges[1:]]
+        for k, (first, last) in pairs_of:
+            for index in range(first, last + 1):
+                gathers[k].step(index)
+
+    def at(i, plan):
+        for k, ranges in plan.items():
+            pl.when(i == k)(functools.partial(advance, *ranges))
+
+    advance((0, 0), (0, 0))
     for copy in loads[:3]:
         copy.wait()
     unpack_rows(in_slab, (w, wo))
@@ -1091,13 +1130,7 @@
             adapt_ref, bias_ref, qkv.at[part, :], mid_ref.at[part, :], x.at[part, :],
         )
 
-        @pl.when(i == tiles - 3)
-        def _():
-            advance(1, 3)
-
-        @pl.when(i == tiles - 1)
-        def _():
-            advance(4, 5)
+        at(i, {tiles - 3: ((1, 3), (1, 3)), tiles - 1: ((4, 5),)})
 
     early = [
         pltpu.make_async_copy(qkv, qkv_out, out_sems.at[0]),
@@ -1114,10 +1147,12 @@
             ctx.at[:, column(0)], log_ref.at[pl.ds(p, 1)],
         )
 
-        for k, (first, last) in {1: (6, 7), 3: (8, 9), 5: (10, 13)}.items():
-            pl.when(p == pairs - 6 + k)(functools.partial(advance, first, last))
-
-    for copy in loads[3:5]:
+        at(
+            p - (pairs - 6),
+            {0: ((1, 0), (4, 11)), 1: ((6, 7),), 3: ((8, 9), (12, 19)), 4: ((10, 11),)},
+        )
+
+    for copy in loads[3:6]:
         copy.wait()
 
     def tile_copies(i):
@@ -1135,7 +1170,7 @@
             )
         ]
 
-    plan = {tiles - 4: (14, 16), tiles - 3: (17, 19), tiles - 2: (20, 23), tiles - 1: (24, 27)}
+    plan = {0: ((12, 13), (20, 27)), 1: ((14, 17),), 2: ((18, 21),), 3: ((22, 27),)}
 
     @pl.loop(0, tiles)
     def _(i):
@@ -1153,23 +1188,22 @@
         )
         for copy in tile_copies(i):
             copy.start()
-        for k, (first, last) in plan.items():
-            pl.when(i == k)(functools.partial(advance, first, last))
+        at(i - (tiles - 4), plan)
 
     for gather in gathers:
         gather.finish()
     for i in (tiles - 2, tiles - 1):
         for copy in tile_copies(i):
             copy.wait()
-    for copy in early + loads[5:]:
+    for copy in early + loads[6:]:
         copy.wait()
 
 
 def first_layer(own, got, first_in, feed, chunk, more, shards):
     whole = pl.BlockSpec(memory_space=pltpu.VMEM)
     anywhere = pl.BlockSpec(memory_space=pl.ANY)
-    code, down = more[0], more[4]
-    rows, hidden = code.shape[0], own.shape[1]
+    down, seg_row = more[4], more[-1]
+    rows, hidden = seg_row.shape[1], own.shape[1]
     tile = split_of(rows, 256, 16)
     pairs = HEADS // 2
     units = 4 * hidden
@@ -1206,7 +1240,7 @@
             pltpu.VMEM((2, tile, hidden), F32),
             pltpu.VMEM((2, tile, hidden), F32),
             pltpu.VMEM((2, tile, units), BF),
-            sems((6,)),
+            sems((7,)),
             sems((4, rows // tile)),
             sems((2,)),
             *gather_sems(streams),
@@ -1220,18 +1254,26 @@
 GROUP = 16
 
 
-def look_up_body(ids, low_ref, table, out_ref, stage):
-    @pl.loop(0, out_ref.shape[0] // PICK)
-    def _(b):
-        part = pl.ds(pl.multiple_of(b * PICK, PICK), PICK)
-
-        def one(t, carry):
-            stage[t] = table[ids[b * PICK + t]]
-            return carry
-
-        lax.fori_loop(0, PICK, one, 0, unroll=8)
-        choose = lax.broadcasted_iota(jnp.int32, (PICK, PICK * GROUP), 1) == low_ref[part, :]
-        out_ref[part, :] = mm(choose.astype(F32).astype(BF), flat(stage)).astype(BF)
+def look_up_body(ids, low_ref, table, first_ref, second_ref, stage):
+    half = first_ref.shape[0]
+    for k, out_ref in enumerate((first_ref, second_ref)):
+
+        @pl.loop(0, half // PICK)
+        def _(b, k=k, out_ref=out_ref):
+            at = k * half + b * PICK
+
+            def one(t, carry):
+                stage[t] = table[ids[at + t]]
+                return carry
+
+            lax.fori_loop(0, PICK, one, 0, unroll=16)
+            choose = (
+                lax.broadcasted_iota(jnp.int32, (PICK, PICK * GROUP), 1)
+                == low_ref[pl.ds(pl.multiple_of(at, PICK), PICK), :]
+            )
+            out_ref[pl.ds(pl.multiple_of(b * PICK, PICK), PICK), :] = mm(
+                choose.astype(F32).astype(BF), flat(stage)
+            ).astype(BF)
 
 
 def look_up(ids, table):
@@ -1241,8 +1283,8 @@
     return pl.pallas_call(
         look_up_body,
         in_specs=[pl.BlockSpec(memory_space=pltpu.SMEM), whole, whole],
-        out_specs=whole,
-        out_shape=jax.ShapeDtypeStruct((ids.size, hidden), table.dtype),
+        out_specs=[whole] * 2,
+        out_shape=[jax.ShapeDtypeStruct((ids.size // 2, hidden), table.dtype)] * 2,
         scratch_shapes=[pltpu.VMEM((PICK, GROUP, hidden), table.dtype)],
         compiler_params=params(),
         name="look_up",
@@ -1263,7 +1305,7 @@
 
 def finish_body(
     shards, edge,
-    dout_any, one_any, two_any, slope_any, wo_any, up_any, dn_any, qkv_any, gain_ref, log_ref, seg_ref,
+    dout_any, one_any, two_any, slope_any, wo_any, in_any, feed_any, qkv_any, gain_ref, log_ref, seg_ref,
     seg_row_ref, mid_ref, parts, late_ref, facts,
     sums_ref, dense_ref, total_ref,
     dout, one, two, slope, wo, up, dn, qkv, dctx, dv, grad, core_got, chip_sum, dense_got, grad_got, note, notes,
@@ -1284,6 +1326,7 @@
         ]
 
     here = position()
+    cut = dn.shape[1] - feed_any.shape[1]
     chips = shards // 2
     chip, core = me // 2, here["c"]
     to_core = pltpu.make_async_remote_copy(
@@ -1310,21 +1353,22 @@
         pltpu.make_async_copy(source, target, load_sems.at[k])
         for k, (source, target) in enumerate(
             (
-                (dn_any.at[:, pl.ds(0, dn.shape[1]), :], dn),
-                (up_any.at[:, pl.ds(0, up.shape[1]), :], up),
+                (in_any.at[:, pl.ds(up.shape[1], cut), :], dn.at[:, pl.ds(0, cut), :]),
+                (feed_any, dn.at[:, pl.ds(cut, dn.shape[1] - cut), :]),
+                (in_any.at[:, pl.ds(0, up.shape[1]), :], up),
                 (wo_any, wo),
                 (qkv_any, qkv),
             )
         )
     ]
-    for copy in tile_loads(0) + loads[:3]:
+    for copy in tile_loads(0) + loads[:4]:
         copy.start()
     for i in range(1, tiles):
         for copy in tile_loads(i):
             copy.start()
-    loads[3].start()
+    loads[4].start()
     greet_all(shards)
-    for copy in loads[:3]:
+    for copy in loads[:4]:
         copy.wait()
 
     @pl.loop(0, tiles)
@@ -1356,7 +1400,7 @@
             def _(k):
                 to_chip(k).start()
 
-    loads[3].wait()
+    loads[4].wait()
     lanes = 2 * (hidden // HEADS)
     pairs = hidden // lanes
 
@@ -1443,7 +1487,8 @@
 
 
 def finish(back, qkv, logs, seg_wide, seg_row, mid, parts, late, facts, edge, shards):
-    dout, one, two, slope, wo, up, dn, gains = back
+    dout, one, two, slope, wo, first_in, feed, gains = back
+    slab = pltpu.VMEM((shards, slope.shape[1] // shards, dout.shape[1]), BF)
     parts = parts.reshape(-1, 2, *parts.shape[1:])
     rows, hidden = dout.shape
     each = hidden // shards
@@ -1467,8 +1512,8 @@
             pltpu.VMEM((rows, hidden), F32),
             pltpu.VMEM(slope.shape, BF),
             pltpu.VMEM(wo.shape, BF),
-            slab_scratch(up),
-            slab_scratch(dn),
+            slab,
+            slab,
             pltpu.VMEM(qkv.shape, BF),
             pltpu.VMEM((rows, hidden), BF),
             pltpu.VMEM((rows, 2 * (hidden // HEADS)), F32),
@@ -1480,7 +1525,7 @@
             pltpu.VMEM((8, 128), F32),
             pltpu.VMEM((shards, 8, 128), F32),
             sems((4, tiles)),
-            sems((4,)),
+            sems((5,)),
             sems((2,)),
             sems((2,)),
             sems((2,)),
@@ -1488,7 +1533,7 @@
         ],
         compiler_params=params(collective_id=2, has_side_effects=True),
         name="finish",
-    )(dout, one, two, slope, wo, up[0], dn[0], qkv, gains, logs, seg_wide, seg_row, mid, parts, late, facts)
+    )(dout, one, two, slope, wo, first_in, feed, qkv, gains, logs, seg_wide, seg_row, mid, parts, late, facts)
 
 
 LOG_ROWS = 16
@@ -1773,10 +1818,11 @@
     grouped = (lax.axis_size("dp"), lax.axis_size("fsdp")) == (2, 16)
     feeds = [[feedforward_up[layer].T, feedforward_down[layer]] for layer in range(layers)]
     attends = [[attention_in_weight[layer].T, attention_out_weight[layer].T] for layer in range(layers)]
+    cut = ff_rows // 32 * 16
     first_in = lax.all_gather(
-        jnp.concatenate([feeds[0][0], *attends[0]], 0), BOTH, axis=0, tiled=False
+        jnp.concatenate([feeds[0][0], feeds[0][1][:cut], *attends[0]], 0), BOTH, axis=0, tiled=False
     )
-    feed_chunk = feeds[0][1]
+    feed_chunk = feeds[0][1][cut:]
     last_chunk = pad_rows(
         jnp.concatenate([feeds[1][0], *attends[1], head_projection.astype(BF)], 0), 32
     )
@@ -1794,11 +1840,15 @@
     slice_rows = vocabulary_bias.shape[0]
     ups = adapter_up_matrix.reshape(-1)
     if grouped:
-        ids_of = lambda part: lax.dynamic_index_in_dim(group_ids, part, 0, keepdims=False)
-        other_rows = look_up(ids_of(1 - dp_index), embed)
+        pair_ids = jnp.concatenate(
+            [
+                lax.dynamic_index_in_dim(group_ids, (dp_index + shift) % 2, 0, keepdims=False)
+                for shift in (1, 0)
+            ]
+        )
+        other_rows, own_rows = look_up(pair_ids, embed)
         got = lax.ppermute(other_rows, "dp", [(0, 1), (1, 0)])
-        own_ids, other_rows = lax.optimization_barrier((ids_of(dp_index), other_rows))
-        own_rows = look_up(own_ids, embed)
+        feed_chunk, own_rows = lax.optimization_barrier((feed_chunk, own_rows))
         fact = jnp.concatenate([vocabulary_bias, ups, sequence_task_index.astype(F32)])
         fact_rows = -(-fact.size // 1024) * 8
         facts, feed_full, own_turned = start_exchange(
@@ -1807,7 +1857,7 @@
             embed,
             shards,
         )
-        last_feed, facts = lax.optimization_barrier((last_feed, facts))
+        facts, got, last_feed = lax.optimization_barrier((facts, got, last_feed))
         facts = facts.reshape(shards, -1)
         all_bias = facts[:, :slice_rows].reshape(-1)
         every_up = facts[:, slice_rows : slice_rows + ups.size]
@@ -1854,9 +1904,8 @@
             for layer in range(layers)
         ]
     )
-    target_rows = jnp.where(mine[tokens:, None], own_rows[tokens:], got[tokens:])
     segments = sentence_numbers[0]
-    code = (2 * seg_positions(segments) + mine[:tokens].astype(jnp.int32))[:, None]
+    code = (jnp.pad(2 * seg_positions(segments), (0, labels)) + mine.astype(jnp.int32))[:, None]
     seg_real = segments.astype(F32)
     seg_wide = jnp.broadcast_to(seg_real[:, None], (tokens, 128))
     seg_row = seg_real[None, :]
@@ -1877,7 +1926,7 @@
         qkv, x_last, one, two, slope, out_first, last_full, mid, logs = first_layer(
             own_rows, got, first_in, feed_full, last_chunk, more, shards
         )
-        slabs = [slabs_of(first_in, feed_full), slabs_of(last_full, last_dn)]
+        slabs = [None, slabs_of(last_full, last_dn)]
         *saved, in_last, out_last, head_full = last_forward(
             x_last, *last_inputs, (last_full,), (in_start, in_start + qkv_rows + out_rows), *slabs[1], gains,
             shifts, head_dense_bias[None, :],
@@ -1890,15 +1939,16 @@
     else:
         feed_full = lax.all_gather(feed_chunk, BOTH, axis=0, tiled=False)
         last_full = lax.all_gather(last_chunk, BOTH, axis=0, tiled=False)
-        slabs = [slabs_of(first_in, feed_full), slabs_of(last_full, last_dn)]
+        dn_full = jnp.concatenate([first_in[:, ff_rows : ff_rows + cut], feed_full], 1)
+        slabs = [slabs_of(first_in, dn_full), slabs_of(last_full, last_dn)]
         taken = lambda full_chunk, start, size: full_chunk[:, start : start + size].reshape(-1, hidden)
-        in_first = taken(first_in, ff_rows, qkv_rows)
-        out_first = taken(first_in, ff_rows + qkv_rows, out_rows)
+        in_first = taken(first_in, ff_rows + cut, qkv_rows)
+        out_first = taken(first_in, ff_rows + cut + qkv_rows, out_rows)
         in_last = taken(last_full, in_start, qkv_rows)
         out_last = taken(last_full, in_start + qkv_rows, out_rows)
         head_full = taken(last_full, in_start + qkv_rows + out_rows, head_rows)
         qkv, mid, hidden_rows = project(
-            own_rows, got, code, position_embedding, gains, shifts, downs, in_first, adapters, layer_bias_vector
+            own_rows, got, code, position_embedding, gains, shifts, downs, in_first, adapters, layer_bias_vector, tokens
         )
         context, logs = attend(qkv, seg_wide, seg_row)
         x_last, one, two, slope = after(
@@ -1951,19 +2001,19 @@
         [lanes(value) for value in (row_weight, *fades, target_bias)] + [jnp.zeros((4, 128), F32)]
     )
     hidden_grad, dense_gradient, late, facts = last_backward(
-        mean_t, own_logs, target_rows, facts, saved, place_col, place_row, seg_wide, downs, in_last, adapters,
+        mean_t, own_logs, own_rows, got, code, facts, saved, place_col, place_row, seg_wide, downs, in_last, adapters,
         out_last, *slabs[1], gains, head_full, 3 * rank, shards if grouped else None,
     )
-    back = (hidden_grad, one, two, slope, out_first, *slabs[0], gains)
+    back = (hidden_grad, one, two, slope, out_first)
     adapts = (adapter_up_matrix, adapter_moment_first, adapter_moment_second)
     heads = (head_projection, head_moment_first, head_moment_second)
     if grouped:
         sums, dense_portion, adapter_portion = finish(
-            back, qkv, logs, seg_wide, seg_row, mid, dense_gradient, late, facts, rank, shards
+            (*back, first_in, feed_full, gains), qkv, logs, seg_wide, seg_row, mid, dense_gradient, late, facts, rank, shards
         )
         loss, norm, *new = update(sums, dense_portion, adapter_portion, facts, heads, adapts)
         return (loss[0, 0], norm[0, 0], *new[3:], *new[:3])
-    dctx = after_back(*back)
+    dctx = after_back(*back, *slabs[0], gains)
     first = attend_back(qkv, dctx, logs, seg_wide, seg_row, mid, rank)
     adapter_gradient = (first + late)[:, : 2 * rank * layers].T.reshape(layers, 2, rank, hidden)
     dense_portion = lax.psum_scatter(dense_gradient, BOTH, scatter_dimension=0, tiled=True)

time: 404 us -> 418 us (1.035)
  Pallas kernels: 344 us -> 367 us
  local copies, waits for them, and re-layouts: 20.8 us -> 15.3 us
    pallas_call x1, Pallas kernels: 53.5 us -> 89.8 us  [start_exchange(): pl.pallas_call(functools.partial(start_body, streams, shards), in_specs=[...]
    pallas_call x2 -> x1, Pallas kernels: 48.5 us -> 34.2 us  [look_up(): pl.pallas_call(look_up_body, in_specs=[pl.BlockSpec(memory_space=pltpu.SM...]
  transfers between devices with their start and end apart: 3 -> 3, of which waited for: 0 -> 0; matrix products, arithmetic and copies ran while one was open for 6% -> 4% of each run, Pallas kernels for 49% -> 52%
where the time goes in v1:
time: 418 us; the launch traced here: 413 us
  Pallas kernels  367 us (88%)
  between operations  16.3 us (4%)
  local copies, waits for them, and re-layouts  15.3 us (4%)
  other arithmetic  7.41 us (2%)
  blocking collectives  5.23 us (1%)
    pallas_call x1, Pallas kernels, first_layer(): pl.pallas_call(functools.partial(first_layer_body, streams, shards), in_s...  90 us
    pallas_call x1, Pallas kernels, start_exchange(): pl.pallas_call(functools.partial(start_body, streams, shards), in_specs=[...  89.8 us
    pallas_call x1, Pallas kernels, finish(): pl.pallas_call(functools.partial(finish_body, shards, edge), in_specs=[an...  59.9 us
    pallas_call x1, Pallas kernels, head(): pl.pallas_call(head_body, in_specs=[whole] * 2 + [anywhere] * 2, out_spec...  44.7 us
    pallas_call x1, Pallas kernels, look_up(): pl.pallas_call(look_up_body, in_specs=[pl.BlockSpec(memory_space=pltpu.SM...  34.2 us
    pallas_call x1, Pallas kernels, last_backward(): pl.pallas_call(functools.partial(last_backward_body, places=(up[1], dn[1]...  25.6 us
    pallas_call x1, Pallas kernels, last_forward(): pl.pallas_call(body, in_specs=[whole] * 7 + [anywhere] * (len(weights) +...  20.7 us
  transfers between devices with their start and end apart: 3, of which 0 were waited for; matrix products, arithmetic and copies ran while one was open for 4% of the time, Pallas kernels for 52%

profile of v1, /device:TPU:0, one launch (start us, length us, event | category | flops | bytes accessed | tf_op | source)
XLA Modules:
  0.0 413.3 jit_solution(8014878753320802786)
XLA Ops:
  7.2 0.0 all-gather.7.cloned.1.call-start
  7.2 0.8 slice_bitcast_fusion.7
  8.0 1.6 slice_bitcast_fusion.5
  9.6 1.0 slice_bitcast_fusion.3
  10.6 1.0 slice_bitcast_fusion
  11.6 0.8 pad_maximum_fusion.2
  12.4 0.0 all-gather.7.cloned.1.call-update
  12.4 0.0 all-gather.9.cloned.1.call-start
  12.5 5.2 %all-gather.3 = s32[2,1,1152]{2,1,0:T(1,128)S(1)} all-gather(s32[1,1,1152]{2,1,0:T(1,128)S(1)} %reshape.294), channel_id=2, replica_groups=mesh['dp'=2,'fsdp'=16] {'dp'}, dimensions={0}, use_global_device_ids=true | all-gather | bytes 13824 | tf_op jit(solution)/shard_map/all_gather | solution.py:1834
  17.8 0.1 dynamic-slice_reduce_fusion.1
  17.9 0.5 copy.63
  18.4 0.4 copy.60
  18.8 0.6 add_select_fusion.2.ids
  19.4 1.6 fusion.1.low_ref
  21.0 34.2 %look_up.1 = (bf16[1152,768]{1,0:T(8,128)(2,1)}, bf16[1152,768]{1,0:T(8,128)(2,1)}) custom-call(s32[2304]{0:T(1024)} %add_select_fusion.2.ids, s32[2304,1]{1,0:T(8,128)} %fusion.1.low_ref, bf16[1600,16,768]{2,1,0:T(8,128)(2,1)} %bitcast.99), custom_call_target="tpu_custom_call" | custom-call | tf_op jit(solution)/shard_map/look_up/pallas_call | solution.py:1283
  55.2 2.1 collective-permute-start
  58.0 0.1 reshape.263
  58.1 0.1 concatenate.77
  58.2 0.6 pad_bitcast_fusion.2.fact
  58.8 0.0 copy-start.6
  58.8 89.8 %start_exchange.1 = (f32[32,24,128]{2,1,0:T(8,128)}, bf16[32,48,768]{2,1,0:T(8,128)(2,1)}, bf16[768,6400]{1,0:T(8,128)(2,1)}) custom-call(f32[24,128]{1,0:T(8,128)} %pad_bitcast_fusion.2.fact, bf16[48,768]{1,0:T(8,128)(2,1)} %get-tuple-element.60.chunk, bf16[25600,768]{1,0:T(8,128)(2,1)} %table_any.3), custom_call_target="tpu_custom_call" | custom-call | bytes 200000000 | tf_op jit(solution)/shard_map/start_exchange/pallas_call | solution.py:1035
  148.7 0.7 slice_bitcast_fusion.2
  149.4 0.0 all-gather.9.cloned.1.call-update
  150.2 0.1 pad.51.clone
  150.2 0.1 pad.48.clone
  150.3 0.6 broadcast_in_dim.55.refs_12_
  150.9 0.1 compare_reduce_fusion
  151.0 0.1 add_select_fusion.3
  151.1 0.3 reduce-window.9
  151.4 0.1 slice.105
  151.6 0.2 copy.64
  151.7 0.2 copy.65
  151.9 0.1 slice_reduce_fusion
  152.1 0.1 fusion.34
  152.1 1.1 broadcast_in_dim.58.code_ref
  153.3 0.1 pad_bitcast_fusion
  153.4 0.7 fusion.26.chunk
  154.2 0.8 pad_maximum_fusion.1.down_ref.refs_4_
  155.0 0.1 copy.90
  155.0 0.1 slice.158
  155.2 0.1 slice_convert_fusion.1
  155.2 0.1 copy.88
  155.3 0.1 reshape.269
  155.4 0.4 reshape.267
  155.8 0.1 copy.66
  155.9 0.3 reshape.268
  156.3 1.2 gather_fusion
  157.4 0.1 convert_reduce_fusion
  157.5 0.6 fusion.35
  158.2 0.6 pad.40
  158.8 0.6 concatenate.90.fact_ref
  159.4 0.7 dynamic-slice_bitcast_fusion.bias_ref
  160.1 0.1 fusion.23
  160.2 0.1 fusion.19
  160.4 1.2 pad_maximum_fusion.adapt_ref.refs_5_
  161.5 1.0 broadcast_in_dim.52.seg_ref.refs_3_
  162.5 90.0 %first_layer.1 = (bf16[1024,2304]{1,0:T(8,128)(2,1)}, f32[1024,768]{1,0:T(8,128)}, f32[1024,768]{1,0:T(8,128)}, f32[1024,768]{1,0:T(8,128)}, bf16[1024,3072]{1,0...) custom-call(bf16[1152,768]{1,0:T(8,128)(2,1)} %get-tuple-element.59., ...), custom_call_target="tpu_custom_call" | custom-call | tf_op jit(solution)/shard_map/first_layer/pallas_call | solution.py:1214
  252.6 0.0 all-gather.9.cloned.1.call-done
  252.6 0.7 broadcast_in_dim.54.refs_1_.place_ref
  253.3 20.7 %last_forward.1 = (bf16[1024,1536]{1,0:T(8,128)(2,1)}, bf16[128,768]{1,0:T(8,128)(2,1)}, bf16[1024,128]{1,0:T(8,128)(2,1)}, f32[6,256]{1,0:T(8,128)}, f32[128,76...) custom-call(f32[1024,768]{1,0:T(8,128)} %get-tuple-element.66.refs_0, ...), custom_call_target="tpu_custom_call" | custom-call | tf_op jit(solution)/shard_map/last_forward/pallas_call | solution.py:461
  274.0 44.7 %head.1 = (f32[768,128]{1,0:T(8,128)}, f32[1,128]{1,0:T(1,128)}) custom-call(bf16[128,768]{1,0:T(8,128)(2,1)} %get-tuple-element.69.u_ref.feat_ref, f32[50,128]{1,0:T(8,128)} %dynamic-slice_bitcast_fusion.bias_ref, bf16[25600,768]{1,0:T(8,128)(2,1)} %table_any.3, bf16[768,6400]{1,0:T(8,128)(2,1)} %get-tuple-element.70.et_any), custom_call_target="tpu_custom_call" | custom-call | tf_op jit(solution)/shard_map/head/pallas_call | solution.py:1740
  318.7 25.6 %last_backward.1 = (f32[1024,768]{1,0:T(8,128)}, bf16[32,32,768]{2,1,0:T(8,128)(2,1)}, f32[768,128]{1,0:T(8,128)}, f32[8,128]{1,0:T(8,128)}) custom-call(bf16[1152,768]{1,0:T(8,128)(2,1)} %get-tuple-element.59.own_any, bf16[1152,768]{1,0:T(8,128)(2,1)} %copy-done, f32[768,128]{1,0:T(8,128)} %get-tuple-element.71.mean_ref, ...), custom_call_target="tpu_custom_call" | custom-call | tf_op jit(solution)/shard_map/last_backward/pallas_call | solution.py:672
  344.3 59.9 %finish.1 = (f32[8,128]{1,0:T(8,128)}, f32[24,768]{1,0:T(8,128)}, f32[24,128]{1,0:T(8,128)}) custom-call(f32[1024,768]{1,0:T(8,128)} %get-tuple-element.86.dout_any, f32[1024,768]{1,0:T(8,128)} %get-tuple-element.87.one_any, f32[1024,768]{1,0:T(8,128)} %get-tuple-element.88.two_any, bf16[1024,3072]{1,0:T(8,128)(2,1)} %get-tuple-element.89.slope_any, ...), custom_call_target="tpu_custom_call" | custom-call | tf_op jit(solution)/shard_map/finish/pallas_call | solution.py:1500
  404.2 1.8 update.1
  (51 shorter events, 0.3 us)
Async XLA Ops:
  7.2 154.3 %all-gather.7.cloned.1.call-start = ((), (), s32[]{:S(2)}) async-start(), calls=%async_computation | async-start | bytes 12165120 | tf_op jit(solution)/shard_map/all_gather | solution.py:1822
  9.6 2.9 copy-start.10
  9.6 2.9 copy-start.12
  12.4 240.2 %all-gather.9.cloned.1.call-start = ((), (), s32[]{:S(2)}) async-start(), calls=%async_computation.1 | async-start | bytes 4866048 | tf_op jit(solution)/shard_map/all_gather | solution.py:1920
  21.0 37.0 %copy-start.5 = (f32[2,2,8,24]{3,2,1,0:T(8,128)S(1)}, f32[2,2,8,24]{3,2,1,0:T(8,128)}, u32[]{:S(2)}) copy-start(f32[2,2,8,24]{3,2,1,0:T(8,128)} %adapt_w.1) | copy-start | bytes 9220
  21.0 37.1 %copy-start.8 = (f32[1600]{0:T(1024)S(1)}, f32[1600]{0:T(1024)}, u32[]{:S(2)}) copy-start(f32[1600]{0:T(1024)} %param.42) | copy-start | bytes 19204
  55.2 94.1 %collective-permute-start = (bf16[1152,768]{1,0:T(8,128)(2,1)}, bf16[1152,768]{1,0:T(8,128)(2,1)S(1)}, u32[]{:S(2)}, u32[]{:S(2)}) collective-permute-start(bf16[1152,768]{1,0:T(8,128)(2,1)} %get-tuple-element.62), channel_id=1, source_target_pairs={{0,16},{16,0},{1,17},{17,1},{2,18},{18,2},{3,19},{19,3},{4,20},{20... | collective-permute-start | bytes 5308424 | tf_op jit(solution)/shard_map/ppermute | solution.py:1850
  58.8 89.9 %copy-start.2 = (bf16[2,96,768]{2,1,0:T(8,128)(2,1)S(1)}, bf16[2,96,768]{2,1,0:T(8,128)(2,1)}, u32[]{:S(2)}) copy-start(bf16[2,96,768]{2,1,0:T(8,128)(2,1)} %param.39) | copy-start | bytes 884740
  58.8 91.5 %copy-start.11 = (f32[768]{0:T(1024)S(1)}, f32[768]{0:T(1024)}, u32[]{:S(2)}) copy-start(f32[768]{0:T(1024)} %param.41) | copy-start | bytes 9220
  58.8 92.1 %copy-start.7 = (s32[1,1024]{1,0:T(1,128)S(1)}, s32[1,1024]{1,0:T(1,128)}, u32[]{:S(2)}) copy-start(s32[1,1024]{1,0:T(1,128)} %param.26) | copy-start | bytes 12292
  58.8 92.7 %copy-start.3 = (f32[24,768]{1,0:T(8,128)S(1)}, f32[24,768]{1,0:T(8,128)}, u32[]{:S(2)}) copy-start(f32[24,768]{1,0:T(8,128)} %head_w.1) | copy-start | bytes 221188
  58.8 92.7 %copy-start.6 = (bf16[2,2,768,8]{2,3,1,0:T(8,128)(2,1)S(1)}, bf16[2,2,768,8]{2,3,1,0:T(8,128)(2,1)}, u32[]{:S(2)}) copy-start(bf16[2,2,768,8]{2,3,1,0:T(8,128)(2,1)} %param.43) | copy-start | bytes 147460
  149.3 4.1 copy-start
  150.9 10.6 %copy-start.4 = (f32[1,1024]{1,0:T(1,128)}, f32[1,1024]{1,0:T(1,128)S(1)}, u32[]{:S(2)}) copy-start(f32[1,1024]{1,0:T(1,128)S(1)} %convert_element_type.56.seg_row_ref) | copy-start | bytes 12292
  153.2 1.7 copy-start.1
  155.1 2.4 copy-start.13
  162.5 90.1 %copy-start.9 = (s32[1,128]{1,0:T(1,128)S(1)}, s32[1,128]{1,0:T(1,128)}, u32[]{:S(2)}) copy-start(s32[1,128]{1,0:T(1,128)} %place_row_ref.1) | copy-start | bytes 1540
Sparse Core Ops, SparseCore 0:
  12.5 121.1 all-gather.6
  149.5 75.7 all-gather.8

commit v2 on v1

--- a/solution.py
+++ b/solution.py
@@ -962,21 +962,29 @@
 ITEMS = 28
 
 
+PICK = 64
+GROUP = 16
+
+
 def start_body(
-    streams, shards, fact, chunk, table_any, facts, full_chunk, et_out, e_ref, et_ref,
-    fact_sems, own_sems, sends, receives, hands, hands_got,
+    streams, shards, ids, low_ref, groups_any, fact, chunk, got, own_rows, facts, full_chunk, et_out,
+    table, stage, rows, et_ref,
+    row_sends, row_gets, fact_sems, own_sems, sends, receives, hands, hands_got,
 ):
     here = position()
     me = number_of(here)
+    across = device_of(dict(here, x=1 - here["x"]))
+    half, hidden = own_rows.shape
+    batches = half // PICK
+    fill = pltpu.make_async_copy(groups_any, table, own_sems.at[0])
+    fill.start()
+    greet_all(shards)
     own = [
-        pltpu.make_async_copy(source, target, own_sems.at[k])
-        for k, (source, target) in enumerate(
-            ((vocab_rows(table_any, e_ref), e_ref), (fact, facts.at[me]), (chunk, full_chunk.at[me]))
-        )
+        pltpu.make_async_copy(source, target, own_sems.at[1 + k])
+        for k, (source, target) in enumerate(((fact, facts.at[me]), (chunk, full_chunk.at[me])))
     ]
     for copy in own:
         copy.start()
-    greet_all(shards)
     await_all(shards)
     gathers = [
         Gather(
@@ -987,21 +995,65 @@
     for gather in gathers:
         gather.step(0)
     spread(lambda peer: fact, facts, fact_sems, me, shards)
-    own[0].wait()
-    blocks = e_ref.shape[0] // 128
-    each = -(-blocks // (ITEMS - 1))
+
+    def send_rows(b):
+        part = pl.ds(b * PICK, PICK)
+        return pltpu.make_async_remote_copy(
+            src_ref=rows.at[part, :],
+            dst_ref=got.at[part, :],
+            send_sem=row_sends.at[b],
+            recv_sem=row_gets.at[b],
+            device_id=across,
+            device_id_type=MESH,
+        )
+
+    def pick(b):
+        @pl.loop(0, PICK // 8)
+        def _(t):
+            found = [table[ids[b * PICK + t * 8 + k]] for k in range(8)]
+            stage[pl.ds(pl.multiple_of(t * 8, 8), 8)] = jnp.stack(found)
+
+        choose = (
+            lax.broadcasted_iota(jnp.int32, (PICK, PICK * GROUP), 1)
+            == low_ref[b * PICK : (b + 1) * PICK, :]
+        )
+        rows[b * PICK : (b + 1) * PICK, :] = mm(choose.astype(F32).astype(BF), flat(stage)).astype(BF)
+        if b < batches:
+            send_rows(b).start()
+
+    count = et_ref.shape[1]
+    first_group = (here["y"] * 2 + here["c"]) * (count // GROUP)
+
+    def turn(k):
+        block = table[pl.ds(first_group + k * (128 // GROUP), 128 // GROUP)].reshape(128, hidden)
+        et_ref[:, k * 128 : (k + 1) * 128] = block.astype(F32).T.astype(BF)
+
+    fill.wait()
+    picked, turned, blocks = 0, 0, count // 128
     for index in range(1, ITEMS):
-        for k in range((index - 1) * each, min(index * each, blocks)):
-            part = slice(k * 128, (k + 1) * 128)
-            et_ref[:, part] = e_ref[part, :].astype(F32).T.astype(BF)
+        while picked < min(2 * batches, 6 + 4 * index):
+            pick(picked)
+            picked += 1
+        if picked == 2 * batches:
+            for k in range(turned, min(turned + 3, blocks)):
+                turn(k)
+            turned = min(turned + 3, blocks)
         for gather in gathers:
             gather.step(index)
-    turned = pltpu.make_async_copy(et_ref, et_out, own_sems.at[3])
-    turned.start()
+    for k in range(turned, blocks):
+        turn(k)
+    outs = [
+        pltpu.make_async_copy(et_ref, et_out, own_sems.at[3]),
+        pltpu.make_async_copy(rows.at[pl.ds(half, half), :], own_rows, own_sems.at[4]),
+    ]
+    for copy in outs:
+        copy.start()
     for gather in gathers:
         gather.finish()
     collect(facts, fact_sems, me, shards)
-    for copy in own[1:] + [turned]:
+    for b in range(batches):
+        send_rows(b).wait()
+    for copy in own + outs:
         copy.wait()
 
 
@@ -1026,37 +1078,48 @@
     return streams
 
 
-def start_exchange(fact, chunk, table, shards):
+def start_exchange(ids, table, fact, chunk, shards):
     anywhere = pl.BlockSpec(memory_space=pl.ANY)
     shape = jax.ShapeDtypeStruct
     sems = pltpu.SemaphoreType.DMA
-    streams = streams_of(chunk.shape[0], (("zxy", 0.34), ("zyx", 0.34), ("xzy", 0.32)))
-    count, hidden = table.shape[0] // 4, table.shape[1]
+    streams = streams_of(chunk.shape[0], (("xzy", 0.5), ("zxy", 0.28), ("xyz", 0.22)))
+    half, hidden = ids.shape[0] // 2, table.shape[1]
+    count = table.shape[0] // 4
+    low = jnp.arange(ids.size, dtype=jnp.int32) % PICK * GROUP + ids % GROUP
     return pl.pallas_call(
         functools.partial(start_body, streams, shards),
-        in_specs=[anywhere] * 3,
-        out_specs=[anywhere] * 3,
+        in_specs=[
+            pl.BlockSpec(memory_space=pltpu.SMEM),
+            pl.BlockSpec(memory_space=pltpu.VMEM),
+        ]
+        + [anywhere] * 3,
+        out_specs=[anywhere] * 5,
         out_shape=[
+            shape((half, hidden), table.dtype),
+            shape((half, hidden), table.dtype),
             shape((shards, *fact.shape), fact.dtype),
             shape((shards, *chunk.shape), chunk.dtype),
             shape((hidden, count), BF),
         ],
         scratch_shapes=[
-            pltpu.VMEM((count, hidden), BF),
+            pltpu.VMEM((table.shape[0] // GROUP, GROUP, hidden), BF),
+            pltpu.VMEM((PICK, GROUP, hidden), BF),
+            pltpu.VMEM((2 * half, hidden), BF),
             pltpu.VMEM((hidden, count), BF),
+            sems((half // PICK,)),
+            sems((half // PICK,)),
             sems((2,)),
-            sems((4,)),
+            sems((5,)),
             *gather_sems(streams),
         ],
         compiler_params=params(collective_id=1, has_side_effects=True),
-        cost_estimate=pl.CostEstimate(flops=0, bytes_accessed=200_000_000, transcendentals=0),
         name="start_exchange",
-    )(fact, chunk, table)
+    )(ids // GROUP, low[:, None], table.reshape(-1, GROUP, hidden), fact, chunk)
 
 
 def first_layer_body(
     streams, shards,
-    own_any, got_any, in_any, feed_any, chunk, code_ref, spots_ref, gain_ref, shift_ref, down_ref,
+    own_any, got_any, first_any, chunk, code_ref, spots_ref, gain_ref, shift_ref, down_ref,
     adapt_ref, bias_ref, seg_ref, seg_row_ref,
     qkv_out, x_out, one_out, two_out, slope_out, wo_out, full_chunk, mid_ref, log_ref,
     own, got, in_slab, w, wo, up, dn, x, qkv, ctx, two, out, slope,
@@ -1070,8 +1133,6 @@
     lanes = 2 * (hidden // HEADS)
     pairs = hidden // lanes
 
-    cut = dn.shape[1] - feed_any.shape[1]
-
     def slab(source, target, start):
         return source.at[:, pl.ds(start, target.shape[1]), :]
 
@@ -1081,10 +1142,9 @@
             (
                 (own_any.at[pl.ds(0, rows), :], own),
                 (got_any.at[pl.ds(0, rows), :], got),
-                (slab(in_any, in_slab, in_any.shape[1] - in_slab.shape[1]), in_slab),
-                (slab(in_any, up, 0), up),
-                (in_any.at[:, pl.ds(up.shape[1], cut), :], dn.at[:, pl.ds(0, cut), :]),
-                (feed_any, dn.at[:, pl.ds(cut, dn.shape[1] - cut), :]),
+                (slab(first_any, in_slab, 2 * up.shape[1]), in_slab),
+                (slab(first_any, up, 0), up),
+                (slab(first_any, dn, up.shape[1]), dn),
                 (chunk, full_chunk.at[me]),
             )
         )
@@ -1152,7 +1212,7 @@
             {0: ((1, 0), (4, 11)), 1: ((6, 7),), 3: ((8, 9), (12, 19)), 4: ((10, 11),)},
         )
 
-    for copy in loads[3:6]:
+    for copy in loads[3:5]:
         copy.wait()
 
     def tile_copies(i):
@@ -1195,11 +1255,11 @@
     for i in (tiles - 2, tiles - 1):
         for copy in tile_copies(i):
             copy.wait()
-    for copy in early + loads[6:]:
+    for copy in early + loads[5:]:
         copy.wait()
 
 
-def first_layer(own, got, first_in, feed, chunk, more, shards):
+def first_layer(own, got, first, chunk, more, shards):
     whole = pl.BlockSpec(memory_space=pltpu.VMEM)
     anywhere = pl.BlockSpec(memory_space=pl.ANY)
     down, seg_row = more[4], more[-1]
@@ -1213,7 +1273,7 @@
     streams = streams_of(chunk.shape[0], (("zxy", 0.4), ("zyx", 0.4), ("xyz", 0.2)))
     return pl.pallas_call(
         functools.partial(first_layer_body, streams, shards),
-        in_specs=[anywhere] * 5 + [whole] * len(more),
+        in_specs=[anywhere] * 4 + [whole] * len(more),
         out_specs=[anywhere] * 7 + [whole] * 2,
         out_shape=[
             shape((rows, 3 * hidden), BF),
@@ -1240,55 +1300,14 @@
             pltpu.VMEM((2, tile, hidden), F32),
             pltpu.VMEM((2, tile, hidden), F32),
             pltpu.VMEM((2, tile, units), BF),
-            sems((7,)),
+            sems((6,)),
             sems((4, rows // tile)),
             sems((2,)),
             *gather_sems(streams),
         ],
         compiler_params=params(collective_id=3, has_side_effects=True),
         name="first_layer",
-    )(own, got, first_in, feed, chunk, *more)
-
-
-PICK = 64
-GROUP = 16
-
-
-def look_up_body(ids, low_ref, table, first_ref, second_ref, stage):
-    half = first_ref.shape[0]
-    for k, out_ref in enumerate((first_ref, second_ref)):
-
-        @pl.loop(0, half // PICK)
-        def _(b, k=k, out_ref=out_ref):
-            at = k * half + b * PICK
-
-            def one(t, carry):
-                stage[t] = table[ids[at + t]]
-                return carry
-
-            lax.fori_loop(0, PICK, one, 0, unroll=16)
-            choose = (
-                lax.broadcasted_iota(jnp.int32, (PICK, PICK * GROUP), 1)
-                == low_ref[pl.ds(pl.multiple_of(at, PICK), PICK), :]
-            )
-            out_ref[pl.ds(pl.multiple_of(b * PICK, PICK), PICK), :] = mm(
-                choose.astype(F32).astype(BF), flat(stage)
-            ).astype(BF)
-
-
-def look_up(ids, table):
-    whole = pl.BlockSpec(memory_space=pltpu.VMEM)
-    hidden = table.shape[1]
-    low = jnp.arange(ids.size, dtype=jnp.int32) % PICK * GROUP + ids % GROUP
-    return pl.pallas_call(
-        look_up_body,
-        in_specs=[pl.BlockSpec(memory_space=pltpu.SMEM), whole, whole],
-        out_specs=[whole] * 2,
-        out_shape=[jax.ShapeDtypeStruct((ids.size // 2, hidden), table.dtype)] * 2,
-        scratch_shapes=[pltpu.VMEM((PICK, GROUP, hidden), table.dtype)],
-        compiler_params=params(),
-        name="look_up",
-    )(ids // GROUP, low[:, None], table.reshape(-1, GROUP, hidden))
+    )(own, got, first, chunk, *more)
 
 
 def adam(weight, gradient, moment_one, moment_two, fade_one, fade_two):
@@ -1305,7 +1324,7 @@
 
 def finish_body(
     shards, edge,
-    dout_any, one_any, two_any, slope_any, wo_any, in_any, feed_any, qkv_any, gain_ref, log_ref, seg_ref,
+    dout_any, one_any, two_any, slope_any, wo_any, first_any, qkv_any, gain_ref, log_ref, seg_ref,
     seg_row_ref, mid_ref, parts, late_ref, facts,
     sums_ref, dense_ref, total_ref,
     dout, one, two, slope, wo, up, dn, qkv, dctx, dv, grad, core_got, chip_sum, dense_got, grad_got, note, notes,
@@ -1326,7 +1345,6 @@
         ]
 
     here = position()
-    cut = dn.shape[1] - feed_any.shape[1]
     chips = shards // 2
     chip, core = me // 2, here["c"]
     to_core = pltpu.make_async_remote_copy(
@@ -1353,22 +1371,21 @@
         pltpu.make_async_copy(source, target, load_sems.at[k])
         for k, (source, target) in enumerate(
             (
-                (in_any.at[:, pl.ds(up.shape[1], cut), :], dn.at[:, pl.ds(0, cut), :]),
-                (feed_any, dn.at[:, pl.ds(cut, dn.shape[1] - cut), :]),
-                (in_any.at[:, pl.ds(0, up.shape[1]), :], up),
+                (first_any.at[:, pl.ds(up.shape[1], dn.shape[1]), :], dn),
+                (first_any.at[:, pl.ds(0, up.shape[1]), :], up),
                 (wo_any, wo),
                 (qkv_any, qkv),
             )
         )
     ]
-    for copy in tile_loads(0) + loads[:4]:
+    for copy in tile_loads(0) + loads[:3]:
         copy.start()
     for i in range(1, tiles):
         for copy in tile_loads(i):
             copy.start()
-    loads[4].start()
+    loads[3].start()
     greet_all(shards)
-    for copy in loads[:4]:
+    for copy in loads[:3]:
         copy.wait()
 
     @pl.loop(0, tiles)
@@ -1400,7 +1417,7 @@
             def _(k):
                 to_chip(k).start()
 
-    loads[4].wait()
+    loads[3].wait()
     lanes = 2 * (hidden // HEADS)
     pairs = hidden // lanes
 
@@ -1487,7 +1504,7 @@
 
 
 def finish(back, qkv, logs, seg_wide, seg_row, mid, parts, late, facts, edge, shards):
-    dout, one, two, slope, wo, first_in, feed, gains = back
+    dout, one, two, slope, wo, first, gains = back
     slab = pltpu.VMEM((shards, slope.shape[1] // shards, dout.shape[1]), BF)
     parts = parts.reshape(-1, 2, *parts.shape[1:])
     rows, hidden = dout.shape
@@ -1499,7 +1516,7 @@
     tiles = rows // split_of(rows, BACK_TILE, 16)
     return pl.pallas_call(
         functools.partial(finish_body, shards, edge),
-        in_specs=[anywhere] * 8 + [whole] * 8,
+        in_specs=[anywhere] * 7 + [whole] * 8,
         out_specs=[whole] * 3,
         out_shape=[
             shape((8, 128), F32),
@@ -1525,7 +1542,7 @@
             pltpu.VMEM((8, 128), F32),
             pltpu.VMEM((shards, 8, 128), F32),
             sems((4, tiles)),
-            sems((5,)),
+            sems((4,)),
             sems((2,)),
             sems((2,)),
             sems((2,)),
@@ -1533,7 +1550,7 @@
         ],
         compiler_params=params(collective_id=2, has_side_effects=True),
         name="finish",
-    )(dout, one, two, slope, wo, first_in, feed, qkv, gains, logs, seg_wide, seg_row, mid, parts, late, facts)
+    )(dout, one, two, slope, wo, first, qkv, gains, logs, seg_wide, seg_row, mid, parts, late, facts)
 
 
 LOG_ROWS = 16
@@ -1818,11 +1835,7 @@
     grouped = (lax.axis_size("dp"), lax.axis_size("fsdp")) == (2, 16)
     feeds = [[feedforward_up[layer].T, feedforward_down[layer]] for layer in range(layers)]
     attends = [[attention_in_weight[layer].T, attention_out_weight[layer].T] for layer in range(layers)]
-    cut = ff_rows // 32 * 16
-    first_in = lax.all_gather(
-        jnp.concatenate([feeds[0][0], feeds[0][1][:cut], *attends[0]], 0), BOTH, axis=0, tiled=False
-    )
-    feed_chunk = feeds[0][1][cut:]
+    first_chunk = jnp.concatenate(feeds[0] + attends[0], 0)
     last_chunk = pad_rows(
         jnp.concatenate([feeds[1][0], *attends[1], head_projection.astype(BF)], 0), 32
     )
@@ -1846,18 +1859,16 @@
                 for shift in (1, 0)
             ]
         )
-        other_rows, own_rows = look_up(pair_ids, embed)
-        got = lax.ppermute(other_rows, "dp", [(0, 1), (1, 0)])
-        feed_chunk, own_rows = lax.optimization_barrier((feed_chunk, own_rows))
         fact = jnp.concatenate([vocabulary_bias, ups, sequence_task_index.astype(F32)])
         fact_rows = -(-fact.size // 1024) * 8
-        facts, feed_full, own_turned = start_exchange(
+        got, own_rows, facts, first_full, own_turned = start_exchange(
+            pair_ids,
+            embed,
             jnp.pad(fact, (0, fact_rows * 128 - fact.size)).reshape(fact_rows, 128),
-            feed_chunk,
-            embed,
+            first_chunk,
             shards,
         )
-        facts, got, last_feed = lax.optimization_barrier((facts, got, last_feed))
+        facts, last_feed = lax.optimization_barrier((facts, last_feed))
         facts = facts.reshape(shards, -1)
         all_bias = facts[:, :slice_rows].reshape(-1)
         every_up = facts[:, slice_rows : slice_rows + ups.size]
@@ -1924,7 +1935,7 @@
             code, position_embedding, gains, shifts, downs, adapters, layer_bias_vector, seg_wide, seg_row,
         )
         qkv, x_last, one, two, slope, out_first, last_full, mid, logs = first_layer(
-            own_rows, got, first_in, feed_full, last_chunk, more, shards
+            own_rows, got, first_full, last_chunk, more, shards
         )
         slabs = [None, slabs_of(last_full, last_dn)]
         *saved, in_last, out_last, head_full = last_forward(
@@ -1937,13 +1948,15 @@
         ).reshape(-1, 128)
         mean_t, own_logs = head(saved[-1], own_bias, embed, own_turned)
     else:
-        feed_full = lax.all_gather(feed_chunk, BOTH, axis=0, tiled=False)
+        first_full = lax.all_gather(first_chunk, BOTH, axis=0, tiled=False)
         last_full = lax.all_gather(last_chunk, BOTH, axis=0, tiled=False)
-        dn_full = jnp.concatenate([first_in[:, ff_rows : ff_rows + cut], feed_full], 1)
-        slabs = [slabs_of(first_in, dn_full), slabs_of(last_full, last_dn)]
+        slabs = [
+            (slab_of(first_full, 0, ff_rows), slab_of(first_full, ff_rows, ff_rows)),
+            slabs_of(last_full, last_dn),
+        ]
         taken = lambda full_chunk, start, size: full_chunk[:, start : start + size].reshape(-1, hidden)
-        in_first = taken(first_in, ff_rows + cut, qkv_rows)
-        out_first = taken(first_in, ff_rows + cut + qkv_rows, out_rows)
+        in_first = taken(first_full, 2 * ff_rows, qkv_rows)
+        out_first = taken(first_full, 2 * ff_rows + qkv_rows, out_rows)
         in_last = taken(last_full, in_start, qkv_rows)
         out_last = taken(last_full, in_start + qkv_rows, out_rows)
         head_full = taken(last_full, in_start + qkv_rows + out_rows, head_rows)
@@ -2009,7 +2022,7 @@
     heads = (head_projection, head_moment_first, head_moment_second)
     if grouped:
         sums, dense_portion, adapter_portion = finish(
-            (*back, first_in, feed_full, gains), qkv, logs, seg_wide, seg_row, mid, dense_gradient, late, facts, rank, shards
+            (*back, first_full, gains), qkv, logs, seg_wide, seg_row, mid, dense_gradient, late, facts, rank, shards
         )
         loss, norm, *new = update(sums, dense_portion, adapter_portion, facts, heads, adapts)
         return (loss[0, 0], norm[0, 0], *new[3:], *new[:3])

time: 418 us -> 403 us (0.964)
  Pallas kernels: 367 us -> 351 us
    pallas_call x1 -> x0, Pallas kernels: 34.2 us -> none  [look_up(): pl.pallas_call(look_up_body, in_specs=[pl.BlockSpec(memory_space=pltpu.SM...]
    pallas_call x1, Pallas kernels: 89.8 us -> 107 us  [start_exchange(): pl.pallas_call(functools.partial(start_body, streams, shards), in_specs=[...]
  transfers between devices with their start and end apart: 3 -> 1, of which waited for: 0 -> 0; matrix products, arithmetic and copies ran while one was open for 4% -> 3% of each run, Pallas kernels for 52% -> 23%
where the time goes in v2:
time: 403 us; the launch traced here: 396 us
  Pallas kernels  351 us (87%)
  between operations  16.3 us (4%)
  local copies, waits for them, and re-layouts  15.2 us (4%)
  other arithmetic  8.18 us (2%)
  blocking collectives  5.23 us (1%)
    pallas_call x1, Pallas kernels, start_exchange(): pl.pallas_call(functools.partial(start_body, streams, shards), in_specs=[...  107 us
    pallas_call x1, Pallas kernels, first_layer(): pl.pallas_call(functools.partial(first_layer_body, streams, shards), in_s...  90 us
    pallas_call x1, Pallas kernels, finish(): pl.pallas_call(functools.partial(finish_body, shards, edge), in_specs=[an...  59.2 us
    pallas_call x1, Pallas kernels, head(): pl.pallas_call(head_body, in_specs=[whole] * 2 + [anywhere] * 2, out_spec...  46.4 us
    pallas_call x1, Pallas kernels, last_backward(): pl.pallas_call(functools.partial(last_backward_body, places=(up[1], dn[1]...  25.7 us
    pallas_call x1, Pallas kernels, last_forward(): pl.pallas_call(body, in_specs=[whole] * 7 + [anywhere] * (len(weights) +...  20.7 us
  transfers between devices with their start and end apart: 1, of which 0 were waited for; matrix products, arithmetic and copies ran while one was open for 3% of the time, Pallas kernels for 23%

profile of v2, /device:TPU:0, one launch (start us, length us, event | category | flops | bytes accessed | tf_op | source)
XLA Modules:
  0.0 395.7 jit_solution(13090458863642679597)
XLA Ops:
  7.2 0.0 all-gather.5.cloned.1.call-start
  8.0 0.8 reshape.261
  8.8 0.8 concatenate.77
  9.5 0.6 pad_bitcast_fusion.2.fact
  10.1 0.7 pad_add_fusion.2
  10.9 5.2 %all-gather.2 = s32[2,1,1152]{2,1,0:T(1,128)S(1)} all-gather(s32[1,1,1152]{2,1,0:T(1,128)S(1)} %reshape.291), channel_id=2, replica_groups=mesh['dp'=2,'fsdp'=16] {'dp'}, dimensions={0}, use_global_device_ids=true | all-gather | bytes 13824 | tf_op jit(solution)/shard_map/all_gather | solution.py:1847
  16.1 0.8 slice_bitcast_fusion.6
  16.9 1.0 slice_bitcast_fusion.4
  17.9 0.1 dynamic-slice_reduce_fusion.1
  18.0 0.5 copy.63
  18.5 0.0 copy-done
  18.5 0.7 slice_bitcast_fusion
  19.2 0.4 copy.60
  19.6 0.6 add_select_fusion.2.ids
  20.2 1.6 fusion.1.low_ref
  21.9 0.8 pad_maximum_fusion.1.chunk
  22.7 106.9 %start_exchange.1 = (bf16[1152,768]{1,0:T(8,128)(2,1)}, bf16[1152,768]{1,0:T(8,128)(2,1)}, f32[32,24,128]{2,1,0:T(8,128)}, bf16[32,288,768]{2,1,0:T(8,128)(2,1)}, bf16[768,6400]{1,0:T(8,128)(2,1)}) custom-call(s32[2304]{0:T(1024)} %add_select_fusion.2.ids, s32[2304,1]{1,0:T(8,128)} %fusion.1.low_ref, bf16[1600,16,768]{2,1,0:T(8,128)(2,1)} %bitcast.96, ...), custom_call_target="tpu_custom_call" | custom-call | tf_op jit(solution)/shard_map/start_exchange/pallas_call | solution.py:1089
  129.6 0.0 copy-start.7
  129.6 0.0 copy-start.5
  129.7 0.0 copy-start.2
  129.7 0.0 copy-start.4
  129.7 0.0 all-gather.5.cloned.1.call-update
  129.7 1.1 copy.90
  130.8 0.1 slice.142
  131.7 0.1 pad.51.clone
  131.7 0.1 pad.48.clone
  131.8 0.0 copy-done.7
  131.8 0.6 broadcast_in_dim.55.refs_12_
  132.4 0.1 compare_reduce_fusion
  132.5 0.1 add_select_fusion.3
  132.6 0.3 reduce-window.9
  132.9 0.1 slice.89
  133.1 0.2 copy.64
  133.2 0.2 copy.65
  133.4 0.0 copy-start.8
  133.4 0.1 slice_reduce_fusion
  133.5 0.1 fusion.34
  133.6 1.1 broadcast_in_dim.58.code_ref
  134.7 0.1 slice_convert_fusion.1
  134.8 0.1 copy.88
  134.9 0.1 reshape.267
  135.0 0.4 reshape.265
  135.4 0.1 copy.66
  135.5 0.3 reshape.266
  135.9 1.1 gather_fusion
  137.0 0.1 convert_reduce_fusion
  137.1 0.6 fusion.35
  137.8 0.6 pad.40
  138.4 0.6 concatenate.90.fact_ref
  139.1 0.1 pad_bitcast_fusion
  139.2 0.8 fusion.26.chunk
  140.0 0.8 pad_maximum_fusion.2.down_ref.refs_4_
  140.8 0.1 fusion.23
  140.9 0.1 fusion.19
  141.0 1.2 pad_maximum_fusion.adapt_ref.refs_5_
  142.2 1.0 broadcast_in_dim.52.seg_ref.refs_3_
  143.1 90.0 %first_layer.1 = (bf16[1024,2304]{1,0:T(8,128)(2,1)}, f32[1024,768]{1,0:T(8,128)}, f32[1024,768]{1,0:T(8,128)}, f32[1024,768]{1,0:T(8,128)}, bf16[1024,3072]{1,0...) custom-call(bf16[1152,768]{1,0:T(8,128)(2,1)} %get-tuple-element.55., ...), custom_call_target="tpu_custom_call" | custom-call | tf_op jit(solution)/shard_map/first_layer/pallas_call | solution.py:1274
  233.2 0.7 dynamic-slice_bitcast_fusion.bias_ref
  233.9 0.7 broadcast_in_dim.54.refs_1_.place_ref
  234.6 20.7 %last_forward.1 = (bf16[1024,1536]{1,0:T(8,128)(2,1)}, bf16[128,768]{1,0:T(8,128)(2,1)}, bf16[1024,128]{1,0:T(8,128)(2,1)}, f32[6,256]{1,0:T(8,128)}, f32[128,76...) custom-call(f32[1024,768]{1,0:T(8,128)} %get-tuple-element.60.refs_0, ...), custom_call_target="tpu_custom_call" | custom-call | tf_op jit(solution)/shard_map/last_forward/pallas_call | solution.py:461
  255.3 46.4 %head.1 = (f32[768,128]{1,0:T(8,128)}, f32[1,128]{1,0:T(1,128)}) custom-call(bf16[128,768]{1,0:T(8,128)(2,1)} %get-tuple-element.63.u_ref.feat_ref, f32[50,128]{1,0:T(8,128)} %dynamic-slice_bitcast_fusion.bias_ref, bf16[25600,768]{1,0:T(8,128)(2,1)} %table_any.1, bf16[768,6400]{1,0:T(8,128)(2,1)} %get-tuple-element.64.et_any), custom_call_target="tpu_custom_call" | custom-call | tf_op jit(solution)/shard_map/head/pallas_call | solution.py:1757
  301.7 25.7 %last_backward.1 = (f32[1024,768]{1,0:T(8,128)}, bf16[32,32,768]{2,1,0:T(8,128)(2,1)}, f32[768,128]{1,0:T(8,128)}, f32[8,128]{1,0:T(8,128)}) custom-call(bf16[1152,768]{1,0:T(8,128)(2,1)} %get-tuple-element.55.own_any, bf16[1152,768]{1,0:T(8,128)(2,1)} %get-tuple-element.56.got_any, f32[768,128]{1,0:T(8,128)} %get-tuple-element.65.mean_ref, ...), custom_call_target="tpu_custom_call" | custom-call | tf_op jit(solution)/shard_map/last_backward/pallas_call | solution.py:672
  327.4 59.2 %finish.1 = (f32[8,128]{1,0:T(8,128)}, f32[24,768]{1,0:T(8,128)}, f32[24,128]{1,0:T(8,128)}) custom-call(f32[1024,768]{1,0:T(8,128)} %get-tuple-element.80.dout_any, f32[1024,768]{1,0:T(8,128)} %get-tuple-element.81.one_any, f32[1024,768]{1,0:T(8,128)} %get-tuple-element.82.two_any, bf16[1024,3072]{1,0:T(8,128)(2,1)} %get-tuple-element.83.slope_any, ...), custom_call_target="tpu_custom_call" | custom-call | tf_op jit(solution)/shard_map/finish/pallas_call | solution.py:1517
  386.6 1.8 update.1
  (36 shorter events, 0.2 us)
Async XLA Ops:
  7.2 11.3 %copy-start = (bf16[2,768,96]{1,2,0:T(8,128)(2,1)S(1)}, bf16[2,768,96]{1,2,0:T(8,128)(2,1)}, u32[]{:S(2)}) copy-start(bf16[2,768,96]{1,2,0:T(8,128)(2,1)} %param.38) | copy-start | bytes 884740
  7.2 11.4 %copy-start.1 = (bf16[2,96,768]{2,1,0:T(8,128)(2,1)S(1)}, bf16[2,96,768]{2,1,0:T(8,128)(2,1)}, u32[]{:S(2)}) copy-start(bf16[2,96,768]{2,1,0:T(8,128)(2,1)} %param.39) | copy-start | bytes 884740
  7.2 226.7 %all-gather.5.cloned.1.call-start = ((), (), s32[]{:S(2)}) async-start(), calls=%async_computation | async-start | bytes 4866048 | tf_op jit(solution)/shard_map/all_gather | solution.py:1931
  129.6 2.2 copy-start.7
  129.6 2.8 copy-start.5
  129.7 3.3 copy-start.2
  129.7 3.4 copy-start.4
  132.4 9.7 %copy-start.3 = (f32[1,1024]{1,0:T(1,128)}, f32[1,1024]{1,0:T(1,128)S(1)}, u32[]{:S(2)}) copy-start(f32[1,1024]{1,0:T(1,128)S(1)} %convert_element_type.56.seg_row_ref) | copy-start | bytes 12292
  133.4 2.4 copy-start.8
  134.7 2.4 copy-start.9
  143.1 90.7 %copy-start.6 = (s32[1,128]{1,0:T(1,128)S(1)}, s32[1,128]{1,0:T(1,128)}, u32[]{:S(2)}) copy-start(s32[1,128]{1,0:T(1,128)} %place_row_ref.1) | copy-start | bytes 1540
Sparse Core Ops, SparseCore 0:
  129.8 75.9 all-gather.4

commit v3 on v2

--- a/solution.py
+++ b/solution.py
@@ -857,13 +857,13 @@
 
 
 class Gather:
-    def __init__(self, chunk, full_buffer, start, rows, order, sends, receives, hands, hands_got):
+    def __init__(self, chunk, full_buffer, start, rows, order, sends, receives, hands, hands_got, cross=None):
         self.chunk, self.full, self.order = chunk, full_buffer, order
         self.part = pl.ds(start, rows)
         self.sends, self.receives, self.hands, self.hands_got = sends, receives, hands, hands_got
+        self.cross = cross
         self.here = position()
         self.items = relative_places(order)
-        self.pending = []
 
     def origin(self, item):
         here = self.here
@@ -881,7 +881,10 @@
             ways += [("z", 1), ("z", -1)] if axis == "z" else [(axis, 1)]
         return ways
 
-    def copy(self, index, way, slot, item):
+    def handed(self, item):
+        return self.cross is None or sum(abs(step) for step in item.values()) != 1
+
+    def copy(self, index, way, slot, item, crossing=False):
         here = self.here
         place = self.origin(item)
         number, key = number_of(place), self.key(place)
@@ -895,6 +898,9 @@
             target = dict(here)
             target[axis] = here["z"] + step if axis == "z" else 1 - here[axis]
             sends, receives = self.sends.at[index * 4 + slot], self.receives.at[key]
+            if crossing:
+                target["c"] = 1 - here["c"]
+                sends, receives = self.cross.at[slot], self.hands_got.at[key]
         return pltpu.make_async_remote_copy(
             src_ref=source,
             dst_ref=self.full.at[number, self.part, :],
@@ -917,7 +923,11 @@
                 self.arrived(index, item)
             for slot, way in enumerate(self.outward(item)):
                 self.when_way(way, lambda way=way, slot=slot: self.copy(index, way, slot, item).start())
-            self.copy(index, None, 0, item).start()
+            if self.handed(item):
+                self.copy(index, None, 0, item).start()
+            if self.cross is not None and not any(item.values()):
+                for slot, way in enumerate(self.outward(item)):
+                    self.when_way(way, lambda way=way, slot=slot: self.copy(index, way, slot, item, True).start())
 
     def when_way(self, way, act):
         axis, step = way
@@ -946,7 +956,13 @@
             def _(index=index, item=item):
                 for slot, way in enumerate(self.outward(item)):
                     self.when_way(way, lambda way=way, slot=slot: self.copy(index, way, slot, item).wait_send())
-                self.copy(index, None, 0, item).wait_send()
+                if self.cross is not None and not any(item.values()):
+                    for slot, way in enumerate(self.outward(item)):
+                        self.when_way(
+                            way, lambda way=way, slot=slot: self.copy(index, way, slot, item, True).wait_send()
+                        )
+                if self.handed(item):
+                    self.copy(index, None, 0, item).wait_send()
                 place = dict(self.origin(item), c=1 - self.here["c"])
                 spot = self.full.at[number_of(place), self.part, :]
                 pltpu.make_async_remote_copy(
@@ -1119,11 +1135,11 @@
 
 def first_layer_body(
     streams, shards,
-    own_any, got_any, first_any, chunk, code_ref, spots_ref, gain_ref, shift_ref, down_ref,
+    own_any, got_any, first_any, other_any, chunk, code_ref, spots_ref, gain_ref, shift_ref, down_ref,
     adapt_ref, bias_ref, seg_ref, seg_row_ref,
     qkv_out, x_out, one_out, two_out, slope_out, wo_out, full_chunk, mid_ref, log_ref,
     own, got, in_slab, w, wo, up, dn, x, qkv, ctx, two, out, slope,
-    load_sems, tile_sems, out_sems, sends, receives, hands, hands_got,
+    load_sems, tile_sems, out_sems, cross, sends, receives, hands, hands_got,
 ):
     here = position()
     me = number_of(here)
@@ -1133,6 +1149,9 @@
     lanes = 2 * (hidden // HEADS)
     pairs = hidden // lanes
 
+    rest = first_any.shape[1] - up.shape[1]
+    cut = dn.shape[1] - rest
+
     def slab(source, target, start):
         return source.at[:, pl.ds(start, target.shape[1]), :]
 
@@ -1142,9 +1161,10 @@
             (
                 (own_any.at[pl.ds(0, rows), :], own),
                 (got_any.at[pl.ds(0, rows), :], got),
-                (slab(first_any, in_slab, 2 * up.shape[1]), in_slab),
+                (slab(other_any, in_slab, cut), in_slab),
                 (slab(first_any, up, 0), up),
-                (slab(first_any, dn, up.shape[1]), dn),
+                (other_any.at[:, pl.ds(0, cut), :], dn.at[:, pl.ds(0, cut), :]),
+                (first_any.at[:, pl.ds(up.shape[1], rest), :], dn.at[:, pl.ds(cut, rest), :]),
                 (chunk, full_chunk.at[me]),
             )
         )
@@ -1152,18 +1172,18 @@
     for copy in loads:
         copy.start()
     barrier = pltpu.get_barrier_semaphore()
-    peers = [
-        dict(here, c=1 - here["c"]),
-        dict(here, x=1 - here["x"]),
-        dict(here, y=1 - here["y"]),
-        *[dict(here, z=flip(here["z"], k)) for k in (1, 2, 3)],
-    ]
+    peers = [dict(here, c=1 - here["c"])]
+    for core in (here["c"], 1 - here["c"]):
+        there = dict(here, c=core)
+        peers += [dict(there, x=1 - here["x"]), dict(there, y=1 - here["y"])]
+        peers += [dict(there, z=flip(here["z"], k)) for k in (1, 2, 3)]
     for peer in peers:
         pl.semaphore_signal(barrier, inc=1, device_id=device_of(peer), device_id_type=MESH)
     pl.semaphore_wait(barrier, len(peers))
     gathers = [
         Gather(
-            chunk, full_chunk, start, size, order, sends.at[k], receives.at[k], hands.at[k], hands_got.at[k]
+            chunk, full_chunk, start, size, order, sends.at[k], receives.at[k], hands.at[k], hands_got.at[k],
+            cross.at[k],
         )
         for k, (start, size, order) in enumerate(streams)
     ]
@@ -1209,10 +1229,17 @@
 
         at(
             p - (pairs - 6),
-            {0: ((1, 0), (4, 11)), 1: ((6, 7),), 3: ((8, 9), (12, 19)), 4: ((10, 11),)},
-        )
-
-    for copy in loads[3:5]:
+            {
+                0: ((1, 0), (4, 11)),
+                1: ((6, 7),),
+                2: ((14, 15),),
+                3: ((8, 9),),
+                4: ((16, 17), (12, 19)),
+                5: ((10, 11),),
+            },
+        )
+
+    for copy in loads[3:6]:
         copy.wait()
 
     def tile_copies(i):
@@ -1230,7 +1257,7 @@
             )
         ]
 
-    plan = {0: ((12, 13), (20, 27)), 1: ((14, 17),), 2: ((18, 21),), 3: ((22, 27),)}
+    plan = {0: ((12, 13),), 1: ((18, 21), (20, 27)), 2: ((22, 25),), 3: ((26, 27),)}
 
     @pl.loop(0, tiles)
     def _(i):
@@ -1255,11 +1282,11 @@
     for i in (tiles - 2, tiles - 1):
         for copy in tile_copies(i):
             copy.wait()
-    for copy in early + loads[5:]:
+    for copy in early + loads[6:]:
         copy.wait()
 
 
-def first_layer(own, got, first, chunk, more, shards):
+def first_layer(own, got, first, other, chunk, more, shards):
     whole = pl.BlockSpec(memory_space=pltpu.VMEM)
     anywhere = pl.BlockSpec(memory_space=pl.ANY)
     down, seg_row = more[4], more[-1]
@@ -1273,7 +1300,7 @@
     streams = streams_of(chunk.shape[0], (("zxy", 0.4), ("zyx", 0.4), ("xyz", 0.2)))
     return pl.pallas_call(
         functools.partial(first_layer_body, streams, shards),
-        in_specs=[anywhere] * 4 + [whole] * len(more),
+        in_specs=[anywhere] * 5 + [whole] * len(more),
         out_specs=[anywhere] * 7 + [whole] * 2,
         out_shape=[
             shape((rows, 3 * hidden), BF),
@@ -1300,14 +1327,15 @@
             pltpu.VMEM((2, tile, hidden), F32),
             pltpu.VMEM((2, tile, hidden), F32),
             pltpu.VMEM((2, tile, units), BF),
-            sems((6,)),
+            sems((7,)),
             sems((4, rows // tile)),
             sems((2,)),
+            sems((len(streams), 4)),
             *gather_sems(streams),
         ],
         compiler_params=params(collective_id=3, has_side_effects=True),
         name="first_layer",
-    )(own, got, first, chunk, *more)
+    )(own, got, first, other, chunk, *more)
 
 
 def adam(weight, gradient, moment_one, moment_two, fade_one, fade_two):
@@ -1324,7 +1352,7 @@
 
 def finish_body(
     shards, edge,
-    dout_any, one_any, two_any, slope_any, wo_any, first_any, qkv_any, gain_ref, log_ref, seg_ref,
+    dout_any, one_any, two_any, slope_any, wo_any, first_any, other_any, qkv_any, gain_ref, log_ref, seg_ref,
     seg_row_ref, mid_ref, parts, late_ref, facts,
     sums_ref, dense_ref, total_ref,
     dout, one, two, slope, wo, up, dn, qkv, dctx, dv, grad, core_got, chip_sum, dense_got, grad_got, note, notes,
@@ -1345,6 +1373,8 @@
         ]
 
     here = position()
+    rest = first_any.shape[1] - up.shape[1]
+    cut = dn.shape[1] - rest
     chips = shards // 2
     chip, core = me // 2, here["c"]
     to_core = pltpu.make_async_remote_copy(
@@ -1371,21 +1401,22 @@
         pltpu.make_async_copy(source, target, load_sems.at[k])
         for k, (source, target) in enumerate(
             (
-                (first_any.at[:, pl.ds(up.shape[1], dn.shape[1]), :], dn),
+                (other_any.at[:, pl.ds(0, cut), :], dn.at[:, pl.ds(0, cut), :]),
+                (first_any.at[:, pl.ds(up.shape[1], rest), :], dn.at[:, pl.ds(cut, rest), :]),
                 (first_any.at[:, pl.ds(0, up.shape[1]), :], up),
                 (wo_any, wo),
                 (qkv_any, qkv),
             )
         )
     ]
-    for copy in tile_loads(0) + loads[:3]:
+    for copy in tile_loads(0) + loads[:4]:
         copy.start()
     for i in range(1, tiles):
         for copy in tile_loads(i):
             copy.start()
-    loads[3].start()
+    loads[4].start()
     greet_all(shards)
-    for copy in loads[:3]:
+    for copy in loads[:4]:
         copy.wait()
 
     @pl.loop(0, tiles)
@@ -1417,7 +1448,7 @@
             def _(k):
                 to_chip(k).start()
 
-    loads[3].wait()
+    loads[4].wait()
     lanes = 2 * (hidden // HEADS)
     pairs = hidden // lanes
 
@@ -1504,7 +1535,7 @@
 
 
 def finish(back, qkv, logs, seg_wide, seg_row, mid, parts, late, facts, edge, shards):
-    dout, one, two, slope, wo, first, gains = back
+    dout, one, two, slope, wo, first, other, gains = back
     slab = pltpu.VMEM((shards, slope.shape[1] // shards, dout.shape[1]), BF)
     parts = parts.reshape(-1, 2, *parts.shape[1:])
     rows, hidden = dout.shape
@@ -1516,7 +1547,7 @@
     tiles = rows // split_of(rows, BACK_TILE, 16)
     return pl.pallas_call(
         functools.partial(finish_body, shards, edge),
-        in_specs=[anywhere] * 7 + [whole] * 8,
+        in_specs=[anywhere] * 8 + [whole] * 8,
         out_specs=[whole] * 3,
         out_shape=[
             shape((8, 128), F32),
@@ -1542,7 +1573,7 @@
             pltpu.VMEM((8, 128), F32),
             pltpu.VMEM((shards, 8, 128), F32),
             sems((4, tiles)),
-            sems((4,)),
+            sems((5,)),
             sems((2,)),
             sems((2,)),
             sems((2,)),
@@ -1550,7 +1581,7 @@
         ],
         compiler_params=params(collective_id=2, has_side_effects=True),
         name="finish",
-    )(dout, one, two, slope, wo, first, qkv, gains, logs, seg_wide, seg_row, mid, parts, late, facts)
+    )(dout, one, two, slope, wo, first, other, qkv, gains, logs, seg_wide, seg_row, mid, parts, late, facts)
 
 
 LOG_ROWS = 16
@@ -1835,7 +1866,11 @@
     grouped = (lax.axis_size("dp"), lax.axis_size("fsdp")) == (2, 16)
     feeds = [[feedforward_up[layer].T, feedforward_down[layer]] for layer in range(layers)]
     attends = [[attention_in_weight[layer].T, attention_out_weight[layer].T] for layer in range(layers)]
-    first_chunk = jnp.concatenate(feeds[0] + attends[0], 0)
+    cut = ff_rows // 32 * 16
+    first_chunk = jnp.concatenate([feeds[0][0], feeds[0][1][cut:]], 0)
+    other_full = lax.all_gather(
+        jnp.concatenate([feeds[0][1][:cut], *attends[0]], 0), BOTH, axis=0, tiled=False
+    )
     last_chunk = pad_rows(
         jnp.concatenate([feeds[1][0], *attends[1], head_projection.astype(BF)], 0), 32
     )
@@ -1935,7 +1970,7 @@
             code, position_embedding, gains, shifts, downs, adapters, layer_bias_vector, seg_wide, seg_row,
         )
         qkv, x_last, one, two, slope, out_first, last_full, mid, logs = first_layer(
-            own_rows, got, first_full, last_chunk, more, shards
+            own_rows, got, first_full, other_full, last_chunk, more, shards
         )
         slabs = [None, slabs_of(last_full, last_dn)]
         *saved, in_last, out_last, head_full = last_forward(
@@ -1950,13 +1985,11 @@
     else:
         first_full = lax.all_gather(first_chunk, BOTH, axis=0, tiled=False)
         last_full = lax.all_gather(last_chunk, BOTH, axis=0, tiled=False)
-        slabs = [
-            (slab_of(first_full, 0, ff_rows), slab_of(first_full, ff_rows, ff_rows)),
-            slabs_of(last_full, last_dn),
-        ]
+        dn_full = jnp.concatenate([other_full[:, :cut], first_full[:, ff_rows:]], 1)
+        slabs = [slabs_of(first_full[:, :ff_rows], dn_full), slabs_of(last_full, last_dn)]
         taken = lambda full_chunk, start, size: full_chunk[:, start : start + size].reshape(-1, hidden)
-        in_first = taken(first_full, 2 * ff_rows, qkv_rows)
-        out_first = taken(first_full, 2 * ff_rows + qkv_rows, out_rows)
+        in_first = taken(other_full, cut, qkv_rows)
+        out_first = taken(other_full, cut + qkv_rows, out_rows)
         in_last = taken(last_full, in_start, qkv_rows)
         out_last = taken(last_full, in_start + qkv_rows, out_rows)
         head_full = taken(last_full, in_start + qkv_rows + out_rows, head_rows)
@@ -2022,7 +2055,7 @@
     heads = (head_projection, head_moment_first, head_moment_second)
     if grouped:
         sums, dense_portion, adapter_portion = finish(
-            (*back, first_full, gains), qkv, logs, seg_wide, seg_row, mid, dense_gradient, late, facts, rank, shards
+            (*back, first_full, other_full, gains), qkv, logs, seg_wide, seg_row, mid, dense_gradient, late, facts, rank, shards
         )
         loss, norm, *new = update(sums, dense_portion, adapter_portion, facts, heads, adapts)
         return (loss[0, 0], norm[0, 0], *new[3:], *new[:3])

time: 403 us -> 410 us (1.017)
  Pallas kernels: 351 us -> 358 us
    pallas_call x1, Pallas kernels: 90 us -> 99.9 us  [first_layer(): pl.pallas_call(functools.partial(first_layer_body, streams, shards), in_s...]
  transfers between devices with their start and end apart: 1 -> 2, of which waited for: 0 -> 0; matrix products, arithmetic and copies ran while one was open for 3% -> 5% of each run, Pallas kernels for 23% -> 52%
where the time goes in v3:
time: 410 us; the launch traced here: 403 us
  Pallas kernels  358 us (87%)
  between operations  16.3 us (4%)
  local copies, waits for them, and re-layouts  14.7 us (4%)
  other arithmetic  8.06 us (2%)
  blocking collectives  5.23 us (1%)
    pallas_call x1, Pallas kernels, start_exchange(): pl.pallas_call(functools.partial(start_body, streams, shards), in_specs=[...  108 us
    pallas_call x1, Pallas kernels, first_layer(): pl.pallas_call(functools.partial(first_layer_body, streams, shards), in_s...  99.9 us
    pallas_call x1, Pallas kernels, finish(): pl.pallas_call(functools.partial(finish_body, shards, edge), in_specs=[an...  58.7 us
    pallas_call x1, Pallas kernels, head(): pl.pallas_call(head_body, in_specs=[whole] * 2 + [anywhere] * 2, out_spec...  43.9 us
    pallas_call x1, Pallas kernels, last_backward(): pl.pallas_call(functools.partial(last_backward_body, places=(up[1], dn[1]...  25.7 us
    pallas_call x1, Pallas kernels, last_forward(): pl.pallas_call(body, in_specs=[whole] * 7 + [anywhere] * (len(weights) +...  20.7 us
  transfers between devices with their start and end apart: 2, of which 0 were waited for; matrix products, arithmetic and copies ran while one was open for 5% of the time, Pallas kernels for 52%

profile of v3, /device:TPU:0, one launch (start us, length us, event | category | flops | bytes accessed | tf_op | source)
XLA Modules:
  0.0 402.9 jit_solution(16046612970238141481)
XLA Ops:
  7.2 0.0 all-gather.7.cloned.1.call-start
  7.2 0.8 slice_bitcast_fusion.7
  8.0 0.9 slice_bitcast_fusion.5
  9.0 1.0 slice_bitcast_fusion.3
  9.9 0.0 copy-start.7
  10.0 0.7 pad_maximum_fusion.3
  10.7 0.0 all-gather.7.cloned.1.call-update
  10.7 0.0 all-gather.9.cloned.1.call-start
  11.4 0.1 reshape.263
  11.6 5.2 %all-gather.3 = s32[2,1,1152]{2,1,0:T(1,128)S(1)} all-gather(s32[1,1,1152]{2,1,0:T(1,128)S(1)} %reshape.294), channel_id=2, replica_groups=mesh['dp'=2,'fsdp'=16] {'dp'}, dimensions={0}, use_global_device_ids=true | all-gather | bytes 13824 | tf_op jit(solution)/shard_map/all_gather | solution.py:1882
  16.8 0.1 dynamic-slice_reduce_fusion.1
  16.9 0.5 copy.63
  17.4 0.4 copy.60
  17.9 0.1 concatenate.80
  18.0 0.6 pad_bitcast_fusion.2.fact
  18.6 0.6 add_select_fusion.2.ids
  19.2 0.7 pad_maximum_fusion.2.chunk
  19.9 1.6 fusion.1.low_ref
  21.5 107.8 %start_exchange.1 = (bf16[1152,768]{1,0:T(8,128)(2,1)}, bf16[1152,768]{1,0:T(8,128)(2,1)}, f32[32,24,128]{2,1,0:T(8,128)}, bf16[32,144,768]{2,1,0:T(8,128)(2,1)}, bf16[768,6400]{1,0:T(8,128)(2,1)}) custom-call(s32[2304]{0:T(1024)} %add_select_fusion.2.ids, s32[2304,1]{1,0:T(8,128)} %fusion.1.low_ref, bf16[1600,16,768]{2,1,0:T(8,128)(2,1)} %bitcast.99, ...), custom_call_target="tpu_custom_call" | custom-call | tf_op jit(solution)/shard_map/start_exchange/pallas_call | solution.py:1105
  129.4 0.0 copy-start.2
  129.4 0.0 copy-start.5
  129.4 0.7 slice_bitcast_fusion
  130.1 0.0 all-gather.9.cloned.1.call-update
  130.1 1.1 copy.90
  131.2 0.1 slice.158
  132.0 0.1 pad.51.clone
  132.1 0.1 pad.48.clone
  132.2 0.6 broadcast_in_dim.55.refs_12_
  132.8 0.1 compare_reduce_fusion
  132.9 0.1 add_select_fusion.3
  133.0 0.3 reduce-window.9
  133.3 0.1 slice.104
  133.4 0.2 copy.64
  133.6 0.2 copy.65
  133.8 0.1 slice_reduce_fusion
  133.9 0.1 fusion.34
  134.0 1.1 broadcast_in_dim.58.code_ref
  135.1 0.1 slice_convert_fusion.1
  135.1 0.1 copy.88
  135.2 0.1 reshape.269
  135.4 0.4 reshape.267
  135.7 0.1 copy.66
  135.9 0.3 reshape.268
  136.2 1.1 gather_fusion
  137.4 0.1 convert_reduce_fusion
  137.5 0.6 fusion.35
  138.1 0.6 pad.40
  138.8 0.6 concatenate.94.fact_ref
  139.4 0.7 dynamic-slice_bitcast_fusion.bias_ref
  140.1 0.1 pad_bitcast_fusion
  140.2 0.8 fusion.26.chunk
  141.0 0.8 pad_maximum_fusion.1.down_ref.refs_4_
  141.8 0.1 fusion.23
  141.9 0.1 fusion.19
  142.0 1.1 pad_maximum_fusion.adapt_ref.refs_5_
  143.2 1.0 broadcast_in_dim.52.seg_ref.refs_3_
  144.2 99.9 %first_layer.1 = (bf16[1024,2304]{1,0:T(8,128)(2,1)}, f32[1024,768]{1,0:T(8,128)}, f32[1024,768]{1,0:T(8,128)}, f32[1024,768]{1,0:T(8,128)}, bf16[1024,3072]{1,0...) custom-call(bf16[1152,768]{1,0:T(8,128)(2,1)} %get-tuple-element.55., ...), custom_call_target="tpu_custom_call" | custom-call | tf_op jit(solution)/shard_map/first_layer/pallas_call | solution.py:1301
  244.1 0.0 all-gather.9.cloned.1.call-done
  244.1 0.7 broadcast_in_dim.54.refs_1_.place_ref
  244.8 20.7 %last_forward.1 = (bf16[1024,1536]{1,0:T(8,128)(2,1)}, bf16[128,768]{1,0:T(8,128)(2,1)}, bf16[1024,128]{1,0:T(8,128)(2,1)}, f32[6,256]{1,0:T(8,128)}, f32[128,76...) custom-call(f32[1024,768]{1,0:T(8,128)} %get-tuple-element.60.refs_0, ...), custom_call_target="tpu_custom_call" | custom-call | tf_op jit(solution)/shard_map/last_forward/pallas_call | solution.py:461
  265.6 43.9 %head.1 = (f32[768,128]{1,0:T(8,128)}, f32[1,128]{1,0:T(1,128)}) custom-call(bf16[128,768]{1,0:T(8,128)(2,1)} %get-tuple-element.63.u_ref.feat_ref, f32[50,128]{1,0:T(8,128)} %dynamic-slice_bitcast_fusion.bias_ref, bf16[25600,768]{1,0:T(8,128)(2,1)} %table_any.1, bf16[768,6400]{1,0:T(8,128)(2,1)} %get-tuple-element.64.et_any), custom_call_target="tpu_custom_call" | custom-call | tf_op jit(solution)/shard_map/head/pallas_call | solution.py:1788
  309.4 25.7 %last_backward.1 = (f32[1024,768]{1,0:T(8,128)}, bf16[32,32,768]{2,1,0:T(8,128)(2,1)}, f32[768,128]{1,0:T(8,128)}, f32[8,128]{1,0:T(8,128)}) custom-call(bf16[1152,768]{1,0:T(8,128)(2,1)} %get-tuple-element.55.own_any, bf16[1152,768]{1,0:T(8,128)(2,1)} %get-tuple-element.56.got_any, f32[768,128]{1,0:T(8,128)} %get-tuple-element.65.mean_ref, ...), custom_call_target="tpu_custom_call" | custom-call | tf_op jit(solution)/shard_map/last_backward/pallas_call | solution.py:672
  335.1 58.7 %finish.1 = (f32[8,128]{1,0:T(8,128)}, f32[24,768]{1,0:T(8,128)}, f32[24,128]{1,0:T(8,128)}) custom-call(f32[1024,768]{1,0:T(8,128)} %get-tuple-element.80.dout_any, f32[1024,768]{1,0:T(8,128)} %get-tuple-element.81.one_any, f32[1024,768]{1,0:T(8,128)} %get-tuple-element.82.two_any, bf16[1024,3072]{1,0:T(8,128)(2,1)} %get-tuple-element.83.slope_any, ...), custom_call_target="tpu_custom_call" | custom-call | tf_op jit(solution)/shard_map/finish/pallas_call | solution.py:1548
  393.8 1.8 update.1
  (47 shorter events, 0.3 us)
Async XLA Ops:
  7.2 4.3 %copy-start.4 = (f32[2,2,8,24]{3,2,1,0:T(8,128)S(1)}, f32[2,2,8,24]{3,2,1,0:T(8,128)}, u32[]{:S(2)}) copy-start(f32[2,2,8,24]{3,2,1,0:T(8,128)} %adapt_w.1) | copy-start | bytes 9220
  7.2 4.3 %copy-start.11 = (s32[1,128]{1,0:T(1,128)S(1)}, s32[1,128]{1,0:T(1,128)}, u32[]{:S(2)}) copy-start(s32[1,128]{1,0:T(1,128)} %param.28) | copy-start | bytes 1540
  7.2 4.3 %copy-start.9 = (s32[1,1024]{1,0:T(1,128)S(1)}, s32[1,1024]{1,0:T(1,128)}, u32[]{:S(2)}) copy-start(s32[1,1024]{1,0:T(1,128)} %param.25) | copy-start | bytes 12292
  7.2 136.0 %all-gather.7.cloned.1.call-start = ((), (), s32[]{:S(2)}) async-start(), calls=%async_computation | async-start | bytes 7299072 | tf_op jit(solution)/shard_map/all_gather | solution.py:1871
  9.9 7.9 %copy-start.7 = (f32[1600]{0:T(1024)S(1)}, f32[1600]{0:T(1024)}, u32[]{:S(2)}) copy-start(f32[1600]{0:T(1024)} %param.42) | copy-start | bytes 19204
  10.0 9.2 %copy-start = (bf16[2,768,96]{1,2,0:T(8,128)(2,1)S(1)}, bf16[2,768,96]{1,2,0:T(8,128)(2,1)}, u32[]{:S(2)}) copy-start(bf16[2,768,96]{1,2,0:T(8,128)(2,1)} %param.38) | copy-start | bytes 884740
  10.7 233.4 %all-gather.9.cloned.1.call-start = ((), (), s32[]{:S(2)}) async-start(), calls=%async_computation.1 | async-start | bytes 4866048 | tf_op jit(solution)/shard_map/all_gather | solution.py:1966
  21.5 107.8 %copy-start.1 = (bf16[2,96,768]{2,1,0:T(8,128)(2,1)S(1)}, bf16[2,96,768]{2,1,0:T(8,128)(2,1)}, u32[]{:S(2)}) copy-start(bf16[2,96,768]{2,1,0:T(8,128)(2,1)} %param.39) | copy-start | bytes 884740
  129.4 2.9 copy-start.10
  129.4 3.4 copy-start.6
  129.4 4.0 copy-start.2
  129.4 4.0 copy-start.5
  132.8 10.4 %copy-start.3 = (f32[1,1024]{1,0:T(1,128)}, f32[1,1024]{1,0:T(1,128)S(1)}, u32[]{:S(2)}) copy-start(f32[1,1024]{1,0:T(1,128)S(1)} %convert_element_type.56.seg_row_ref) | copy-start | bytes 12292
  135.1 2.4 copy-start.12
  144.2 100.0 %copy-start.8 = (s32[1,128]{1,0:T(1,128)S(1)}, s32[1,128]{1,0:T(1,128)}, u32[]{:S(2)}) copy-start(s32[1,128]{1,0:T(1,128)} %place_row_ref.1) | copy-start | bytes 1540
Sparse Core Ops, SparseCore 0:
  10.9 98.2 all-gather.6
  130.2 76.3 all-gather.8

commit v4 on v3

--- a/solution.py
+++ b/solution.py
@@ -857,11 +857,10 @@
 
 
 class Gather:
-    def __init__(self, chunk, full_buffer, start, rows, order, sends, receives, hands, hands_got, cross=None):
+    def __init__(self, chunk, full_buffer, start, rows, order, sends, receives, hands, hands_got):
         self.chunk, self.full, self.order = chunk, full_buffer, order
         self.part = pl.ds(start, rows)
         self.sends, self.receives, self.hands, self.hands_got = sends, receives, hands, hands_got
-        self.cross = cross
         self.here = position()
         self.items = relative_places(order)
 
@@ -881,10 +880,7 @@
             ways += [("z", 1), ("z", -1)] if axis == "z" else [(axis, 1)]
         return ways
 
-    def handed(self, item):
-        return self.cross is None or sum(abs(step) for step in item.values()) != 1
-
-    def copy(self, index, way, slot, item, crossing=False):
+    def copy(self, index, way, slot, item):
         here = self.here
         place = self.origin(item)
         number, key = number_of(place), self.key(place)
@@ -898,9 +894,6 @@
             target = dict(here)
             target[axis] = here["z"] + step if axis == "z" else 1 - here[axis]
             sends, receives = self.sends.at[index * 4 + slot], self.receives.at[key]
-            if crossing:
-                target["c"] = 1 - here["c"]
-                sends, receives = self.cross.at[slot], self.hands_got.at[key]
         return pltpu.make_async_remote_copy(
             src_ref=source,
             dst_ref=self.full.at[number, self.part, :],
@@ -923,11 +916,7 @@
                 self.arrived(index, item)
             for slot, way in enumerate(self.outward(item)):
                 self.when_way(way, lambda way=way, slot=slot: self.copy(index, way, slot, item).start())
-            if self.handed(item):
-                self.copy(index, None, 0, item).start()
-            if self.cross is not None and not any(item.values()):
-                for slot, way in enumerate(self.outward(item)):
-                    self.when_way(way, lambda way=way, slot=slot: self.copy(index, way, slot, item, True).start())
+            self.copy(index, None, 0, item).start()
 
     def when_way(self, way, act):
         axis, step = way
@@ -956,13 +945,7 @@
             def _(index=index, item=item):
                 for slot, way in enumerate(self.outward(item)):
                     self.when_way(way, lambda way=way, slot=slot: self.copy(index, way, slot, item).wait_send())
-                if self.cross is not None and not any(item.values()):
-                    for slot, way in enumerate(self.outward(item)):
-                        self.when_way(
-                            way, lambda way=way, slot=slot: self.copy(index, way, slot, item, True).wait_send()
-                        )
-                if self.handed(item):
-                    self.copy(index, None, 0, item).wait_send()
+                self.copy(index, None, 0, item).wait_send()
                 place = dict(self.origin(item), c=1 - self.here["c"])
                 spot = self.full.at[number_of(place), self.part, :]
                 pltpu.make_async_remote_copy(
@@ -983,8 +966,8 @@
 
 
 def start_body(
-    streams, shards, ids, low_ref, groups_any, fact, chunk, got, own_rows, facts, full_chunk, et_out,
-    table, stage, rows, et_ref,
+    streams, shards, ids, low_ref, groups_any, fact, chunk, got, own_rows, facts, full_chunk,
+    table, stage, rows,
     row_sends, row_gets, fact_sems, own_sems, sends, receives, hands, hands_got,
 ):
     here = position()
@@ -1037,31 +1020,15 @@
         if b < batches:
             send_rows(b).start()
 
-    count = et_ref.shape[1]
-    first_group = (here["y"] * 2 + here["c"]) * (count // GROUP)
-
-    def turn(k):
-        block = table[pl.ds(first_group + k * (128 // GROUP), 128 // GROUP)].reshape(128, hidden)
-        et_ref[:, k * 128 : (k + 1) * 128] = block.astype(F32).T.astype(BF)
-
     fill.wait()
-    picked, turned, blocks = 0, 0, count // 128
+    picked = 0
     for index in range(1, ITEMS):
         while picked < min(2 * batches, 6 + 4 * index):
             pick(picked)
             picked += 1
-        if picked == 2 * batches:
-            for k in range(turned, min(turned + 3, blocks)):
-                turn(k)
-            turned = min(turned + 3, blocks)
         for gather in gathers:
             gather.step(index)
-    for k in range(turned, blocks):
-        turn(k)
-    outs = [
-        pltpu.make_async_copy(et_ref, et_out, own_sems.at[3]),
-        pltpu.make_async_copy(rows.at[pl.ds(half, half), :], own_rows, own_sems.at[4]),
-    ]
+    outs = [pltpu.make_async_copy(rows.at[pl.ds(half, half), :], own_rows, own_sems.at[3])]
     for copy in outs:
         copy.start()
     for gather in gathers:
@@ -1100,7 +1067,6 @@
     sems = pltpu.SemaphoreType.DMA
     streams = streams_of(chunk.shape[0], (("xzy", 0.5), ("zxy", 0.28), ("xyz", 0.22)))
     half, hidden = ids.shape[0] // 2, table.shape[1]
-    count = table.shape[0] // 4
     low = jnp.arange(ids.size, dtype=jnp.int32) % PICK * GROUP + ids % GROUP
     return pl.pallas_call(
         functools.partial(start_body, streams, shards),
@@ -1109,23 +1075,21 @@
             pl.BlockSpec(memory_space=pltpu.VMEM),
         ]
         + [anywhere] * 3,
-        out_specs=[anywhere] * 5,
+        out_specs=[anywhere] * 4,
         out_shape=[
             shape((half, hidden), table.dtype),
             shape((half, hidden), table.dtype),
             shape((shards, *fact.shape), fact.dtype),
             shape((shards, *chunk.shape), chunk.dtype),
-            shape((hidden, count), BF),
         ],
         scratch_shapes=[
             pltpu.VMEM((table.shape[0] // GROUP, GROUP, hidden), BF),
             pltpu.VMEM((PICK, GROUP, hidden), BF),
             pltpu.VMEM((2 * half, hidden), BF),
-            pltpu.VMEM((hidden, count), BF),
             sems((half // PICK,)),
             sems((half // PICK,)),
             sems((2,)),
-            sems((5,)),
+            sems((4,)),
             *gather_sems(streams),
         ],
         compiler_params=params(collective_id=1, has_side_effects=True),
@@ -1135,11 +1099,11 @@
 
 def first_layer_body(
     streams, shards,
-    own_any, got_any, first_any, other_any, chunk, code_ref, spots_ref, gain_ref, shift_ref, down_ref,
+    own_any, got_any, first_any, other_any, chunk, table_any, code_ref, spots_ref, gain_ref, shift_ref, down_ref,
     adapt_ref, bias_ref, seg_ref, seg_row_ref,
-    qkv_out, x_out, one_out, two_out, slope_out, wo_out, full_chunk, mid_ref, log_ref,
+    qkv_out, x_out, one_out, two_out, slope_out, wo_out, full_chunk, et_out, mid_ref, log_ref,
     own, got, in_slab, w, wo, up, dn, x, qkv, ctx, two, out, slope,
-    load_sems, tile_sems, out_sems, cross, sends, receives, hands, hands_got,
+    e_in, et_stage, load_sems, tile_sems, out_sems, e_sems, et_sems, sends, receives, hands, hands_got,
 ):
     here = position()
     me = number_of(here)
@@ -1172,32 +1136,66 @@
     for copy in loads:
         copy.start()
     barrier = pltpu.get_barrier_semaphore()
-    peers = [dict(here, c=1 - here["c"])]
-    for core in (here["c"], 1 - here["c"]):
-        there = dict(here, c=core)
-        peers += [dict(there, x=1 - here["x"]), dict(there, y=1 - here["y"])]
-        peers += [dict(there, z=flip(here["z"], k)) for k in (1, 2, 3)]
+    peers = [
+        dict(here, c=1 - here["c"]),
+        dict(here, x=1 - here["x"]),
+        dict(here, y=1 - here["y"]),
+        *[dict(here, z=flip(here["z"], k)) for k in (1, 2, 3)],
+    ]
     for peer in peers:
         pl.semaphore_signal(barrier, inc=1, device_id=device_of(peer), device_id_type=MESH)
     pl.semaphore_wait(barrier, len(peers))
     gathers = [
         Gather(
-            chunk, full_chunk, start, size, order, sends.at[k], receives.at[k], hands.at[k], hands_got.at[k],
-            cross.at[k],
+            chunk, full_chunk, start, size, order, sends.at[k], receives.at[k], hands.at[k], hands_got.at[k]
         )
         for k, (start, size, order) in enumerate(streams)
     ]
-    def advance(*ranges):
-        pairs_of = [(0, ranges[0]), (1, ranges[0])] + [(2, r) for r in ranges[1:]]
-        for k, (first, last) in pairs_of:
-            for index in range(first, last + 1):
-                gathers[k].step(index)
+    def advance(first, last):
+        for index in range(first, last + 1):
+            for gather in gathers:
+                gather.step(index)
 
     def at(i, plan):
-        for k, ranges in plan.items():
-            pl.when(i == k)(functools.partial(advance, *ranges))
-
-    advance((0, 0), (0, 0))
+        for k, ends in plan.items():
+            pl.when(i == k)(functools.partial(advance, *ends))
+
+    advance(0, 0)
+
+    groups = pairs + tiles
+    size = e_in.shape[1]
+    here_rows = (here["y"] * 2 + here["c"]) * (groups * size)
+    unit = (
+        (lax.broadcasted_iota(jnp.int32, (256, 256), 0) == lax.broadcasted_iota(jnp.int32, (256, 256), 1))
+        .astype(F32)
+        .astype(BF)
+    )
+
+    def group_in(g):
+        source = table_any.at[pl.ds(pl.multiple_of(here_rows + g * size, 16), size), :]
+        return pltpu.make_async_copy(source, e_in.at[g % 2], e_sems.at[g])
+
+    def group_out(g):
+        target = et_out.at[:, pl.ds(pl.multiple_of(g * size, 128), size)]
+        return pltpu.make_async_copy(et_stage.at[g % 2], target, et_sems.at[g])
+
+    def turn_group(g):
+        group_in(g).wait()
+
+        @pl.when(g >= 2)
+        def _():
+            group_out(g - 2).wait()
+
+        for k in range(0, hidden, 256):
+            et_stage[g % 2, k : k + 256, :] = mm_nt(unit, e_in[g % 2, :, k : k + 256]).astype(BF)
+        group_out(g).start()
+
+        @pl.when(g + 2 < groups)
+        def _():
+            group_in(g + 2).start()
+
+    group_in(0).start()
+    group_in(1).start()
     for copy in loads[:3]:
         copy.wait()
     unpack_rows(in_slab, (w, wo))
@@ -1210,7 +1208,7 @@
             adapt_ref, bias_ref, qkv.at[part, :], mid_ref.at[part, :], x.at[part, :],
         )
 
-        at(i, {tiles - 3: ((1, 3), (1, 3)), tiles - 1: ((4, 5),)})
+        at(i, {tiles - 3: (1, 3), tiles - 1: (4, 5)})
 
     early = [
         pltpu.make_async_copy(qkv, qkv_out, out_sems.at[0]),
@@ -1227,17 +1225,8 @@
             ctx.at[:, column(0)], log_ref.at[pl.ds(p, 1)],
         )
 
-        at(
-            p - (pairs - 6),
-            {
-                0: ((1, 0), (4, 11)),
-                1: ((6, 7),),
-                2: ((14, 15),),
-                3: ((8, 9),),
-                4: ((16, 17), (12, 19)),
-                5: ((10, 11),),
-            },
-        )
+        turn_group(p)
+        at(p - (pairs - 6), {1: (6, 7), 3: (8, 9), 5: (10, 13)})
 
     for copy in loads[3:6]:
         copy.wait()
@@ -1257,7 +1246,7 @@
             )
         ]
 
-    plan = {0: ((12, 13),), 1: ((18, 21), (20, 27)), 2: ((22, 25),), 3: ((26, 27),)}
+    plan = {0: (14, 16), 1: (17, 19), 2: (20, 23), 3: (24, 27)}
 
     @pl.loop(0, tiles)
     def _(i):
@@ -1275,6 +1264,7 @@
         )
         for copy in tile_copies(i):
             copy.start()
+        turn_group(pairs + i)
         at(i - (tiles - 4), plan)
 
     for gather in gathers:
@@ -1282,11 +1272,11 @@
     for i in (tiles - 2, tiles - 1):
         for copy in tile_copies(i):
             copy.wait()
-    for copy in early + loads[6:]:
+    for copy in early + loads[6:] + [group_out(g) for g in (groups - 2, groups - 1)]:
         copy.wait()
 
 
-def first_layer(own, got, first, other, chunk, more, shards):
+def first_layer(own, got, first, other, chunk, table, more, shards):
     whole = pl.BlockSpec(memory_space=pltpu.VMEM)
     anywhere = pl.BlockSpec(memory_space=pl.ANY)
     down, seg_row = more[4], more[-1]
@@ -1295,13 +1285,14 @@
     pairs = HEADS // 2
     units = 4 * hidden
     each = units // shards
+    count, groups = table.shape[0] // 4, pairs + rows // tile
     shape = jax.ShapeDtypeStruct
     sems = pltpu.SemaphoreType.DMA
     streams = streams_of(chunk.shape[0], (("zxy", 0.4), ("zyx", 0.4), ("xyz", 0.2)))
     return pl.pallas_call(
         functools.partial(first_layer_body, streams, shards),
-        in_specs=[anywhere] * 5 + [whole] * len(more),
-        out_specs=[anywhere] * 7 + [whole] * 2,
+        in_specs=[anywhere] * 6 + [whole] * len(more),
+        out_specs=[anywhere] * 8 + [whole] * 2,
         out_shape=[
             shape((rows, 3 * hidden), BF),
             shape((rows, hidden), F32),
@@ -1310,6 +1301,7 @@
             shape((rows, units), BF),
             shape((hidden, hidden), BF),
             shape((shards, *chunk.shape), BF),
+            shape((hidden, count), BF),
             shape((rows, down.shape[2]), BF),
             shape((pairs, 1, 2 * rows), F32),
         ],
@@ -1327,15 +1319,18 @@
             pltpu.VMEM((2, tile, hidden), F32),
             pltpu.VMEM((2, tile, hidden), F32),
             pltpu.VMEM((2, tile, units), BF),
+            pltpu.VMEM((2, count // groups, hidden), BF),
+            pltpu.VMEM((2, hidden, count // groups), BF),
             sems((7,)),
             sems((4, rows // tile)),
             sems((2,)),
-            sems((len(streams), 4)),
+            sems((groups,)),
+            sems((groups,)),
             *gather_sems(streams),
         ],
         compiler_params=params(collective_id=3, has_side_effects=True),
         name="first_layer",
-    )(own, got, first, other, chunk, *more)
+    )(own, got, first, other, chunk, table, *more)
 
 
 def adam(weight, gradient, moment_one, moment_two, fade_one, fade_two):
@@ -1896,7 +1891,7 @@
         )
         fact = jnp.concatenate([vocabulary_bias, ups, sequence_task_index.astype(F32)])
         fact_rows = -(-fact.size // 1024) * 8
-        got, own_rows, facts, first_full, own_turned = start_exchange(
+        got, own_rows, facts, first_full = start_exchange(
             pair_ids,
             embed,
             jnp.pad(fact, (0, fact_rows * 128 - fact.size)).reshape(fact_rows, 128),
@@ -1969,8 +1964,8 @@
         more = (
             code, position_embedding, gains, shifts, downs, adapters, layer_bias_vector, seg_wide, seg_row,
         )
-        qkv, x_last, one, two, slope, out_first, last_full, mid, logs = first_layer(
-            own_rows, got, first_full, other_full, last_chunk, more, shards
+        qkv, x_last, one, two, slope, out_first, last_full, own_turned, mid, logs = first_layer(
+            own_rows, got, first_full, other_full, last_chunk, embed, more, shards
         )
         slabs = [None, slabs_of(last_full, last_dn)]
         *saved, in_last, out_last, head_full = last_forward(

time: 410 us -> 406 us (level)
  no operation moved by 1% of the time
where the time goes in v4:
time: 406 us; the launch traced here: 398 us
  Pallas kernels  354 us (87%)
  between operations  16.1 us (4%)
  local copies, waits for them, and re-layouts  14.7 us (4%)
  other arithmetic  8.06 us (2%)
  blocking collectives  5.23 us (1%)
    pallas_call x1, Pallas kernels, start_exchange(): pl.pallas_call(functools.partial(start_body, streams, shards), in_specs=[...  105 us
    pallas_call x1, Pallas kernels, first_layer(): pl.pallas_call(functools.partial(first_layer_body, streams, shards), in_s...  101 us
    pallas_call x1, Pallas kernels, finish(): pl.pallas_call(functools.partial(finish_body, shards, edge), in_specs=[an...  55.7 us
    pallas_call x1, Pallas kernels, head(): pl.pallas_call(head_body, in_specs=[whole] * 2 + [anywhere] * 2, out_spec...  44.8 us
    pallas_call x1, Pallas kernels, last_backward(): pl.pallas_call(functools.partial(last_backward_body, places=(up[1], dn[1]...  25.6 us
    pallas_call x1, Pallas kernels, last_forward(): pl.pallas_call(body, in_specs=[whole] * 7 + [anywhere] * (len(weights) +...  20.5 us
  transfers between devices with their start and end apart: 2, of which 0 were waited for; matrix products, arithmetic and copies ran while one was open for 5% of the time, Pallas kernels for 52%

profile of v4, /device:TPU:0, one launch (start us, length us, event | category | flops | bytes accessed | tf_op | source)
XLA Modules:
  0.0 398.4 jit_solution(4185908870523887211)
XLA Ops:
  7.2 0.0 copy-start.4
  7.2 0.0 all-gather.7.cloned.1.call-start
  7.2 0.8 slice_bitcast_fusion.7
  8.0 0.9 slice_bitcast_fusion.5
  9.0 1.0 slice_bitcast_fusion.3
  10.0 0.0 copy-start
  10.0 0.7 pad_maximum_fusion.3
  10.7 0.0 all-gather.7.cloned.1.call-update
  10.7 0.0 all-gather.9.cloned.1.call-start
  11.4 0.1 reshape.263
  11.6 5.2 %all-gather.3 = s32[2,1,1152]{2,1,0:T(1,128)S(1)} all-gather(s32[1,1,1152]{2,1,0:T(1,128)S(1)} %reshape.294), channel_id=2, replica_groups=mesh['dp'=2,'fsdp'=16] {'dp'}, dimensions={0}, use_global_device_ids=true | all-gather | bytes 13824 | tf_op jit(solution)/shard_map/all_gather | solution.py:1877
  16.8 0.1 dynamic-slice_reduce_fusion.1
  16.9 0.5 copy.63
  17.4 0.4 copy.60
  17.9 0.1 concatenate.80
  18.0 0.6 pad_bitcast_fusion.2.fact
  18.6 0.6 add_select_fusion.2.ids
  19.2 0.7 pad_maximum_fusion.2.chunk
  19.9 1.6 fusion.1.low_ref
  21.5 105.0 %start_exchange.1 = (bf16[1152,768]{1,0:T(8,128)(2,1)}, bf16[1152,768]{1,0:T(8,128)(2,1)}, f32[32,24,128]{2,1,0:T(8,128)}, bf16[32,144,768]{2,1,0:T(8,128)(2,1)}) custom-call(s32[2304]{0:T(1024)} %add_select_fusion.2.ids, s32[2304,1]{1,0:T(8,128)} %fusion.1.low_ref, bf16[1600,16,768]{2,1,0:T(8,128)(2,1)} %bitcast.99, f32[24,128]{1,0:T(8,128)} %pad_bitcast_fusion.2.fact, ...), custom_call_target="tpu_custom_call" | custom-call | tf_op jit(solution)/shard_map/start_exchange/pallas_call | solution.py:1071
  126.5 0.0 copy-start.10
  126.6 0.7 slice_bitcast_fusion
  127.2 0.0 all-gather.9.cloned.1.call-update
  127.3 1.1 copy.90
  128.4 0.1 slice.158
  129.2 0.1 pad.51.clone
  129.3 0.1 pad.48.clone
  129.4 0.6 broadcast_in_dim.55.refs_12_
  130.0 0.1 compare_reduce_fusion
  130.1 0.1 add_select_fusion.3
  130.2 0.3 reduce-window.9
  130.5 0.1 slice.104
  130.6 0.2 copy.64
  130.8 0.2 copy.65
  131.0 0.1 slice_reduce_fusion
  131.1 0.1 fusion.34
  131.2 1.1 broadcast_in_dim.58.code_ref
  132.2 0.1 slice_convert_fusion.1
  132.3 0.1 copy.88
  132.4 0.1 reshape.269
  132.5 0.4 reshape.267
  132.9 0.1 copy.66
  133.0 0.3 reshape.268
  133.4 1.1 gather_fusion
  134.5 0.1 convert_reduce_fusion
  134.7 0.6 fusion.35
  135.3 0.6 pad.40
  135.9 0.6 concatenate.94.fact_ref
  136.5 0.7 dynamic-slice_bitcast_fusion.bias_ref
  137.3 0.1 pad_bitcast_fusion
  137.4 0.8 fusion.26.chunk
  138.2 0.8 pad_maximum_fusion.1.down_ref.refs_4_
  139.0 0.1 fusion.23
  139.1 0.1 fusion.19
  139.2 1.1 pad_maximum_fusion.adapt_ref.refs_5_
  140.3 1.0 broadcast_in_dim.52.seg_ref.refs_3_
  141.3 100.9 %first_layer.1 = (bf16[1024,2304]{1,0:T(8,128)(2,1)}, f32[1024,768]{1,0:T(8,128)}, f32[1024,768]{1,0:T(8,128)}, f32[1024,768]{1,0:T(8,128)}, bf16[1024,3072]{1,0...) custom-call(bf16[1152,768]{1,0:T(8,128)(2,1)} %get-tuple-element.55., ...), custom_call_target="tpu_custom_call" | custom-call | tf_op jit(solution)/shard_map/first_layer/pallas_call | solution.py:1292
  242.2 0.0 all-gather.9.cloned.1.call-done
  242.3 0.7 broadcast_in_dim.54.refs_1_.place_ref
  243.0 20.5 %last_forward.1 = (bf16[1024,1536]{1,0:T(8,128)(2,1)}, bf16[128,768]{1,0:T(8,128)(2,1)}, bf16[1024,128]{1,0:T(8,128)(2,1)}, f32[6,256]{1,0:T(8,128)}, f32[128,76...) custom-call(f32[1024,768]{1,0:T(8,128)} %get-tuple-element.60.refs_0, ...), custom_call_target="tpu_custom_call" | custom-call | tf_op jit(solution)/shard_map/last_forward/pallas_call | solution.py:461
  263.5 44.8 %head.1 = (f32[768,128]{1,0:T(8,128)}, f32[1,128]{1,0:T(1,128)}) custom-call(bf16[128,768]{1,0:T(8,128)(2,1)} %get-tuple-element.63.u_ref.feat_ref, f32[50,128]{1,0:T(8,128)} %dynamic-slice_bitcast_fusion.bias_ref, bf16[25600,768]{1,0:T(8,128)(2,1)} %table_any.3, bf16[768,6400]{1,0:T(8,128)(2,1)} %get-tuple-element.64.et_any), custom_call_target="tpu_custom_call" | custom-call | tf_op jit(solution)/shard_map/head/pallas_call | solution.py:1783
  308.3 25.6 %last_backward.1 = (f32[1024,768]{1,0:T(8,128)}, bf16[32,32,768]{2,1,0:T(8,128)(2,1)}, f32[768,128]{1,0:T(8,128)}, f32[8,128]{1,0:T(8,128)}) custom-call(bf16[1152,768]{1,0:T(8,128)(2,1)} %get-tuple-element.55.own_any, bf16[1152,768]{1,0:T(8,128)(2,1)} %get-tuple-element.56.got_any, f32[768,128]{1,0:T(8,128)} %get-tuple-element.65.mean_ref, ...), custom_call_target="tpu_custom_call" | custom-call | tf_op jit(solution)/shard_map/last_backward/pallas_call | solution.py:672
  333.9 55.7 %finish.1 = (f32[8,128]{1,0:T(8,128)}, f32[24,768]{1,0:T(8,128)}, f32[24,128]{1,0:T(8,128)}) custom-call(f32[1024,768]{1,0:T(8,128)} %get-tuple-element.80.dout_any, f32[1024,768]{1,0:T(8,128)} %get-tuple-element.81.one_any, f32[1024,768]{1,0:T(8,128)} %get-tuple-element.82.two_any, bf16[1024,3072]{1,0:T(8,128)(2,1)} %get-tuple-element.83.slope_any, ...), custom_call_target="tpu_custom_call" | custom-call | tf_op jit(solution)/shard_map/finish/pallas_call | solution.py:1543
  389.6 1.8 update.1
  (47 shorter events, 0.3 us)
Async XLA Ops:
  7.2 4.3 %copy-start.4 = (f32[2,2,8,24]{3,2,1,0:T(8,128)S(1)}, f32[2,2,8,24]{3,2,1,0:T(8,128)}, u32[]{:S(2)}) copy-start(f32[2,2,8,24]{3,2,1,0:T(8,128)} %adapt_w.1) | copy-start | bytes 9220
  7.2 4.3 %copy-start.11 = (s32[1,128]{1,0:T(1,128)S(1)}, s32[1,128]{1,0:T(1,128)}, u32[]{:S(2)}) copy-start(s32[1,128]{1,0:T(1,128)} %param.28) | copy-start | bytes 1540
  7.2 4.3 %copy-start.9 = (s32[1,1024]{1,0:T(1,128)S(1)}, s32[1,1024]{1,0:T(1,128)}, u32[]{:S(2)}) copy-start(s32[1,1024]{1,0:T(1,128)} %param.25) | copy-start | bytes 12292
  7.2 133.1 %all-gather.7.cloned.1.call-start = ((), (), s32[]{:S(2)}) async-start(), calls=%async_computation | async-start | bytes 7299072 | tf_op jit(solution)/shard_map/all_gather | solution.py:1866
  9.9 7.9 %copy-start.7 = (f32[1600]{0:T(1024)S(1)}, f32[1600]{0:T(1024)}, u32[]{:S(2)}) copy-start(f32[1600]{0:T(1024)} %param.42) | copy-start | bytes 19204
  10.0 9.2 %copy-start = (bf16[2,768,96]{1,2,0:T(8,128)(2,1)S(1)}, bf16[2,768,96]{1,2,0:T(8,128)(2,1)}, u32[]{:S(2)}) copy-start(bf16[2,768,96]{1,2,0:T(8,128)(2,1)} %param.38) | copy-start | bytes 884740
  10.7 231.5 %all-gather.9.cloned.1.call-start = ((), (), s32[]{:S(2)}) async-start(), calls=%async_computation.1 | async-start | bytes 4866048 | tf_op jit(solution)/shard_map/all_gather | solution.py:1961
  21.5 105.0 %copy-start.1 = (bf16[2,96,768]{2,1,0:T(8,128)(2,1)S(1)}, bf16[2,96,768]{2,1,0:T(8,128)(2,1)}, u32[]{:S(2)}) copy-start(bf16[2,96,768]{2,1,0:T(8,128)(2,1)} %param.39) | copy-start | bytes 884740
  126.5 2.9 copy-start.10
  126.5 3.4 copy-start.6
  126.6 4.0 %copy-start.2 = (f32[24,768]{1,0:T(8,128)S(1)}, f32[24,768]{1,0:T(8,128)}, u32[]{:S(2)}) copy-start(f32[24,768]{1,0:T(8,128)} %head_w.1) | copy-start | bytes 221188
  126.6 4.0 %copy-start.5 = (bf16[2,2,768,8]{2,3,1,0:T(8,128)(2,1)S(1)}, bf16[2,2,768,8]{2,3,1,0:T(8,128)(2,1)}, u32[]{:S(2)}) copy-start(bf16[2,2,768,8]{2,3,1,0:T(8,128)(2,1)} %param.43) | copy-start | bytes 147460
  130.0 10.4 %copy-start.3 = (f32[1,1024]{1,0:T(1,128)}, f32[1,1024]{1,0:T(1,128)S(1)}, u32[]{:S(2)}) copy-start(f32[1,1024]{1,0:T(1,128)S(1)} %convert_element_type.56.seg_row_ref) | copy-start | bytes 12292
  132.2 2.4 copy-start.12
  141.3 100.9 %copy-start.8 = (s32[1,128]{1,0:T(1,128)S(1)}, s32[1,128]{1,0:T(1,128)}, u32[]{:S(2)}) copy-start(s32[1,128]{1,0:T(1,128)} %place_row_ref.1) | copy-start | bytes 1540
Sparse Core Ops, SparseCore 0:
  10.9 98.2 all-gather.6
  127.4 76.9 all-gather.8

commit v5 on v4

--- a/solution.py
+++ b/solution.py
@@ -1023,7 +1023,7 @@
     fill.wait()
     picked = 0
     for index in range(1, ITEMS):
-        while picked < min(2 * batches, 6 + 4 * index):
+        while picked < min(2 * batches, 2 + 3 * index):
             pick(picked)
             picked += 1
         for gather in gathers:
@@ -1099,7 +1099,7 @@
 
 def first_layer_body(
     streams, shards,
-    own_any, got_any, first_any, other_any, chunk, table_any, code_ref, spots_ref, gain_ref, shift_ref, down_ref,
+    own_any, got_any, first_any, chunk, table_any, code_ref, spots_ref, gain_ref, shift_ref, down_ref,
     adapt_ref, bias_ref, seg_ref, seg_row_ref,
     qkv_out, x_out, one_out, two_out, slope_out, wo_out, full_chunk, et_out, mid_ref, log_ref,
     own, got, in_slab, w, wo, up, dn, x, qkv, ctx, two, out, slope,
@@ -1113,9 +1113,6 @@
     lanes = 2 * (hidden // HEADS)
     pairs = hidden // lanes
 
-    rest = first_any.shape[1] - up.shape[1]
-    cut = dn.shape[1] - rest
-
     def slab(source, target, start):
         return source.at[:, pl.ds(start, target.shape[1]), :]
 
@@ -1125,10 +1122,9 @@
             (
                 (own_any.at[pl.ds(0, rows), :], own),
                 (got_any.at[pl.ds(0, rows), :], got),
-                (slab(other_any, in_slab, cut), in_slab),
+                (slab(first_any, in_slab, 2 * up.shape[1]), in_slab),
                 (slab(first_any, up, 0), up),
-                (other_any.at[:, pl.ds(0, cut), :], dn.at[:, pl.ds(0, cut), :]),
-                (first_any.at[:, pl.ds(up.shape[1], rest), :], dn.at[:, pl.ds(cut, rest), :]),
+                (slab(first_any, dn, up.shape[1]), dn),
                 (chunk, full_chunk.at[me]),
             )
         )
@@ -1228,7 +1224,7 @@
         turn_group(p)
         at(p - (pairs - 6), {1: (6, 7), 3: (8, 9), 5: (10, 13)})
 
-    for copy in loads[3:6]:
+    for copy in loads[3:5]:
         copy.wait()
 
     def tile_copies(i):
@@ -1272,11 +1268,11 @@
     for i in (tiles - 2, tiles - 1):
         for copy in tile_copies(i):
             copy.wait()
-    for copy in early + loads[6:] + [group_out(g) for g in (groups - 2, groups - 1)]:
+    for copy in early + loads[5:] + [group_out(g) for g in (groups - 2, groups - 1)]:
         copy.wait()
 
 
-def first_layer(own, got, first, other, chunk, table, more, shards):
+def first_layer(own, got, first, chunk, table, more, shards):
     whole = pl.BlockSpec(memory_space=pltpu.VMEM)
     anywhere = pl.BlockSpec(memory_space=pl.ANY)
     down, seg_row = more[4], more[-1]
@@ -1291,7 +1287,7 @@
     streams = streams_of(chunk.shape[0], (("zxy", 0.4), ("zyx", 0.4), ("xyz", 0.2)))
     return pl.pallas_call(
         functools.partial(first_layer_body, streams, shards),
-        in_specs=[anywhere] * 6 + [whole] * len(more),
+        in_specs=[anywhere] * 5 + [whole] * len(more),
         out_specs=[anywhere] * 8 + [whole] * 2,
         out_shape=[
             shape((rows, 3 * hidden), BF),
@@ -1321,7 +1317,7 @@
             pltpu.VMEM((2, tile, units), BF),
             pltpu.VMEM((2, count // groups, hidden), BF),
             pltpu.VMEM((2, hidden, count // groups), BF),
-            sems((7,)),
+            sems((6,)),
             sems((4, rows // tile)),
             sems((2,)),
             sems((groups,)),
@@ -1330,7 +1326,7 @@
         ],
         compiler_params=params(collective_id=3, has_side_effects=True),
         name="first_layer",
-    )(own, got, first, other, chunk, table, *more)
+    )(own, got, first, chunk, table, *more)
 
 
 def adam(weight, gradient, moment_one, moment_two, fade_one, fade_two):
@@ -1347,7 +1343,7 @@
 
 def finish_body(
     shards, edge,
-    dout_any, one_any, two_any, slope_any, wo_any, first_any, other_any, qkv_any, gain_ref, log_ref, seg_ref,
+    dout_any, one_any, two_any, slope_any, wo_any, first_any, qkv_any, gain_ref, log_ref, seg_ref,
     seg_row_ref, mid_ref, parts, late_ref, facts,
     sums_ref, dense_ref, total_ref,
     dout, one, two, slope, wo, up, dn, qkv, dctx, dv, grad, core_got, chip_sum, dense_got, grad_got, note, notes,
@@ -1368,8 +1364,6 @@
         ]
 
     here = position()
-    rest = first_any.shape[1] - up.shape[1]
-    cut = dn.shape[1] - rest
     chips = shards // 2
     chip, core = me // 2, here["c"]
     to_core = pltpu.make_async_remote_copy(
@@ -1396,22 +1390,21 @@
         pltpu.make_async_copy(source, target, load_sems.at[k])
         for k, (source, target) in enumerate(
             (
-                (other_any.at[:, pl.ds(0, cut), :], dn.at[:, pl.ds(0, cut), :]),
-                (first_any.at[:, pl.ds(up.shape[1], rest), :], dn.at[:, pl.ds(cut, rest), :]),
+                (first_any.at[:, pl.ds(up.shape[1], dn.shape[1]), :], dn),
                 (first_any.at[:, pl.ds(0, up.shape[1]), :], up),
                 (wo_any, wo),
                 (qkv_any, qkv),
             )
         )
     ]
-    for copy in tile_loads(0) + loads[:4]:
+    for copy in tile_loads(0) + loads[:3]:
         copy.start()
     for i in range(1, tiles):
         for copy in tile_loads(i):
             copy.start()
-    loads[4].start()
+    loads[3].start()
     greet_all(shards)
-    for copy in loads[:4]:
+    for copy in loads[:3]:
         copy.wait()
 
     @pl.loop(0, tiles)
@@ -1443,7 +1436,7 @@
             def _(k):
                 to_chip(k).start()
 
-    loads[4].wait()
+    loads[3].wait()
     lanes = 2 * (hidden // HEADS)
     pairs = hidden // lanes
 
@@ -1530,7 +1523,7 @@
 
 
 def finish(back, qkv, logs, seg_wide, seg_row, mid, parts, late, facts, edge, shards):
-    dout, one, two, slope, wo, first, other, gains = back
+    dout, one, two, slope, wo, first, gains = back
     slab = pltpu.VMEM((shards, slope.shape[1] // shards, dout.shape[1]), BF)
     parts = parts.reshape(-1, 2, *parts.shape[1:])
     rows, hidden = dout.shape
@@ -1542,7 +1535,7 @@
     tiles = rows // split_of(rows, BACK_TILE, 16)
     return pl.pallas_call(
         functools.partial(finish_body, shards, edge),
-        in_specs=[anywhere] * 8 + [whole] * 8,
+        in_specs=[anywhere] * 7 + [whole] * 8,
         out_specs=[whole] * 3,
         out_shape=[
             shape((8, 128), F32),
@@ -1568,7 +1561,7 @@
             pltpu.VMEM((8, 128), F32),
             pltpu.VMEM((shards, 8, 128), F32),
             sems((4, tiles)),
-            sems((5,)),
+            sems((4,)),
             sems((2,)),
             sems((2,)),
             sems((2,)),
@@ -1576,7 +1569,7 @@
         ],
         compiler_params=params(collective_id=2, has_side_effects=True),
         name="finish",
-    )(dout, one, two, slope, wo, first, other, qkv, gains, logs, seg_wide, seg_row, mid, parts, late, facts)
+    )(dout, one, two, slope, wo, first, qkv, gains, logs, seg_wide, seg_row, mid, parts, late, facts)
 
 
 LOG_ROWS = 16
@@ -1861,11 +1854,7 @@
     grouped = (lax.axis_size("dp"), lax.axis_size("fsdp")) == (2, 16)
     feeds = [[feedforward_up[layer].T, feedforward_down[layer]] for layer in range(layers)]
     attends = [[attention_in_weight[layer].T, attention_out_weight[layer].T] for layer in range(layers)]
-    cut = ff_rows // 32 * 16
-    first_chunk = jnp.concatenate([feeds[0][0], feeds[0][1][cut:]], 0)
-    other_full = lax.all_gather(
-        jnp.concatenate([feeds[0][1][:cut], *attends[0]], 0), BOTH, axis=0, tiled=False
-    )
+    first_chunk = jnp.concatenate(feeds[0] + attends[0], 0)
     last_chunk = pad_rows(
         jnp.concatenate([feeds[1][0], *attends[1], head_projection.astype(BF)], 0), 32
     )
@@ -1965,7 +1954,7 @@
             code, position_embedding, gains, shifts, downs, adapters, layer_bias_vector, seg_wide, seg_row,
         )
         qkv, x_last, one, two, slope, out_first, last_full, own_turned, mid, logs = first_layer(
-            own_rows, got, first_full, other_full, last_chunk, embed, more, shards
+            own_rows, got, first_full, last_chunk, embed, more, shards
         )
         slabs = [None, slabs_of(last_full, last_dn)]
         *saved, in_last, out_last, head_full = last_forward(
@@ -1980,11 +1969,13 @@
     else:
         first_full = lax.all_gather(first_chunk, BOTH, axis=0, tiled=False)
         last_full = lax.all_gather(last_chunk, BOTH, axis=0, tiled=False)
-        dn_full = jnp.concatenate([other_full[:, :cut], first_full[:, ff_rows:]], 1)
-        slabs = [slabs_of(first_full[:, :ff_rows], dn_full), slabs_of(last_full, last_dn)]
+        slabs = [
+            (slab_of(first_full, 0, ff_rows), slab_of(first_full, ff_rows, ff_rows)),
+            slabs_of(last_full, last_dn),
+        ]
         taken = lambda full_chunk, start, size: full_chunk[:, start : start + size].reshape(-1, hidden)
-        in_first = taken(other_full, cut, qkv_rows)
-        out_first = taken(other_full, cut + qkv_rows, out_rows)
+        in_first = taken(first_full, 2 * ff_rows, qkv_rows)
+        out_first = taken(first_full, 2 * ff_rows + qkv_rows, out_rows)
         in_last = taken(last_full, in_start, qkv_rows)
         out_last = taken(last_full, in_start + qkv_rows, out_rows)
         head_full = taken(last_full, in_start + qkv_rows + out_rows, head_rows)
@@ -2050,7 +2041,7 @@
     heads = (head_projection, head_moment_first, head_moment_second)
     if grouped:
         sums, dense_portion, adapter_portion = finish(
-            (*back, first_full, other_full, gains), qkv, logs, seg_wide, seg_row, mid, dense_gradient, late, facts, rank, shards
+            (*back, first_full, gains), qkv, logs, seg_wide, seg_row, mid, dense_gradient, late, facts, rank, shards
         )
         loss, norm, *new = update(sums, dense_portion, adapter_portion, facts, heads, adapts)
         return (loss[0, 0], norm[0, 0], *new[3:], *new[:3])

time: 406 us -> 393 us (0.968)
  Pallas kernels: 354 us -> 343 us
    pallas_call x1, Pallas kernels: 105 us -> 96.3 us  [start_exchange(): pl.pallas_call(functools.partial(start_body, streams, shards), in_specs=[...]
  transfers between devices with their start and end apart: 2 -> 1, of which waited for: 0 -> 0; matrix products, arithmetic and copies ran while one was open for 5% -> 3% of each run, Pallas kernels for 52% -> 25%
where the time goes in v5:
time: 393 us; the launch traced here: 387 us
  Pallas kernels  343 us (87%)
  between operations  16.1 us (4%)
  local copies, waits for them, and re-layouts  15.2 us (4%)
  other arithmetic  8.18 us (2%)
  blocking collectives  5.23 us (1%)
    pallas_call x1, Pallas kernels, first_layer(): pl.pallas_call(functools.partial(first_layer_body, streams, shards), in_s...  97.5 us
    pallas_call x1, Pallas kernels, start_exchange(): pl.pallas_call(functools.partial(start_body, streams, shards), in_specs=[...  96.3 us
    pallas_call x1, Pallas kernels, finish(): pl.pallas_call(functools.partial(finish_body, shards, edge), in_specs=[an...  56.4 us
    pallas_call x1, Pallas kernels, head(): pl.pallas_call(head_body, in_specs=[whole] * 2 + [anywhere] * 2, out_spec...  44.5 us
    pallas_call x1, Pallas kernels, last_backward(): pl.pallas_call(functools.partial(last_backward_body, places=(up[1], dn[1]...  25.6 us
    pallas_call x1, Pallas kernels, last_forward(): pl.pallas_call(body, in_specs=[whole] * 7 + [anywhere] * (len(weights) +...  20.5 us
  transfers between devices with their start and end apart: 1, of which 0 were waited for; matrix products, arithmetic and copies ran while one was open for 3% of the time, Pallas kernels for 25%

profile of v5, /device:TPU:0, one launch (start us, length us, event | category | flops | bytes accessed | tf_op | source)
XLA Modules:
  0.0 387.3 jit_solution(13900630482278319918)
XLA Ops:
  7.2 0.0 all-gather.5.cloned.1.call-start
  8.0 0.8 reshape.261
  8.8 0.8 concatenate.77
  9.5 0.6 pad_bitcast_fusion.2.fact
  10.1 0.7 pad_add_fusion.2
  10.9 5.2 %all-gather.2 = s32[2,1,1152]{2,1,0:T(1,128)S(1)} all-gather(s32[1,1,1152]{2,1,0:T(1,128)S(1)} %reshape.291), channel_id=2, replica_groups=mesh['dp'=2,'fsdp'=16] {'dp'}, dimensions={0}, use_global_device_ids=true | all-gather | bytes 13824 | tf_op jit(solution)/shard_map/all_gather | solution.py:1866
  16.1 0.8 slice_bitcast_fusion.6
  16.9 1.0 slice_bitcast_fusion.4
  17.9 0.1 dynamic-slice_reduce_fusion.1
  18.0 0.5 copy.63
  18.5 0.7 slice_bitcast_fusion
  19.2 0.4 copy.60
  19.6 0.6 add_select_fusion.2.ids
  20.2 1.6 fusion.1.low_ref
  21.9 0.8 pad_maximum_fusion.1.chunk
  22.7 96.3 %start_exchange.1 = (bf16[1152,768]{1,0:T(8,128)(2,1)}, bf16[1152,768]{1,0:T(8,128)(2,1)}, f32[32,24,128]{2,1,0:T(8,128)}, bf16[32,288,768]{2,1,0:T(8,128)(2,1)}) custom-call(s32[2304]{0:T(1024)} %add_select_fusion.2.ids, s32[2304,1]{1,0:T(8,128)} %fusion.1.low_ref, bf16[1600,16,768]{2,1,0:T(8,128)(2,1)} %bitcast.96, f32[24,128]{1,0:T(8,128)} %pad_bitcast_fusion.2.fact, ...), custom_call_target="tpu_custom_call" | custom-call | tf_op jit(solution)/shard_map/start_exchange/pallas_call | solution.py:1071
  119.0 0.0 copy-start.7
  119.0 0.0 copy-start.5
  119.0 0.0 copy-start.2
  119.0 0.0 copy-start.4
  119.0 0.0 all-gather.5.cloned.1.call-update
  119.0 1.1 copy.90
  120.1 0.1 slice.142
  121.0 0.1 pad.51.clone
  121.1 0.1 pad.48.clone
  121.2 0.6 broadcast_in_dim.55.refs_12_
  121.7 0.0 copy-done.5
  121.8 0.1 compare_reduce_fusion
  121.9 0.1 add_select_fusion.3
  121.9 0.3 reduce-window.9
  122.2 0.1 slice.89
  122.4 0.2 copy.64
  122.6 0.2 copy.65
  122.7 0.0 copy-start.8
  122.7 0.1 slice_reduce_fusion
  122.8 0.1 fusion.34
  122.9 1.1 broadcast_in_dim.58.code_ref
  124.0 0.1 slice_convert_fusion.1
  124.1 0.1 copy.88
  124.2 0.1 reshape.267
  124.3 0.4 reshape.265
  124.7 0.1 copy.66
  124.8 0.3 reshape.266
  125.2 0.0 copy-done.8
  125.2 1.1 gather_fusion
  126.3 0.1 convert_reduce_fusion
  126.5 0.6 fusion.35
  127.1 0.6 pad.40
  127.7 0.6 concatenate.90.fact_ref
  128.4 0.1 pad_bitcast_fusion
  128.5 0.8 fusion.26.chunk
  129.3 0.8 pad_maximum_fusion.2.down_ref.refs_4_
  130.1 0.1 fusion.23
  130.2 0.1 fusion.19
  130.3 1.2 pad_maximum_fusion.adapt_ref.refs_5_
  131.5 1.0 broadcast_in_dim.52.seg_ref.refs_3_
  132.5 97.5 %first_layer.1 = (bf16[1024,2304]{1,0:T(8,128)(2,1)}, f32[1024,768]{1,0:T(8,128)}, f32[1024,768]{1,0:T(8,128)}, f32[1024,768]{1,0:T(8,128)}, bf16[1024,3072]{1,0...) custom-call(bf16[1152,768]{1,0:T(8,128)(2,1)} %get-tuple-element.55., ...), custom_call_target="tpu_custom_call" | custom-call | tf_op jit(solution)/shard_map/first_layer/pallas_call | solution.py:1288
  230.0 0.7 dynamic-slice_bitcast_fusion.bias_ref
  230.7 0.7 broadcast_in_dim.54.refs_1_.place_ref
  231.4 20.5 %last_forward.1 = (bf16[1024,1536]{1,0:T(8,128)(2,1)}, bf16[128,768]{1,0:T(8,128)(2,1)}, bf16[1024,128]{1,0:T(8,128)(2,1)}, f32[6,256]{1,0:T(8,128)}, f32[128,76...) custom-call(f32[1024,768]{1,0:T(8,128)} %get-tuple-element.60.refs_0, ...), custom_call_target="tpu_custom_call" | custom-call | tf_op jit(solution)/shard_map/last_forward/pallas_call | solution.py:461
  251.9 44.5 %head.1 = (f32[768,128]{1,0:T(8,128)}, f32[1,128]{1,0:T(1,128)}) custom-call(bf16[128,768]{1,0:T(8,128)(2,1)} %get-tuple-element.63.u_ref.feat_ref, f32[50,128]{1,0:T(8,128)} %dynamic-slice_bitcast_fusion.bias_ref, bf16[25600,768]{1,0:T(8,128)(2,1)} %table_any.3, bf16[768,6400]{1,0:T(8,128)(2,1)} %get-tuple-element.64.et_any), custom_call_target="tpu_custom_call" | custom-call | tf_op jit(solution)/shard_map/head/pallas_call | solution.py:1776
  296.5 25.6 %last_backward.1 = (f32[1024,768]{1,0:T(8,128)}, bf16[32,32,768]{2,1,0:T(8,128)(2,1)}, f32[768,128]{1,0:T(8,128)}, f32[8,128]{1,0:T(8,128)}) custom-call(bf16[1152,768]{1,0:T(8,128)(2,1)} %get-tuple-element.55.own_any, bf16[1152,768]{1,0:T(8,128)(2,1)} %get-tuple-element.56.got_any, f32[768,128]{1,0:T(8,128)} %get-tuple-element.65.mean_ref, ...), custom_call_target="tpu_custom_call" | custom-call | tf_op jit(solution)/shard_map/last_backward/pallas_call | solution.py:672
  322.1 56.4 %finish.1 = (f32[8,128]{1,0:T(8,128)}, f32[24,768]{1,0:T(8,128)}, f32[24,128]{1,0:T(8,128)}) custom-call(f32[1024,768]{1,0:T(8,128)} %get-tuple-element.80.dout_any, f32[1024,768]{1,0:T(8,128)} %get-tuple-element.81.one_any, f32[1024,768]{1,0:T(8,128)} %get-tuple-element.82.two_any, bf16[1024,3072]{1,0:T(8,128)(2,1)} %get-tuple-element.83.slope_any, ...), custom_call_target="tpu_custom_call" | custom-call | tf_op jit(solution)/shard_map/finish/pallas_call | solution.py:1536
  378.5 1.8 update.1
  (36 shorter events, 0.2 us)
Async XLA Ops:
  7.2 11.3 %copy-start = (bf16[2,768,96]{1,2,0:T(8,128)(2,1)S(1)}, bf16[2,768,96]{1,2,0:T(8,128)(2,1)}, u32[]{:S(2)}) copy-start(bf16[2,768,96]{1,2,0:T(8,128)(2,1)} %param.38) | copy-start | bytes 884740
  7.2 11.4 %copy-start.1 = (bf16[2,96,768]{2,1,0:T(8,128)(2,1)S(1)}, bf16[2,96,768]{2,1,0:T(8,128)(2,1)}, u32[]{:S(2)}) copy-start(bf16[2,96,768]{2,1,0:T(8,128)(2,1)} %param.39) | copy-start | bytes 884740
  7.2 223.5 %all-gather.5.cloned.1.call-start = ((), (), s32[]{:S(2)}) async-start(), calls=%async_computation | async-start | bytes 4866048 | tf_op jit(solution)/shard_map/all_gather | solution.py:1950
  119.0 2.2 copy-start.7
  119.0 2.8 copy-start.5
  119.0 3.3 copy-start.2
  119.0 3.4 copy-start.4
  121.7 9.7 %copy-start.3 = (f32[1,1024]{1,0:T(1,128)}, f32[1,1024]{1,0:T(1,128)S(1)}, u32[]{:S(2)}) copy-start(f32[1,1024]{1,0:T(1,128)S(1)} %convert_element_type.56.seg_row_ref) | copy-start | bytes 12292
  122.7 2.4 copy-start.8
  124.0 2.4 copy-start.9
  132.5 98.2 %copy-start.6 = (s32[1,128]{1,0:T(1,128)S(1)}, s32[1,128]{1,0:T(1,128)}, u32[]{:S(2)}) copy-start(s32[1,128]{1,0:T(1,128)} %place_row_ref.1) | copy-start | bytes 1540
Sparse Core Ops, SparseCore 0:
  119.1 73.5 all-gather.4

commit v6 on v5

--- a/solution.py
+++ b/solution.py
@@ -1856,9 +1856,8 @@
     attends = [[attention_in_weight[layer].T, attention_out_weight[layer].T] for layer in range(layers)]
     first_chunk = jnp.concatenate(feeds[0] + attends[0], 0)
     last_chunk = pad_rows(
-        jnp.concatenate([feeds[1][0], *attends[1], head_projection.astype(BF)], 0), 32
+        jnp.concatenate(feeds[1] + attends[1] + [head_projection.astype(BF)], 0), 32
     )
-    last_feed = feeds[1][1]
 
     table_rows = embed.shape[0]
     wanted = jnp.concatenate([input_token_index[0], label_target_token[0]])
@@ -1887,7 +1886,6 @@
             first_chunk,
             shards,
         )
-        facts, last_feed = lax.optimization_barrier((facts, last_feed))
         facts = facts.reshape(shards, -1)
         all_bias = facts[:, :slice_rows].reshape(-1)
         every_up = facts[:, slice_rows : slice_rows + ups.size]
@@ -1946,9 +1944,8 @@
 
     gains, shifts = norm_gain_vector, norm_bias_vector
     last_inputs = (place_col, place_row, seg_wide, downs, adapters, layer_bias_vector)
-    in_start = ff_rows
-    last_dn = lax.all_gather(last_feed, BOTH, axis=0, tiled=False)
-    slabs_of = lambda up_full, dn_full: (slab_of(up_full, 0, ff_rows), slab_of(dn_full, 0, ff_rows))
+    in_start = 2 * ff_rows
+    slabs_of = lambda full_chunk: (slab_of(full_chunk, 0, ff_rows), slab_of(full_chunk, ff_rows, ff_rows))
     if grouped:
         more = (
             code, position_embedding, gains, shifts, downs, adapters, layer_bias_vector, seg_wide, seg_row,
@@ -1956,7 +1953,7 @@
         qkv, x_last, one, two, slope, out_first, last_full, own_turned, mid, logs = first_layer(
             own_rows, got, first_full, last_chunk, embed, more, shards
         )
-        slabs = [None, slabs_of(last_full, last_dn)]
+        slabs = [None, slabs_of(last_full)]
         *saved, in_last, out_last, head_full = last_forward(
             x_last, *last_inputs, (last_full,), (in_start, in_start + qkv_rows + out_rows), *slabs[1], gains,
             shifts, head_dense_bias[None, :],
@@ -1969,10 +1966,7 @@
     else:
         first_full = lax.all_gather(first_chunk, BOTH, axis=0, tiled=False)
         last_full = lax.all_gather(last_chunk, BOTH, axis=0, tiled=False)
-        slabs = [
-            (slab_of(first_full, 0, ff_rows), slab_of(first_full, ff_rows, ff_rows)),
-            slabs_of(last_full, last_dn),
-        ]
+        slabs = [slabs_of(first_full), slabs_of(last_full)]
         taken = lambda full_chunk, start, size: full_chunk[:, start : start + size].reshape(-1, hidden)
         in_first = taken(first_full, 2 * ff_rows, qkv_rows)
         out_first = taken(first_full, 2 * ff_rows + qkv_rows, out_rows)

time: 393 us -> 387 us (0.985)
  between operations: 16.1 us -> 2.69 us
  transfers between devices with their start and end apart: 1 -> 0, of which waited for: 0 -> 0; matrix products, arithmetic and copies ran while one was open for 3% -> 0% of each run, Pallas kernels for 25% -> 0%
where the time goes in v6:
time: 387 us; the launch traced here: 380 us
  Pallas kernels  345 us (89%)
  local copies, waits for them, and re-layouts  17.3 us (4%)
  other arithmetic  9.48 us (2%)
  blocking collectives  5.23 us (1%)
    pallas_call x1, Pallas kernels, first_layer(): pl.pallas_call(functools.partial(first_layer_body, streams, shards), in_s...  101 us
    pallas_call x1, Pallas kernels, start_exchange(): pl.pallas_call(functools.partial(start_body, streams, shards), in_specs=[...  96.3 us
    pallas_call x1, Pallas kernels, finish(): pl.pallas_call(functools.partial(finish_body, shards, edge), in_specs=[an...  56 us
    pallas_call x1, Pallas kernels, head(): pl.pallas_call(head_body, in_specs=[whole] * 2 + [anywhere] * 2, out_spec...  44.5 us
    pallas_call x1, Pallas kernels, last_backward(): pl.pallas_call(functools.partial(last_backward_body, places=(up[1], dn[1]...  25.6 us
    pallas_call x1, Pallas kernels, last_forward(): pl.pallas_call(body, in_specs=[whole] * 7 + [anywhere] * (len(weights) +...  20.5 us

profile of v6, /device:TPU:0, one launch (start us, length us, event | category | flops | bytes accessed | tf_op | source)
XLA Modules:
  0.0 380.0 jit_solution(11657860443062184927)
XLA Ops:
  0.6 0.0 copy-start.1
  0.6 0.0 copy-start
  2.2 0.7 fusion.29
  2.9 0.1 pad.51.clone
  2.9 0.1 pad.48.clone
  3.0 0.9 compare_reduce_fusion
  3.9 0.1 add_select_fusion.3
  3.9 0.3 reduce-window.9
  4.2 1.3 broadcast_in_dim.55.refs_12_
  5.5 0.7 convert_element_type.56.seg_row_ref
  6.2 0.1 slice.90
  6.3 0.1 slice_reduce_fusion
  6.4 0.1 fusion.27
  6.5 0.8 reshape.261
  7.3 0.8 concatenate.77
  8.1 0.6 pad_bitcast_fusion.2.fact
  8.7 0.7 pad_add_fusion.2
  9.4 5.2 %all-gather.1 = s32[2,1,1152]{2,1,0:T(1,128)S(1)} all-gather(s32[1,1,1152]{2,1,0:T(1,128)S(1)} %reshape.290), channel_id=2, replica_groups=mesh['dp'=2,'fsdp'=16] {'dp'}, dimensions={0}, use_global_device_ids=true | all-gather | bytes 13824 | tf_op jit(solution)/shard_map/all_gather | solution.py:1865
  14.6 0.1 dynamic-slice_reduce_fusion.1
  14.7 0.6 add_select_fusion.2.ids
  15.3 0.8 slice_bitcast_fusion.3
  16.1 0.8 slice_bitcast_fusion.7
  16.9 1.4 broadcast_in_dim.54.refs_1_.place_ref
  18.3 0.9 slice_bitcast_fusion.2
  19.2 0.0 copy-done
  19.2 0.8 pad_maximum_fusion.1.chunk
  20.0 0.2 copy.64
  20.2 0.0 copy-start.3
  20.2 0.2 copy.65
  20.4 0.0 copy-start.4
  20.4 0.0 copy-start.2
  20.4 0.1 pad_bitcast_fusion
  20.6 0.8 pad_maximum_fusion.2.down_ref.refs_4_
  21.4 0.5 copy.63
  21.9 0.0 copy-done.4
  22.0 0.8 pad.36.chunk
  22.8 1.0 broadcast_in_dim.52.seg_ref.refs_3_
  23.8 1.1 broadcast_in_dim.58.code_ref
  24.9 0.4 copy.60
  25.3 1.6 fusion.1.low_ref
  27.0 96.3 %start_exchange.1 = (bf16[1152,768]{1,0:T(8,128)(2,1)}, bf16[1152,768]{1,0:T(8,128)(2,1)}, f32[32,24,128]{2,1,0:T(8,128)}, bf16[32,288,768]{2,1,0:T(8,128)(2,1)}) custom-call(s32[2304]{0:T(1024)} %add_select_fusion.2.ids, s32[2304,1]{1,0:T(8,128)} %fusion.1.low_ref, bf16[1600,16,768]{2,1,0:T(8,128)(2,1)} %bitcast.95, f32[24,128]{1,0:T(8,128)} %pad_bitcast_fusion.2.fact, ...), custom_call_target="tpu_custom_call" | custom-call | tf_op jit(solution)/shard_map/start_exchange/pallas_call | solution.py:1071
  123.2 1.1 copy.90
  124.3 0.1 slice_convert_fusion.1
  124.4 0.1 copy.88
  124.5 0.1 convert_reduce_fusion
  124.6 0.6 fusion.28
  125.2 0.6 pad.40
  125.9 0.1 slice.142
  126.0 0.1 reshape.267
  126.1 1.1 gather_fusion
  127.3 0.7 dynamic-slice_bitcast_fusion.bias_ref
  128.0 0.6 concatenate.90.fact_ref
  128.6 0.4 reshape.265
  129.0 0.1 copy.66
  129.1 0.3 reshape.266
  129.4 0.1 fusion.19
  129.5 0.1 fusion.15
  129.6 1.1 pad_maximum_fusion.adapt_ref.refs_5_
  130.8 100.5 %first_layer.1 = (bf16[1024,2304]{1,0:T(8,128)(2,1)}, f32[1024,768]{1,0:T(8,128)}, f32[1024,768]{1,0:T(8,128)}, f32[1024,768]{1,0:T(8,128)}, bf16[1024,3072]{1,0...) custom-call(bf16[1152,768]{1,0:T(8,128)(2,1)} %get-tuple-element.53., ...), custom_call_target="tpu_custom_call" | custom-call | tf_op jit(solution)/shard_map/first_layer/pallas_call | solution.py:1288
  231.3 20.5 %last_forward.1 = (bf16[1024,1536]{1,0:T(8,128)(2,1)}, bf16[128,768]{1,0:T(8,128)(2,1)}, bf16[1024,128]{1,0:T(8,128)(2,1)}, f32[6,256]{1,0:T(8,128)}, f32[128,76...) custom-call(f32[1024,768]{1,0:T(8,128)} %get-tuple-element.57.refs_0, ...), custom_call_target="tpu_custom_call" | custom-call | tf_op jit(solution)/shard_map/last_forward/pallas_call | solution.py:461
  251.9 44.5 %head.1 = (f32[768,128]{1,0:T(8,128)}, f32[1,128]{1,0:T(1,128)}) custom-call(bf16[128,768]{1,0:T(8,128)(2,1)} %get-tuple-element.59.u_ref.feat_ref, f32[50,128]{1,0:T(8,128)} %dynamic-slice_bitcast_fusion.bias_ref, bf16[25600,768]{1,0:T(8,128)(2,1)} %table_any.3, bf16[768,6400]{1,0:T(8,128)(2,1)} %get-tuple-element.60.et_any), custom_call_target="tpu_custom_call" | custom-call | tf_op jit(solution)/shard_map/head/pallas_call | solution.py:1776
  296.3 25.6 %last_backward.1 = (f32[1024,768]{1,0:T(8,128)}, bf16[32,32,768]{2,1,0:T(8,128)(2,1)}, f32[768,128]{1,0:T(8,128)}, f32[8,128]{1,0:T(8,128)}) custom-call(bf16[1152,768]{1,0:T(8,128)(2,1)} %get-tuple-element.53.own_any, bf16[1152,768]{1,0:T(8,128)(2,1)} %get-tuple-element.54.got_any, f32[768,128]{1,0:T(8,128)} %get-tuple-element.61.mean_ref, ...), custom_call_target="tpu_custom_call" | custom-call | tf_op jit(solution)/shard_map/last_backward/pallas_call | solution.py:672
  321.9 56.0 %finish.1 = (f32[8,128]{1,0:T(8,128)}, f32[24,768]{1,0:T(8,128)}, f32[24,128]{1,0:T(8,128)}) custom-call(f32[1024,768]{1,0:T(8,128)} %get-tuple-element.76.dout_any, f32[1024,768]{1,0:T(8,128)} %get-tuple-element.77.one_any, f32[1024,768]{1,0:T(8,128)} %get-tuple-element.78.two_any, bf16[1024,3072]{1,0:T(8,128)(2,1)} %get-tuple-element.79.slope_any, ...), custom_call_target="tpu_custom_call" | custom-call | tf_op jit(solution)/shard_map/finish/pallas_call | solution.py:1536
  378.0 1.8 update.1
  (31 shorter events, 0.3 us)
Async XLA Ops:
  0.6 18.6 %copy-start.1 = (bf16[2,96,768]{2,1,0:T(8,128)(2,1)S(1)}, bf16[2,96,768]{2,1,0:T(8,128)(2,1)}, u32[]{:S(2)}) copy-start(bf16[2,96,768]{2,1,0:T(8,128)(2,1)} %param.39) | copy-start | bytes 884740
  0.6 18.5 %copy-start = (bf16[2,768,96]{1,2,0:T(8,128)(2,1)S(1)}, bf16[2,768,96]{1,2,0:T(8,128)(2,1)}, u32[]{:S(2)}) copy-start(bf16[2,768,96]{1,2,0:T(8,128)(2,1)} %param.38) | copy-start | bytes 884740
  6.2 16.6 %copy-start.5 = (f32[1,1024]{1,0:T(1,128)}, f32[1,1024]{1,0:T(1,128)S(1)}, u32[]{:S(2)}) copy-start(f32[1,1024]{1,0:T(1,128)S(1)} %convert_element_type.56.seg_row_ref) | copy-start | bytes 12292
  20.2 1.7 copy-start.3
  20.4 1.5 copy-start.4
  20.4 1.6 copy-start.2
  27.0 97.6 %copy-start.6 = (f32[4]{0:T(128)S(1)}, f32[4]{0:T(128)}, u32[]{:S(2)}) copy-start(f32[4]{0:T(128)} %param.30) | copy-start | bytes 52
